TPU v7x, 32 devices: a whole 2x2x4 slice. The times are simulated.
32 devices in a mesh: pp: 4 (over y, core), ep: 8 (over z, x).
Axes of the slice: x: 2, y: 2, z: 4, core: 2. Of those that a mesh axis runs over, the one named last changes fastest.
Arguments:
- fwd_in: bfloat16 [4, 1024, 3584], P('pp', 'ep'), may hold values from -6 to 6
- fwd_ids: int32 [4, 1024, 1], P('pp', 'ep'), may hold values from 0 to 7; in each aligned block of 128 rows (0 to 127, 128 to 255, ..., all dimensions but the last counted through in order) at most 20 rows name the same one
- saved_in: bfloat16 [4, 1024, 3584], P('pp', 'ep'), may hold values from -6 to 6
- bwd_ids: int32 [4, 1024, 1], P('pp', 'ep'), may hold values from 0 to 7; in each aligned block of 128 rows (0 to 127, 128 to 255, ..., all dimensions but the last counted through in order) at most 20 rows name the same one
- grad_in: bfloat16 [4, 1024, 3584], P('pp', 'ep'), may hold values from -6 to 6
- router: float32 [4, 3584, 8], P('pp'), may hold values from -0.09375 to 0.09375
- w_gate: bfloat16 [4, 3584, 8192], P('pp', None, 'ep'), may hold values from -0.09375 to 0.09375
- w_up: bfloat16 [4, 3584, 8192], P('pp', None, 'ep'), may hold values from -0.09375 to 0.09375
- w_down: bfloat16 [4, 8192, 3584], P('pp', 'ep'), may hold values from -0.1875 to 0.1875
Outputs:
- fwd_next: bfloat16 [4, 1024, 3584], P('pp', 'ep')
- grad_next: bfloat16 [4, 1024, 3584], P('pp', 'ep')
Inputs may be any that keep to these rules, and one draw needn't show every extreme that they name: `fwd_ids`: within the 128 tokens of one device's aligned block, no expert is chosen more than 20 times; some block chooses some expert exactly 20 times. `bwd_ids`: as for fwd_ids.
All inputs are finite; a program needn't handle non-finite values.
Results may differ from a plain program's by a relative error of at most 0.011.
Values may be sent and summed in bfloat16 or wider, within the bound.
No kernel may reach another device: no remote copies, remote signals or barrier semaphores. Data moves between devices by JAX's collectives and lax.ppermute only.
A program may use at most 128 MiB of HBM per device.

v0:
```python
import jax
import jax.numpy as jnp
from jax import lax
from jax.sharding import PartitionSpec as P

route_scale = 2.5
contract = (((1,), (1,)), ((), ()))


def shortened(value):

    def short(part):
        return part.astype(jnp.bfloat16) if part.dtype == jnp.float32 else part

    return jax.tree.map(short, value)


def swapped(value, axis, distance):
    return lax.ppermute(value, axis, [(i, i ^ 1 << distance) for i in range(lax.axis_size(axis))])


def from_behind(value, axis, steps):
    count = lax.axis_size(axis)
    pairs = [(source, (source + steps) % count) for source in range(count)]
    return lax.ppermute(value, axis, pairs)


def order_slots(chosen, experts, capacity):
    token_count = chosen.shape[0]
    onehot = (chosen[:, None] == jnp.arange(experts, dtype=jnp.int32)[None, :]).astype(jnp.int32)
    before = jnp.cumsum(onehot, axis=0) - onehot
    ranking = jnp.sum(before * onehot, axis=1)
    slot_table = jnp.full((experts * capacity,), token_count, jnp.int32)
    slot_table = slot_table.at[chosen * capacity + ranking].set(
        jnp.arange(token_count, dtype=jnp.int32)
    )
    return (onehot, ranking, slot_table)


def routing_weight(tokens, router, onehot):
    logits = jnp.dot(tokens.astype(jnp.float32), router, precision=lax.Precision.HIGHEST)
    picked = jnp.sum(jnp.where(onehot > 0, logits, 0.0), axis=1)
    return route_scale * jax.nn.sigmoid(picked)


def with_zero_row(tokens):
    return jnp.concatenate([tokens, jnp.zeros((1, tokens.shape[1]), tokens.dtype)], axis=0)


def expert_forward(row_block, gate_cols, up_cols, down_rows):
    gate_proj = jnp.dot(row_block, gate_cols, preferred_element_type=jnp.float32)
    up_proj = jnp.dot(row_block, up_cols, preferred_element_type=jnp.float32)
    hidden = (gate_proj * jax.nn.sigmoid(gate_proj) * up_proj).astype(jnp.bfloat16)
    return jnp.dot(hidden, down_rows, preferred_element_type=jnp.float32).astype(jnp.bfloat16)


def expert_backward(row_block, row_grads, joined_cols, down_rows):
    unit_count = down_rows.shape[0]
    both_proj = jnp.dot(row_block, joined_cols, preferred_element_type=jnp.float32)
    gate_proj = both_proj[:, :unit_count]
    up_proj = both_proj[:, unit_count:]
    d_hidden = lax.dot_general(row_grads, down_rows, contract, preferred_element_type=jnp.float32)
    sigmoid_gate = jax.nn.sigmoid(gate_proj)
    d_gate = (d_hidden * up_proj * sigmoid_gate * (1.0 + gate_proj * (1.0 - sigmoid_gate))).astype(
        jnp.bfloat16
    )
    d_up = (d_hidden * gate_proj * sigmoid_gate).astype(jnp.bfloat16)
    d_joined = jnp.concatenate([d_gate, d_up], axis=1)
    partial_sum = lax.dot_general(
        d_joined, joined_cols, contract, preferred_element_type=jnp.float32
    )
    return partial_sum.astype(jnp.bfloat16)


def arrange(own_rows, peer_rows, own_bit):
    return jnp.where(
        own_bit == 0, jnp.stack([own_rows, peer_rows]), jnp.stack([peer_rows, own_rows])
    )


def per_device(fwd_in, fwd_ids, saved_in, bwd_ids, grad_in, router, w_gate, w_up, w_down):
    experts = router.shape[-1]
    owners = lax.axis_size("ep")
    group_size = owners // experts
    bit_count = group_size.bit_length() - 1
    own_index = lax.axis_index("ep")
    token_count = fwd_in.shape[1]
    width = fwd_in.shape[2]
    capacity = group_size * max(1, 5 * token_count // (4 * experts * group_size))
    quarter_slots = capacity // group_size
    router_section = router[0]
    gate_cols = w_gate[0]
    up_cols = w_up[0]
    down_rows = w_down[0]
    joined_cols = jnp.concatenate([gate_cols, up_cols], axis=1)
    fwd_tokens = fwd_in[0]
    fwd_chosen = fwd_ids[0, :, 0]
    fwd_onehot, fwd_rank, fwd_table = order_slots(fwd_chosen, experts, capacity)
    fwd_weight = routing_weight(fwd_tokens, router_section, fwd_onehot)
    fwd_padded = with_zero_row(fwd_tokens)
    saved_tokens = saved_in[0]
    bwd_chosen = bwd_ids[0, :, 0]
    grad_tokens = grad_in[0]
    bwd_onehot, bwd_rank, bwd_table = order_slots(bwd_chosen, experts, capacity)
    bwd_weight = routing_weight(saved_tokens, router_section, bwd_onehot)
    weighted = (bwd_weight[:, None] * grad_tokens.astype(jnp.float32)).astype(jnp.bfloat16)
    saved_padded = with_zero_row(saved_tokens)
    weighted_padded = with_zero_row(weighted)
    fwd_index = (
        fwd_table.reshape(experts, quarter_slots, group_size)
        .transpose(0, 2, 1)
        .reshape(owners, quarter_slots)
    )
    gathered = lax.all_to_all(
        jnp.take(fwd_padded, fwd_index, axis=0), "ep", split_axis=0, concat_axis=0, tiled=True
    )
    for bit_number in range(bit_count):
        own_bit = own_index >> bit_number & 1
        peer_rows = swapped(shortened(gathered), "ep", bit_number).astype(gathered.dtype)
        gathered = arrange(gathered, peer_rows, own_bit)
    partial_out = expert_forward(gathered.reshape(-1, width), gate_cols, up_cols, down_rows)
    partial_out = partial_out.reshape(group_size, 1, owners * quarter_slots, width)
    for bit_number in reversed(range(bit_count)):
        own_bit = own_index >> bit_number & 1
        half_rows = partial_out.shape[0] // 2
        kept_half = lax.dynamic_slice_in_dim(partial_out, own_bit * half_rows, half_rows, 0)
        sent_half = lax.dynamic_slice_in_dim(partial_out, (1 - own_bit) * half_rows, half_rows, 0)
        partial_out = jnp.concatenate([kept_half, swapped(sent_half, "ep", bit_number)], axis=1)
    summed = jnp.sum(partial_out, axis=(0, 1), dtype=jnp.float32).astype(jnp.bfloat16)
    returned = lax.all_to_all(
        summed.reshape(owners, quarter_slots, width), "ep", split_axis=0, concat_axis=0, tiled=True
    ).reshape(-1, width)
    source_slot = (
        fwd_chosen * group_size + fwd_rank % group_size
    ) * quarter_slots + fwd_rank // group_size
    fwd_expert = jnp.take(returned, source_slot, axis=0).astype(jnp.float32)
    bwd_index = (
        bwd_table.reshape(experts, quarter_slots, group_size)
        .transpose(0, 2, 1)
        .reshape(owners, quarter_slots)
    )
    saved_rows, grad_rows = (
        lax.all_to_all(
            jnp.take(saved_padded, bwd_index, axis=0), "ep", split_axis=0, concat_axis=0, tiled=True
        ),
        lax.all_to_all(
            jnp.take(weighted_padded, bwd_index, axis=0),
            "ep",
            split_axis=0,
            concat_axis=0,
            tiled=True,
        ),
    )
    for bit_number in range(bit_count):
        own_bit = own_index >> bit_number & 1
        peer_saved, peer_grads = (
            swapped(shortened(saved_rows), "ep", bit_number).astype(saved_rows.dtype),
            swapped(shortened(grad_rows), "ep", bit_number).astype(grad_rows.dtype),
        )
        saved_rows = arrange(saved_rows, peer_saved, own_bit)
        grad_rows = arrange(grad_rows, peer_grads, own_bit)
    partial_grad = expert_backward(
        saved_rows.reshape(-1, width), grad_rows.reshape(-1, width), joined_cols, down_rows
    )
    partial_grad = partial_grad.reshape(group_size, 1, owners * quarter_slots, width)
    for bit_number in reversed(range(bit_count)):
        own_bit = own_index >> bit_number & 1
        half_rows = partial_grad.shape[0] // 2
        kept_half = lax.dynamic_slice_in_dim(partial_grad, own_bit * half_rows, half_rows, 0)
        sent_half = lax.dynamic_slice_in_dim(partial_grad, (1 - own_bit) * half_rows, half_rows, 0)
        partial_grad = jnp.concatenate([kept_half, swapped(sent_half, "ep", bit_number)], axis=1)
    summed_grad = jnp.sum(partial_grad, axis=(0, 1), dtype=jnp.float32).astype(jnp.bfloat16)
    returned_grad = lax.all_to_all(
        summed_grad.reshape(owners, quarter_slots, width),
        "ep",
        split_axis=0,
        concat_axis=0,
        tiled=True,
    ).reshape(-1, width)
    grad_slot = (
        bwd_chosen * group_size + bwd_rank % group_size
    ) * quarter_slots + bwd_rank // group_size
    bwd_expert = jnp.take(returned_grad, grad_slot, axis=0).astype(jnp.float32)
    fwd_section = (fwd_tokens.astype(jnp.float32) + fwd_weight[:, None] * fwd_expert).astype(
        jnp.bfloat16
    )
    grad_section = (grad_tokens.astype(jnp.float32) + bwd_expert).astype(jnp.bfloat16)
    fwd_next = from_behind(fwd_section[None], "pp", 1)
    grad_next = from_behind(grad_section[None], "pp", -1)
    return (fwd_next, grad_next)


def solution(mesh):
    in_specs = (
        P("pp", "ep", None),
        P("pp", "ep", None),
        P("pp", "ep", None),
        P("pp", "ep", None),
        P("pp", "ep", None),
        P("pp", None, None),
        P("pp", None, "ep"),
        P("pp", None, "ep"),
        P("pp", "ep", None),
    )
    out_specs = (P("pp", "ep", None), P("pp", "ep", None))
    return jax.shard_map(
        per_device, mesh=mesh, in_specs=in_specs, out_specs=out_specs, check_vma=False
    )
```

profile of v0, /device:TPU:0, one launch (start us, length us, event | category | flops | bytes accessed | tf_op | source)
XLA Modules:
  0.0 221.7 jit_solution(16509754761811841544)
XLA Ops:
  4.8 2.0 fusion.14
  13.0 2.7 %broadcast_select_fusion = (bf16[8,20,3584]{2,1,0:T(8,128)(2,1)S(1)}, bf16[8,20,3584]{2,1,0:T(8,128)(2,1)}) fusion(bf16[8,20,3584]{2,1,0:T(8,128)(2,1)} %reshape.200, pred[8,20]{1,0:T(8,128)(4,1)S(1)} %compare_and_fusion, bf16[8,20,3584]{2,1,0:T(8,128)(2,1)S(1)} %copy-done.4), kind=kLoop, calls=%fused_computation.21 | loop fusion | flops 1146880 | bytes 4587680 | tf_op jit(solution)/shard_map/jit(_take)/select_n | solution.py:144
  15.7 40.6 %all_to_all.25 = bf16[8,20,3584]{2,1,0:T(8,128)(2,1)} all-to-all(bf16[8,20,3584]{2,1,0:T(8,128)(2,1)S(1)} %get-tuple-element.10), channel_id=1, replica_groups=mesh['pp'=4,'ep'=8] {'ep'}, dimensions={0} | all-to-all | bytes 2293760 | tf_op jit(solution)/shard_map/all_to_all | solution.py:143
  56.3 4.4 %all-to-all-start.2 = ((bf16[8,20,3584]{2,1,0:T(8,128)(2,1)}), bf16[8,20,3584]{2,1,0:T(8,128)(2,1)}, u32[]{:S(2)}, u32[]{:S(2)}) async-start(bf16[8,20,3584]{2,1,0:T(8,128)(2,1)} %get-tuple-element.11), calls=%async_computation.2 | async-start | bytes 2752512 | tf_op jit(solution)/shard_map/all_to_all | solution.py:146
  65.0 2.7 %broadcast_select_fusion.2 = bf16[8,20,3584]{2,1,0:T(8,128)(2,1)} fusion(bf16[8,20,3584]{2,1,0:T(8,128)(2,1)} %reshape.190, pred[8,20]{1,0:T(8,128)(4,1)S(1)} %compare_and_fusion.1), kind=kLoop, calls=%fused_computation.23 | loop fusion | flops 573440 | bytes 2293920 | tf_op jit(solution)/shard_map/jit(_take)/select_n | solution.py:115
  68.9 24.0 %all-to-all-done.2 = bf16[8,20,3584]{2,1,0:T(8,128)(2,1)} async-done(((bf16[8,20,3584]{2,1,0:T(8,128)(2,1)}), bf16[8,20,3584]{2,1,0:T(8,128)(2,1)}, u32[]{:S(2)}, u32[]{:S(2)}) %all-to-all-start.2) | async-done | bytes 1146912 | tf_op jit(solution)/shard_map/all_to_all | solution.py:146
  92.8 4.3 %all-to-all-start = ((bf16[8,20,3584]{2,1,0:T(8,128)(2,1)}), bf16[8,20,3584]{2,1,0:T(8,128)(2,1)}, u32[]{:S(2)}, u32[]{:S(2)}) async-start(bf16[8,20,3584]{2,1,0:T(8,128)(2,1)} %broadcast_select_fusion.2), calls=%async_computation | async-start | bytes 2752512 | tf_op jit(solution)/shard_map/all_to_all | solution.py:114
  97.1 2.4 %reshape.119 = bf16[160,3584]{1,0:T(8,128)(2,1)} reshape(bf16[8,20,3584]{2,1,0:T(8,128)(2,1)} %all-to-all-done.2) | data formatting | bytes 2293760 | tf_op jit(solution)/shard_map/reshape | solution.py:163
  99.6 7.2 %fusion.1 = f32[160,2048]{1,0:T(8,128)S(1)} fusion(bf16[160,3584]{1,0:T(8,128)(2,1)} %reshape.120, bf16[3584,1024]{1,0:T(8,128)(2,1)} %bitcast.74, bf16[3584,1024]{1,0:T(8,128)(2,1)} %bitcast.62), kind=kOutput, calls=%fused_computation.9 | convolution fusion | flops 2378170368 | bytes 17137664 | tf_op jit(solution)/shard_map/dot_general | solution.py:59
  106.8 5.7 %fusion.19 = (bf16[160,1024]{1,0:T(8,128)(2,1)S(1)}, bf16[160,1024]{1,0:T(8,128)(2,1)S(1)}) fusion(f32[160,2048]{1,0:T(8,128)S(1)} %fusion.1, bf16[160,3584]{1,0:T(8,128)(2,1)S(1)} %copy-done.7, bf16[1,1024,3584]{2,1,0:T(8,128)(2,1)} %param.21), kind=kOutput, calls=%fused_computation.35 | convolution fusion | flops 1176535040 | bytes 10452992 | tf_op jit(solution)/shard_map/dot_general | solution.py:62
  112.5 8.1 %fusion.9 = bf16[160,3584]{1,0:T(8,128)(2,1)} fusion(bf16[3584,1024]{1,0:T(8,128)(2,1)} %bitcast.75, bf16[3584,1024]{1,0:T(8,128)(2,1)S(1)} %bitcast.65, bf16[160,1024]{1,0:T(8,128)(2,1)S(1)} %get-tuple-element.9, bf16[160,1024]{1,0:T(8,128)(2,1)S(1)} %get-tuple-element.8), kind=kOutput, calls=%fused_computation.15 | convolution fusion | flops 2380054528 | bytes 16482304 | tf_op jit(solution)/shard_map/dot_general | solution.py:69
  120.7 2.3 %convert_element_type.76 = bf16[8,20,3584]{2,1,0:T(8,128)(2,1)} reshape(bf16[160,3584]{1,0:T(8,128)(2,1)} %fusion.9) | data formatting | bytes 2293760 | tf_op jit(solution)/shard_map/convert_element_type | solution.py:172
  122.9 6.5 %all-to-all-done = bf16[8,20,3584]{2,1,0:T(8,128)(2,1)} async-done(((bf16[8,20,3584]{2,1,0:T(8,128)(2,1)}), bf16[8,20,3584]{2,1,0:T(8,128)(2,1)}, u32[]{:S(2)}, u32[]{:S(2)}) %all-to-all-start) | async-done | bytes 1146912 | tf_op jit(solution)/shard_map/all_to_all | solution.py:114
  129.4 3.8 %all-to-all-start.4 = ((bf16[8,20,3584]{2,1,0:T(8,128)(2,1)}), bf16[8,20,3584]{2,1,0:T(8,128)(2,1)S(1)}, u32[]{:S(2)}, u32[]{:S(2)}) async-start(bf16[8,20,3584]{2,1,0:T(8,128)(2,1)} %convert_element_type.76), calls=%async_computation.4 | async-start | bytes 2752512 | tf_op jit(solution)/shard_map/all_to_all | solution.py:173
  133.2 1.4 reshape.117
  134.6 4.4 %fusion.39 = f32[160,1024]{1,0:T(8,128)S(1)} fusion(bf16[160,3584]{1,0:T(8,128)(2,1)S(1)} %reshape.117, bf16[1,3584,1024]{2,1,0:T(8,128)(2,1)} %param.19), kind=kOutput, calls=%fused_computation.78 | convolution fusion | flops 1174405120 | bytes 9142272 | tf_op jit(solution)/shard_map/dot_general | solution.py:51
  139.1 8.8 %fusion.6 = bf16[160,3584]{1,0:T(8,128)(2,1)} fusion(bf16[1,1024,3584]{2,1,0:T(8,128)(2,1)} %param.21, bf16[160,3584]{1,0:T(8,128)(2,1)S(1)} %reshape.117, f32[160,1024]{1,0:T(8,128)S(1)} %fusion.39, bf16[1,3584,1024]{2,1,0:T(8,128)(2,1)} %param.20), kind=kOutput, calls=%fused_computation.14 | convolution fusion | flops 2350366720 | bytes 17629184 | tf_op jit(solution)/shard_map/dot_general | solution.py:54
  147.8 2.3 %convert_element_type.66 = bf16[8,20,3584]{2,1,0:T(8,128)(2,1)} reshape(bf16[160,3584]{1,0:T(8,128)(2,1)} %fusion.6) | data formatting | bytes 2293760 | tf_op jit(solution)/shard_map/convert_element_type | solution.py:129
  150.2 15.8 %all-to-all-done.4 = bf16[8,20,3584]{2,1,0:T(8,128)(2,1)S(1)} async-done(((bf16[8,20,3584]{2,1,0:T(8,128)(2,1)}), bf16[8,20,3584]{2,1,0:T(8,128)(2,1)S(1)}, u32[]{:S(2)}, u32[]{:S(2)}) %all-to-all-start.4) | async-done | bytes 1146912 | tf_op jit(solution)/shard_map/all_to_all | solution.py:173
  166.0 4.3 %all-to-all-start.1 = ((bf16[8,20,3584]{2,1,0:T(8,128)(2,1)}), bf16[8,20,3584]{2,1,0:T(8,128)(2,1)}, u32[]{:S(2)}, u32[]{:S(2)}) async-start(bf16[8,20,3584]{2,1,0:T(8,128)(2,1)} %convert_element_type.66), calls=%async_computation.1 | async-start | bytes 2752512 | tf_op jit(solution)/shard_map/all_to_all | solution.py:130
  175.5 2.5 %fusion.16 = bf16[1,128,3584]{2,1,0:T(8,128)(2,1)} fusion(bf16[1,128,3584]{2,1,0:T(8,128)(2,1)} %param.17, bf16[128,3584]{1,0:T(8,128)(2,1)S(1)} %gather_fusion.4, pred[128]{0:T(512)(128)(4,1)S(1)} %copy-done.12), kind=kLoop, calls=%fused_computation.31 | loop fusion | flops 2293760 | bytes 2752640 | tf_op jit(solution)/shard_map/broadcast_in_dim | solution.py:189
  178.1 24.5 %all-to-all-done.1 = bf16[8,20,3584]{2,1,0:T(8,128)(2,1)} async-done(((bf16[8,20,3584]{2,1,0:T(8,128)(2,1)}), bf16[8,20,3584]{2,1,0:T(8,128)(2,1)}, u32[]{:S(2)}, u32[]{:S(2)}) %all-to-all-start.1) | async-done | bytes 1146912 | tf_op jit(solution)/shard_map/all_to_all | solution.py:130
  205.8 12.8 %collective-permute-done = bf16[1,128,3584]{2,1,0:T(8,128)(2,1)S(1)} collective-permute-done((bf16[1,128,3584]{2,1,0:T(8,128)(2,1)S(1)}, bf16[1,128,3584]{2,1,0:T(8,128)(2,1)S(1)}, u32[]{:S(2)}, u32[]{:S(2)}) %collective-permute-start) | collective-permute-done | bytes 917536 | tf_op jit(solution)/shard_map/ppermute | solution.py:25
  219.6 2.2 copy.22
  (94 shorter events, 24.9 us)
Async XLA Ops:
  0.6 4.1 %copy-start = (f32[1,3584,8]{1,2,0:T(8,128)S(1)}, f32[1,3584,8]{1,2,0:T(8,128)}, u32[]{:S(2)}) copy-start(f32[1,3584,8]{1,2,0:T(8,128)} %param.18) | copy-start | bytes 344068
  0.6 6.2 %copy-start.6 = (bf16[1,128,3584]{2,1,0:T(8,128)(2,1)S(1)}, bf16[1,128,3584]{2,1,0:T(8,128)(2,1)}, u32[]{:S(2)}) copy-start(bf16[1,128,3584]{2,1,0:T(8,128)(2,1)} %param.17) | copy-start | bytes 2752516
  8.4 1.4 copy-start.5
  11.2 1.8 copy-start.4
  56.3 4.4 %copy-start.9 = (s32[1,128,1]{1,2,0:T(1,128)S(1)}, s32[1,128,1]{1,2,0:T(1,128)}, u32[]{:S(2)}) copy-start(s32[1,128,1]{1,2,0:T(1,128)} %param.14) | copy-start | bytes 1540
  56.3 6.0 %copy-start.1 = (bf16[1,128,3584]{2,1,0:T(8,128)(2,1)S(1)}, bf16[1,128,3584]{2,1,0:T(8,128)(2,1)}, u32[]{:S(2)}) copy-start(bf16[1,128,3584]{2,1,0:T(8,128)(2,1)} %param.13) | copy-start | bytes 2752516
  56.3 36.5 %all-to-all-start.2 = ((bf16[8,20,3584]{2,1,0:T(8,128)(2,1)}), bf16[8,20,3584]{2,1,0:T(8,128)(2,1)}, u32[]{:S(2)}, u32[]{:S(2)}) async-start(bf16[8,20,3584]{2,1,0:T(8,128)(2,1)} %get-tuple-element.11), calls=%async_computation.2 | async-start | bytes 2752512 | tf_op jit(solution)/shard_map/all_to_all | solution.py:146
  65.0 2.8 %copy-start.3 = (bf16[8,20,3584]{2,1,0:T(8,128)(2,1)S(1)}, bf16[8,20,3584]{2,1,0:T(8,128)(2,1)}, u32[]{:S(2)}) copy-start(bf16[8,20,3584]{2,1,0:T(8,128)(2,1)} %all_to_all.25) | copy-start | bytes 3440644
  92.8 36.6 %all-to-all-start = ((bf16[8,20,3584]{2,1,0:T(8,128)(2,1)}), bf16[8,20,3584]{2,1,0:T(8,128)(2,1)}, u32[]{:S(2)}, u32[]{:S(2)}) async-start(bf16[8,20,3584]{2,1,0:T(8,128)(2,1)} %broadcast_select_fusion.2), calls=%async_computation | async-start | bytes 2752512 | tf_op jit(solution)/shard_map/all_to_all | solution.py:114
  97.1 15.4 %slice-start = ((s8[7340032]{0:T(1024)(128)(4,1)}), s8[3145728]{0:T(1024)(128)(4,1)S(1)}, s32[]{:S(2)}) async-start(s8[7340032]{0:T(1024)(128)(4,1)} %bitcast.63), calls=%async_computation.5 | async-start | bytes 6291456
  99.6 7.2 %copy-start.7 = (bf16[160,3584]{1,0:T(8,128)(2,1)S(1)}, bf16[160,3584]{1,0:T(8,128)(2,1)}, u32[]{:S(2)}) copy-start(bf16[160,3584]{1,0:T(8,128)(2,1)} %reshape.119) | copy-start | bytes 3440644
  99.6 12.9 %slice-start.1 = ((s8[7340032]{0:T(1024)(128)(4,1)}), s8[4194304]{0:T(1024)(128)(4,1)S(1)}, s32[]{:S(2)}) async-start(s8[7340032]{0:T(1024)(128)(4,1)} %bitcast.63), calls=%async_computation.6 | async-start | bytes 8388608
  129.4 36.6 %all-to-all-start.4 = ((bf16[8,20,3584]{2,1,0:T(8,128)(2,1)}), bf16[8,20,3584]{2,1,0:T(8,128)(2,1)S(1)}, u32[]{:S(2)}, u32[]{:S(2)}) async-start(bf16[8,20,3584]{2,1,0:T(8,128)(2,1)} %convert_element_type.76), calls=%async_computation.4 | async-start | bytes 2752512 | tf_op jit(solution)/shard_map/all_to_all | solution.py:173
  150.1 20.1 %copy-start.8 = (s32[1,128,1]{1,2,0:T(1,128)S(1)}, s32[1,128,1]{1,2,0:T(1,128)}, u32[]{:S(2)}) copy-start(s32[1,128,1]{1,2,0:T(1,128)} %param.16) | copy-start | bytes 1540
  150.1 20.1 %copy-start.14 = (s32[128]{0:T(128)S(1)}, s32[128]{0:T(128)}, u32[]{:S(2)}) copy-start(s32[128]{0:T(128)} %copy-done.13) | copy-start | bytes 1540
  150.1 21.3 %copy-start.10 = (s32[1,128,1]{1,2,0:T(1,128)S(1)}, s32[1,128,1]{1,2,0:T(1,128)}, u32[]{:S(2)}) copy-start(s32[1,128,1]{1,2,0:T(1,128)} %param.14) | copy-start | bytes 1540
  150.1 21.3 %copy-start.16 = (s32[128]{0:T(128)S(1)}, s32[128]{0:T(128)}, u32[]{:S(2)}) copy-start(s32[128]{0:T(128)} %copy-done.15) | copy-start | bytes 1540
  150.2 22.4 %copy-start.2 = (bf16[1,128,3584]{2,1,0:T(8,128)(2,1)S(1)}, bf16[1,128,3584]{2,1,0:T(8,128)(2,1)}, u32[]{:S(2)}) copy-start(bf16[1,128,3584]{2,1,0:T(8,128)(2,1)} %param.13) | copy-start | bytes 2752516
  166.0 36.6 %all-to-all-start.1 = ((bf16[8,20,3584]{2,1,0:T(8,128)(2,1)}), bf16[8,20,3584]{2,1,0:T(8,128)(2,1)}, u32[]{:S(2)}, u32[]{:S(2)}) async-start(bf16[8,20,3584]{2,1,0:T(8,128)(2,1)} %convert_element_type.66), calls=%async_computation.1 | async-start | bytes 2752512 | tf_op jit(solution)/shard_map/all_to_all | solution.py:130
  174.3 1.3 copy-start.12
  178.0 27.9 %collective-permute-start.1 = (bf16[1,128,3584]{2,1,0:T(8,128)(2,1)}, bf16[1,128,3584]{2,1,0:T(8,128)(2,1)}, u32[]{:S(2)}, u32[]{:S(2)}) collective-permute-start(bf16[1,128,3584]{2,1,0:T(8,128)(2,1)} %fusion.16), channel_id=1, source_target_pairs={{0,24},{8,0},{16,8},{24,16},{1,25},{9,1},{17,9},{25,17},{2,26},{10... | collective-permute-start | bytes 2752520 | tf_op jit(solution)/shard_map/ppermute | solution.py:25
  204.1 1.3 copy-start.11
  204.1 1.3 copy-start.17
  205.8 12.9 %collective-permute-start = (bf16[1,128,3584]{2,1,0:T(8,128)(2,1)S(1)}, bf16[1,128,3584]{2,1,0:T(8,128)(2,1)S(1)}, u32[]{:S(2)}, u32[]{:S(2)}) collective-permute-start(bf16[1,128,3584]{2,1,0:T(8,128)(2,1)S(1)} %fusion.15), channel_id=1, source_target_pairs={{0,8},{8,16},{16,24},{24,0},{1,9},{9,17},{17,25},{25,1},{2,10},{10... | collective-permute-start | bytes 2752520 | tf_op jit(solution)/shard_map/ppermute | solution.py:25
  (2 other events, 1.7 us)
where the time goes:
time: 223 us; the launch traced here: 222 us
  waiting for transfers between devices  83.6 us (37%)
  blocking collectives  40.6 us (18%)
  matrix products  37 us (17%)
  local copies, waits for them, and re-layouts  28.5 us (13%)
  starting transfers between devices  16.9 us (8%)
  other arithmetic  14 us (6%)
    all_to_all x1, blocking collectives, per_device(): lax.all_to_all(jnp.take(saved_padded, bwd_index, axis=0), 'ep', split_axi...  40.6 us
    all_to_all x1, waiting for transfers between devices, per_device(): lax.all_to_all(summed.reshape(owners, quarter_slots, width), 'ep', split_...  24.5 us
    all_to_all x1, waiting for transfers between devices, per_device(): lax.all_to_all(jnp.take(weighted_padded, bwd_index, axis=0), 'ep', split_...  24 us
    all_to_all x1, waiting for transfers between devices, per_device(): lax.all_to_all(summed_grad.reshape(owners, quarter_slots, width), 'ep', s...  15.8 us
    ppermute x2, waiting for transfers between devices, from_behind(): return lax.ppermute(value, axis, pairs)  12.8 us
    dot_general x1, matrix products, expert_forward(): jnp.dot(hidden, down_rows, preferred_element_type=jnp.float32)  8.77 us
    dot_general x1, matrix products, expert_backward(): lax.dot_general(d_joined, joined_cols, contract, preferred_element_type=j...  8.13 us
    dot_general x1, matrix products, expert_backward(): jnp.dot(row_block, joined_cols, preferred_element_type=jnp.float32)  7.17 us
  transfers between devices with their start and end apart: 6, of which 5 were waited for; matrix products, arithmetic and copies ran while one was open for 28% of the time, Pallas kernels for 0%

commit v1 on v0

--- a/solution.py
+++ b/solution.py
@@ -1,6 +1,10 @@
+import functools
+
 import jax
 import jax.numpy as jnp
 from jax import lax
+from jax.experimental import pallas as pl
+from jax.experimental.pallas import tpu as pltpu
 from jax.sharding import PartitionSpec as P
 
 route_scale = 2.5
@@ -190,6 +194,307 @@
     return (fwd_next, grad_next)
 
 
+BASE_ROWS = 16
+CUTS = 4
+ROWS_BYTES = 2
+
+
+def transposed_dot(left, right):
+    return lax.dot_general(left, right, contract, preferred_element_type=jnp.float32)
+
+
+def plain_dot(left, right):
+    return jnp.dot(left, right, preferred_element_type=jnp.float32)
+
+
+def slot_masks(ids_row, me, experts):
+    tokens = ids_row.shape[1]
+    wanted = lax.broadcasted_iota(jnp.int32, (experts, tokens), 0) == ids_row
+    chosen = jnp.where(wanted, 1.0, 0.0)
+    earlier = jnp.where(
+        lax.broadcasted_iota(jnp.int32, (tokens, tokens), 0)
+        < lax.broadcasted_iota(jnp.int32, (tokens, tokens), 1),
+        1.0,
+        0.0,
+    )
+    before = plain_dot(chosen.astype(jnp.bfloat16), earlier.astype(jnp.bfloat16))
+    rank = jnp.sum(before * chosen, axis=0, keepdims=True).astype(jnp.int32)
+    row = lax.broadcasted_iota(jnp.int32, (experts * BASE_ROWS, tokens), 0)
+    mine = ids_row == ((row // BASE_ROWS) ^ me)
+    place = row % BASE_ROWS
+    base = jnp.where(mine & (rank == place), 1.0, 0.0).astype(jnp.bfloat16)
+    extra = mine & (rank == BASE_ROWS + place % CUTS)
+    pieces = [
+        jnp.where(extra & (place // CUTS == q), 1.0, 0.0).astype(jnp.bfloat16) for q in range(CUTS)
+    ]
+    return base, pieces
+
+
+def pack_kernel(experts, ids_ref, x_ref, *out_refs):
+    me = lax.axis_index("ep")
+    width = x_ref.shape[1]
+    piece = width // CUTS
+    base, pieces = slot_masks(ids_ref[...], me, experts)
+    for q in range(CUTS):
+        columns = slice(q * piece, (q + 1) * piece)
+        packed = plain_dot(base, x_ref[:, columns]).astype(jnp.bfloat16)
+        for k in range(experts):
+            out_refs[k][:, columns] = packed[k * BASE_ROWS : (k + 1) * BASE_ROWS]
+    extra = plain_dot(pieces[0], x_ref[:, :piece])
+    for q in range(1, CUTS):
+        extra = extra + plain_dot(pieces[q], x_ref[:, q * piece : (q + 1) * piece])
+    extra = extra.astype(jnp.bfloat16)
+    for k in range(experts):
+        out_refs[k][:, width:] = extra[k * BASE_ROWS : (k + 1) * BASE_ROWS]
+
+
+def unpack_kernel(experts, ids_ref, *refs):
+    me = lax.axis_index("ep")
+    message_refs, out_ref = refs[:experts], refs[experts]
+    width = out_ref.shape[1]
+    piece = width // CUTS
+    base, pieces = slot_masks(ids_ref[...], me, experts)
+    from_rows = (((0,), (0,)), ((), ()))
+    extra = jnp.concatenate([ref[:, width:] for ref in message_refs], axis=0)
+    for q in range(CUTS):
+        columns = slice(q * piece, (q + 1) * piece)
+        rows = jnp.concatenate([ref[:, columns] for ref in message_refs], axis=0)
+        total = lax.dot_general(base, rows, from_rows, preferred_element_type=jnp.float32)
+        total = total + lax.dot_general(
+            pieces[q], extra, from_rows, preferred_element_type=jnp.float32
+        )
+        out_ref[:, columns] = total.astype(jnp.bfloat16)
+
+
+def piece_places(experts, q):
+    shape = (experts * CUTS, experts * BASE_ROWS)
+    slot = lax.broadcasted_iota(jnp.int32, shape, 0)
+    row = lax.broadcasted_iota(jnp.int32, shape, 1)
+    same = (slot // CUTS == row // BASE_ROWS) & (row % BASE_ROWS == q * CUTS + slot % CUTS)
+    return jnp.where(same, 1.0, 0.0).astype(jnp.bfloat16)
+
+
+def spread(message_refs, rows_ref):
+    experts = len(message_refs)
+    width = rows_ref.shape[1]
+    piece = width // CUTS
+    first = experts * BASE_ROWS
+    for k, ref in enumerate(message_refs):
+        rows_ref[k * BASE_ROWS : (k + 1) * BASE_ROWS, :] = ref[:, :width]
+    extra = jnp.concatenate([ref[:, width:] for ref in message_refs], axis=0)
+    for q in range(CUTS):
+        picked = plain_dot(piece_places(experts, q), extra)
+        rows_ref[first:, q * piece : (q + 1) * piece] = picked.astype(jnp.bfloat16)
+
+
+def collect(rows_ref, message_refs):
+    experts = len(message_refs)
+    width = rows_ref.shape[1]
+    piece = width // CUTS
+    first = experts * BASE_ROWS
+    from_rows = (((0,), (0,)), ((), ()))
+    extra = 0.0
+    for q in range(CUTS):
+        extra = extra + lax.dot_general(
+            piece_places(experts, q),
+            rows_ref[first:, q * piece : (q + 1) * piece],
+            from_rows,
+            preferred_element_type=jnp.float32,
+        )
+    extra = extra.astype(jnp.bfloat16)
+    for k, ref in enumerate(message_refs):
+        ref[:, :width] = rows_ref[k * BASE_ROWS : (k + 1) * BASE_ROWS, :]
+        ref[:, width:] = extra[k * BASE_ROWS : (k + 1) * BASE_ROWS]
+
+
+def row_weight(rows_ref, router_ref):
+    me = lax.axis_index("ep")
+    centroid = router_ref[pl.ds(me, 1), :]
+    logits = jnp.sum(rows_ref[...].astype(jnp.float32) * centroid, axis=1, keepdims=True)
+    return route_scale * jax.nn.sigmoid(logits)
+
+
+def forward_kernel(experts, router_ref, gate_ref, up_ref, down_ref, *refs):
+    message_refs, out_refs = refs[:experts], refs[experts : 2 * experts]
+    rows_ref, total_ref = refs[2 * experts :]
+    step = pl.program_id(0)
+
+    @pl.when(step == 0)
+    def _():
+        spread(message_refs, rows_ref)
+
+    rows = rows_ref[...]
+    gate_proj = plain_dot(rows, gate_ref[...])
+    up_proj = plain_dot(rows, up_ref[...])
+    hidden = (gate_proj * jax.nn.sigmoid(gate_proj) * up_proj).astype(jnp.bfloat16)
+    part = plain_dot(hidden, down_ref[...])
+
+    @pl.when(step == 0)
+    def _():
+        total_ref[...] = part
+
+    @pl.when(step > 0)
+    def _():
+        total_ref[...] += part
+
+    @pl.when(step == pl.num_programs(0) - 1)
+    def _():
+        weight = row_weight(rows_ref, router_ref)
+        expert = total_ref[...].astype(jnp.bfloat16).astype(jnp.float32)
+        section = rows_ref[...].astype(jnp.float32) + weight * expert
+        rows_ref[...] = section.astype(jnp.bfloat16)
+        collect(rows_ref, out_refs)
+
+
+def backward_kernel(experts, router_ref, gate_ref, up_ref, down_ref, *refs):
+    saved_refs, grad_refs = refs[:experts], refs[experts : 2 * experts]
+    out_refs = refs[2 * experts : 3 * experts]
+    rows_ref, grads_ref, weighted_ref, total_ref = refs[3 * experts :]
+    step = pl.program_id(0)
+
+    @pl.when(step == 0)
+    def _():
+        spread(saved_refs, rows_ref)
+        spread(grad_refs, grads_ref)
+        weight = row_weight(rows_ref, router_ref)
+        weighted = weight * grads_ref[...].astype(jnp.float32)
+        weighted_ref[...] = weighted.astype(jnp.bfloat16)
+
+    rows = rows_ref[...]
+    gate_proj = plain_dot(rows, gate_ref[...])
+    up_proj = plain_dot(rows, up_ref[...])
+    d_hidden = transposed_dot(weighted_ref[...], down_ref[...])
+    sigmoid_gate = jax.nn.sigmoid(gate_proj)
+    d_gate = d_hidden * up_proj * sigmoid_gate * (1.0 + gate_proj * (1.0 - sigmoid_gate))
+    d_up = d_hidden * gate_proj * sigmoid_gate
+    part = transposed_dot(d_gate.astype(jnp.bfloat16), gate_ref[...])
+    part = part + transposed_dot(d_up.astype(jnp.bfloat16), up_ref[...])
+
+    @pl.when(step == 0)
+    def _():
+        total_ref[...] = part
+
+    @pl.when(step > 0)
+    def _():
+        total_ref[...] += part
+
+    @pl.when(step == pl.num_programs(0) - 1)
+    def _():
+        expert = total_ref[...].astype(jnp.bfloat16).astype(jnp.float32)
+        section = grads_ref[...].astype(jnp.float32) + expert
+        rows_ref[...] = section.astype(jnp.bfloat16)
+        collect(rows_ref, out_refs)
+
+
+def pack(ids_row, rows, experts):
+    tokens, width = rows.shape
+    shape = jax.ShapeDtypeStruct((BASE_ROWS, width + width // CUTS), rows.dtype)
+    slots = experts * BASE_ROWS
+    return pl.pallas_call(
+        functools.partial(pack_kernel, experts),
+        out_shape=[shape] * experts,
+        compiler_params=pltpu.CompilerParams(vmem_limit_bytes=16 << 20),
+        cost_estimate=pl.CostEstimate(
+            flops=4 * slots * tokens * width,
+            bytes_accessed=2 * ROWS_BYTES * slots * width,
+            transcendentals=0,
+        ),
+        name="pack",
+    )(ids_row, rows)
+
+
+def unpack(ids_row, messages, experts):
+    tokens = ids_row.shape[1]
+    width = messages[0].shape[1] * CUTS // (CUTS + 1)
+    slots = experts * BASE_ROWS
+    return pl.pallas_call(
+        functools.partial(unpack_kernel, experts),
+        out_shape=jax.ShapeDtypeStruct((tokens, width), messages[0].dtype),
+        compiler_params=pltpu.CompilerParams(vmem_limit_bytes=16 << 20),
+        cost_estimate=pl.CostEstimate(
+            flops=4 * slots * tokens * width,
+            bytes_accessed=2 * ROWS_BYTES * slots * width,
+            transcendentals=0,
+        ),
+        name="unpack",
+    )(ids_row, *messages)
+
+
+def expert_call(kernel, name, router_rows, gate_cols, up_cols, down_rows, messages, experts, products):
+    width, units = gate_cols.shape
+    row_count = experts * (BASE_ROWS + CUTS)
+    steps = 4 if units % 512 == 0 else 1
+    part = units // steps
+    message_shape = messages[0].shape
+    whole = pl.BlockSpec(message_shape, lambda j: (0, 0))
+    extra_scratch = 2 if len(messages) > experts else 0
+    return pl.pallas_call(
+        functools.partial(kernel, experts),
+        grid=(steps,),
+        in_specs=[
+            pl.BlockSpec(router_rows.shape, lambda j: (0, 0)),
+            pl.BlockSpec((width, part), lambda j: (0, j)),
+            pl.BlockSpec((width, part), lambda j: (0, j)),
+            pl.BlockSpec((part, width), lambda j: (j, 0)),
+        ]
+        + [whole] * len(messages),
+        out_specs=[whole] * experts,
+        out_shape=[jax.ShapeDtypeStruct(message_shape, messages[0].dtype)] * experts,
+        scratch_shapes=[pltpu.VMEM((row_count, width), jnp.bfloat16)] * (1 + extra_scratch)
+        + [pltpu.VMEM((row_count, width), jnp.float32)],
+        compiler_params=pltpu.CompilerParams(vmem_limit_bytes=40 << 20),
+        cost_estimate=pl.CostEstimate(
+            flops=2 * products * row_count * width * units,
+            bytes_accessed=3 * ROWS_BYTES * width * units,
+            transcendentals=row_count * units,
+        ),
+        name=name,
+    )(router_rows, gate_cols, up_cols, down_rows, *messages)
+
+
+def exchanged(messages, experts):
+    return [messages[0]] + [
+        lax.ppermute(messages[k], "ep", [(i, i ^ k) for i in range(experts)])
+        for k in range(1, experts)
+    ]
+
+
+def returned(messages, experts, steps):
+    sections = lax.axis_size("pp")
+    back = []
+    for k in range(experts):
+        pairs = [
+            (p * experts + e, (p + steps) % sections * experts + (e ^ k))
+            for p in range(sections)
+            for e in range(experts)
+        ]
+        back.append(lax.ppermute(messages[k], ("pp", "ep"), pairs))
+    return back
+
+
+def per_device_whole(fwd_in, fwd_ids, saved_in, bwd_ids, grad_in, router, w_gate, w_up, w_down):
+    experts = router.shape[-1]
+    token_count = fwd_in.shape[1]
+    router_rows = router[0].T
+    weights = (w_gate[0], w_up[0], w_down[0])
+    fwd_row = fwd_ids.reshape(1, token_count)
+    bwd_row = bwd_ids.reshape(1, token_count)
+    fwd_rows = exchanged(pack(fwd_row, fwd_in[0], experts), experts)
+    saved_rows = exchanged(pack(bwd_row, saved_in[0], experts), experts)
+    grad_rows = exchanged(pack(bwd_row, grad_in[0], experts), experts)
+    fwd_row_next = from_behind(fwd_row, "pp", 1)
+    bwd_row_next = from_behind(bwd_row, "pp", -1)
+    fwd_out = expert_call(forward_kernel, "forward", router_rows, *weights, fwd_rows, experts, 3)
+    fwd_back = returned(fwd_out, experts, 1)
+    bwd_out = expert_call(
+        backward_kernel, "backward", router_rows, *weights, saved_rows + grad_rows, experts, 5
+    )
+    bwd_back = returned(bwd_out, experts, -1)
+    fwd_next = unpack(fwd_row_next, fwd_back, experts)
+    grad_next = unpack(bwd_row_next, bwd_back, experts)
+    return (fwd_next[None], grad_next[None])
+
+
 def solution(mesh):
     in_specs = (
         P("pp", "ep", None),
@@ -203,6 +508,23 @@
         P("pp", "ep", None),
     )
     out_specs = (P("pp", "ep", None), P("pp", "ep", None))
-    return jax.shard_map(
-        per_device, mesh=mesh, in_specs=in_specs, out_specs=out_specs, check_vma=False
-    )
+
+    def layer(*arrays):
+        token_count = arrays[0].shape[1] // mesh.shape["ep"]
+        width = arrays[0].shape[2]
+        experts = arrays[5].shape[-1]
+        whole = (
+            mesh.shape["ep"] == experts
+            and experts & (experts - 1) == 0
+            and 5 * token_count // (4 * experts) == BASE_ROWS + CUTS
+            and width % (128 * CUTS) == 0
+        )
+        return jax.shard_map(
+            per_device_whole if whole else per_device,
+            mesh=mesh,
+            in_specs=in_specs,
+            out_specs=out_specs,
+            check_vma=False,
+        )(*arrays)
+
+    return layer

time: 223 us -> 168 us (0.75)
  the two profiles are of different devices: /device:TPU:0 before, /device:TPU:9 now
where the time goes in v1:
time: 168 us; the launch traced here: 167 us
  starting transfers between devices  75.4 us (45%)
  waiting for transfers between devices  46.2 us (28%)
  Pallas kernels  37.1 us (22%)
  local copies, waits for them, and re-layouts  7.52 us (4%)
    ppermute x16, starting transfers between devices, returned(): back.append(lax.ppermute(messages[k], ('pp', 'ep'), pairs))  37.7 us
    pallas_call x2, Pallas kernels, expert_call(): pl.pallas_call(functools.partial(kernel, experts), grid=(steps,), in_spec...  29.3 us
    ppermute x21, waiting for transfers between devices, exchanged(): lax.ppermute(messages[k], 'ep', [(i, i ^ k) for i in range(experts)])  29.2 us
    ppermute x21, starting transfers between devices, exchanged(): lax.ppermute(messages[k], 'ep', [(i, i ^ k) for i in range(experts)])  24.1 us
    ppermute x16, waiting for transfers between devices, returned(): back.append(lax.ppermute(messages[k], ('pp', 'ep'), pairs))  16.9 us
    ppermute x2, starting transfers between devices, from_behind(): return lax.ppermute(value, axis, pairs)  13.5 us
    unnamed x14, local copies, waits for them, and re-layouts  7.52 us
    pallas_call x3, Pallas kernels, pack(): pl.pallas_call(functools.partial(pack_kernel, experts), out_shape=[shape]...  4.24 us
  transfers between devices with their start and end apart: 39, of which 13 were waited for; matrix products, arithmetic and copies ran while one was open for 0% of the time, Pallas kernels for 20%

profile of v1, /device:TPU:9, one launch (start us, length us, event | category | flops | bytes accessed | tf_op | source)
XLA Modules:
  0.0 166.9 jit_solution(4234252253576217610)
XLA Ops:
  5.9 2.3 %collective-permute-start.20 = (bf16[16,4480]{1,0:T(8,128)(2,1)S(1)}, bf16[16,4480]{1,0:T(8,128)(2,1)S(1)}, u32[]{:S(2)}, u32[]{:S(2)}) collective-permute-start(bf16[16,4480]{1,0:T(8,128)(2,1)S(1)} %get-tuple-element.62), channel_id=1, source_target_pairs={{0,4},{1,5},{2,6},{3,7},{4,0},{5,1},{6,2},{7,3},{8,12},{9,13},{10,... | collective-permute-start | bytes 430088 | tf_op jit(solution)/shard_map/ppermute | solution.py:457
  16.0 2.5 %collective-permute-start.25 = (bf16[16,4480]{1,0:T(8,128)(2,1)S(1)}, bf16[16,4480]{1,0:T(8,128)(2,1)S(1)}, u32[]{:S(2)}, u32[]{:S(2)}) collective-permute-start(bf16[16,4480]{1,0:T(8,128)(2,1)S(1)} %get-tuple-element.68), channel_id=1, source_target_pairs={{0,2},{1,3},{2,0},{3,1},{4,6},{5,7},{6,4},{7,5},{8,10},{9,11},{10,... | collective-permute-start | bytes 430088 | tf_op jit(solution)/shard_map/ppermute | solution.py:457
  18.5 5.3 %collective-permute-done.21.refs_5_ = bf16[16,4480]{1,0:T(8,128)(2,1)S(1)} collective-permute-done((bf16[16,4480]{1,0:T(8,128)(2,1)S(1)}, bf16[16,4480]{1,0:T(8,128)(2,1)S(1)}, u32[]{:S(2)}, u32[]{:S(2)}) %collective-permute-start.21) | collective-permute-done | bytes 143392 | tf_op jit(solution)/shard_map/ppermute | solution.py:457
  23.9 5.3 %collective-permute-done.22.refs_6_ = bf16[16,4480]{1,0:T(8,128)(2,1)S(1)} collective-permute-done((bf16[16,4480]{1,0:T(8,128)(2,1)S(1)}, bf16[16,4480]{1,0:T(8,128)(2,1)S(1)}, u32[]{:S(2)}, u32[]{:S(2)}) %collective-permute-start.22) | collective-permute-done | bytes 143392 | tf_op jit(solution)/shard_map/ppermute | solution.py:457
  29.5 3.8 %collective-permute-done.23.refs_7_ = bf16[16,4480]{1,0:T(8,128)(2,1)S(1)} collective-permute-done((bf16[16,4480]{1,0:T(8,128)(2,1)S(1)}, bf16[16,4480]{1,0:T(8,128)(2,1)S(1)}, u32[]{:S(2)}, u32[]{:S(2)}) %collective-permute-start.23) | collective-permute-done | bytes 143392 | tf_op jit(solution)/shard_map/ppermute | solution.py:457
  37.3 12.3 %collective-permute-start.16 = (s32[1,128]{1,0:T(1,128)}, s32[1,128]{1,0:T(1,128)S(1)}, u32[]{:S(2)}, u32[]{:S(2)}) collective-permute-start(s32[1,128]{1,0:T(1,128)} %bitcast.8.ids_ref), channel_id=1, source_target_pairs={{0,24},{8,0},{16,8},{24,16},{1,25},{9,1},{17,9},{25,17},{2,26},{10... | collective-permute-start | bytes 1544 | tf_op jit(solution)/shard_map/ppermute | solution.py:29
  51.6 5.3 %collective-permute-start.2 = (bf16[16,4480]{1,0:T(8,128)(2,1)S(1)}, bf16[16,4480]{1,0:T(8,128)(2,1)S(1)}, u32[]{:S(2)}, u32[]{:S(2)}) collective-permute-start(bf16[16,4480]{1,0:T(8,128)(2,1)S(1)} %get-tuple-element.44), channel_id=1, source_target_pairs={{0,2},{1,3},{2,0},{3,1},{4,6},{5,7},{6,4},{7,5},{8,10},{9,11},{10,... | collective-permute-start | bytes 430088 | tf_op jit(solution)/shard_map/ppermute | solution.py:457
  57.5 3.1 %copy-done = bf16[1,3584,1024]{2,1,0:T(8,128)(2,1)S(1)} copy-done((bf16[1,3584,1024]{2,1,0:T(8,128)(2,1)S(1)}, bf16[1,3584,1024]{2,1,0:T(8,128)(2,1)}, u32[]{:S(2)}) %copy-start) | copy-done | bytes 7340056
  61.5 19.0 %backward.1 = (bf16[16,4480]{1,0:T(8,128)(2,1)S(1)}, bf16[16,4480]{1,0:T(8,128)(2,1)S(1)}, bf16[16,4480]{1,0:T(8,128)(2,1)S(1)}, bf16[16,4480]{1,0:T(8,128)(2,1)...) custom-call(f32[8,3584]{1,0:T(8,128)S(1)} %bitcast.18, ...), custom_call_target="tpu_custom_call" | custom-call | flops 5872025600 | bytes 22020096 | tf_op jit(solution)/shard_map/backward/pallas_call | solution.py:431
  80.5 2.5 %collective-permute-start.4 = (bf16[16,4480]{1,0:T(8,128)(2,1)S(1)}, bf16[16,4480]{1,0:T(8,128)(2,1)S(1)}, u32[]{:S(2)}, u32[]{:S(2)}) collective-permute-start(bf16[16,4480]{1,0:T(8,128)(2,1)S(1)} %get-tuple-element.46), channel_id=1, source_target_pairs={{0,4},{1,5},{2,6},{3,7},{4,0},{5,1},{6,2},{7,3},{8,12},{9,13},{10,... | collective-permute-start | bytes 430088 | tf_op jit(solution)/shard_map/ppermute | solution.py:457
  85.9 3.5 %collective-permute-start.31 = (bf16[16,4480]{1,0:T(8,128)(2,1)S(1)}, bf16[16,4480]{1,0:T(8,128)(2,1)S(1)}, u32[]{:S(2)}, u32[]{:S(2)}) collective-permute-start(bf16[16,4480]{1,0:T(8,128)(2,1)S(1)} %get-tuple-element.74), channel_id=1, source_target_pairs={{0,24},{1,25},{2,26},{3,27},{4,28},{5,29},{6,30},{7,31},{8,0},{9,1... | collective-permute-start | bytes 430088 | tf_op jit(solution)/shard_map/ppermute | solution.py:471
  89.4 9.2 %collective-permute-done.4.refs_4_ = bf16[16,4480]{1,0:T(8,128)(2,1)S(1)} collective-permute-done((bf16[16,4480]{1,0:T(8,128)(2,1)S(1)}, bf16[16,4480]{1,0:T(8,128)(2,1)S(1)}, u32[]{:S(2)}, u32[]{:S(2)}) %collective-permute-start.4) | collective-permute-done | bytes 143392 | tf_op jit(solution)/shard_map/ppermute | solution.py:457
  101.7 4.3 %collective-permute-start.33 = (bf16[16,4480]{1,0:T(8,128)(2,1)S(1)}, bf16[16,4480]{1,0:T(8,128)(2,1)S(1)}, u32[]{:S(2)}, u32[]{:S(2)}) collective-permute-start(bf16[16,4480]{1,0:T(8,128)(2,1)S(1)} %get-tuple-element.76), channel_id=1, source_target_pairs={{0,26},{1,27},{2,24},{3,25},{4,30},{5,31},{6,28},{7,29},{8,2},{9,3... | collective-permute-start | bytes 430088 | tf_op jit(solution)/shard_map/ppermute | solution.py:471
  109.3 2.6 %collective-permute-start.36 = (bf16[16,4480]{1,0:T(8,128)(2,1)S(1)}, bf16[16,4480]{1,0:T(8,128)(2,1)S(1)}, u32[]{:S(2)}, u32[]{:S(2)}) collective-permute-start(bf16[16,4480]{1,0:T(8,128)(2,1)S(1)} %get-tuple-element.79), channel_id=1, source_target_pairs={{0,29},{1,28},{2,31},{3,30},{4,25},{5,24},{6,27},{7,26},{8,5},{9,4... | collective-permute-start | bytes 430088 | tf_op jit(solution)/shard_map/ppermute | solution.py:471
  111.9 10.3 %forward.1 = (bf16[16,4480]{1,0:T(8,128)(2,1)S(1)}, bf16[16,4480]{1,0:T(8,128)(2,1)S(1)}, bf16[16,4480]{1,0:T(8,128)(2,1)S(1)}, bf16[16,4480]{1,0:T(8,128)(2,1)S...) custom-call(f32[8,3584]{1,0:T(8,128)S(1)} %bitcast.19, ...), custom_call_target="tpu_custom_call" | custom-call | flops 3523215360 | bytes 22020096 | tf_op jit(solution)/shard_map/forward/pallas_call | solution.py:431
  122.2 3.5 %collective-permute-start.37 = (bf16[16,4480]{1,0:T(8,128)(2,1)S(1)}, bf16[16,4480]{1,0:T(8,128)(2,1)S(1)}, u32[]{:S(2)}, u32[]{:S(2)}) collective-permute-start(bf16[16,4480]{1,0:T(8,128)(2,1)S(1)} %get-tuple-element.80), channel_id=1, source_target_pairs={{0,30},{1,31},{2,28},{3,29},{4,26},{5,27},{6,24},{7,25},{8,6},{9,7... | collective-permute-start | bytes 430088 | tf_op jit(solution)/shard_map/ppermute | solution.py:471
  125.8 2.5 %collective-permute-start.10 = (bf16[16,4480]{1,0:T(8,128)(2,1)S(1)}, bf16[16,4480]{1,0:T(8,128)(2,1)S(1)}, u32[]{:S(2)}, u32[]{:S(2)}) collective-permute-start(bf16[16,4480]{1,0:T(8,128)(2,1)S(1)} %get-tuple-element.52), channel_id=1, source_target_pairs={{0,10},{1,11},{2,8},{3,9},{4,14},{5,15},{6,12},{7,13},{8,18},{9,19... | collective-permute-start | bytes 430088 | tf_op jit(solution)/shard_map/ppermute | solution.py:471
  129.2 2.2 %collective-permute-start.12 = (bf16[16,4480]{1,0:T(8,128)(2,1)S(1)}, bf16[16,4480]{1,0:T(8,128)(2,1)S(1)}, u32[]{:S(2)}, u32[]{:S(2)}) collective-permute-start(bf16[16,4480]{1,0:T(8,128)(2,1)S(1)} %get-tuple-element.54), channel_id=1, source_target_pairs={{0,12},{1,13},{2,14},{3,15},{4,8},{5,9},{6,10},{7,11},{8,20},{9,21... | collective-permute-start | bytes 430088 | tf_op jit(solution)/shard_map/ppermute | solution.py:471
  131.3 4.9 %collective-permute-done.37.refs_6_ = bf16[16,4480]{1,0:T(8,128)(2,1)S(1)} collective-permute-done((bf16[16,4480]{1,0:T(8,128)(2,1)S(1)}, bf16[16,4480]{1,0:T(8,128)(2,1)S(1)}, u32[]{:S(2)}, u32[]{:S(2)}) %collective-permute-start.37) | collective-permute-done | bytes 143392 | tf_op jit(solution)/shard_map/ppermute | solution.py:471
  136.2 4.6 %collective-permute-done.38.refs_7_ = bf16[16,4480]{1,0:T(8,128)(2,1)S(1)} collective-permute-done((bf16[16,4480]{1,0:T(8,128)(2,1)S(1)}, bf16[16,4480]{1,0:T(8,128)(2,1)S(1)}, u32[]{:S(2)}, u32[]{:S(2)}) %collective-permute-start.38) | collective-permute-done | bytes 143392 | tf_op jit(solution)/shard_map/ppermute | solution.py:471
  140.8 2.4 %collective-permute-start.14 = (bf16[16,4480]{1,0:T(8,128)(2,1)S(1)}, bf16[16,4480]{1,0:T(8,128)(2,1)S(1)}, u32[]{:S(2)}, u32[]{:S(2)}) collective-permute-start(bf16[16,4480]{1,0:T(8,128)(2,1)S(1)} %get-tuple-element.56), channel_id=1, source_target_pairs={{0,14},{1,15},{2,12},{3,13},{4,10},{5,11},{6,8},{7,9},{8,22},{9,23... | collective-permute-start | bytes 430088 | tf_op jit(solution)/shard_map/ppermute | solution.py:471
  143.2 12.7 %collective-permute-start.15 = (bf16[16,4480]{1,0:T(8,128)(2,1)S(1)}, bf16[16,4480]{1,0:T(8,128)(2,1)S(1)}, u32[]{:S(2)}, u32[]{:S(2)}) collective-permute-start(bf16[16,4480]{1,0:T(8,128)(2,1)S(1)} %get-tuple-element.57), channel_id=1, source_target_pairs={{0,15},{1,14},{2,13},{3,12},{4,11},{5,10},{6,9},{7,8},{8,23},{9,22... | collective-permute-start | bytes 430088 | tf_op jit(solution)/shard_map/ppermute | solution.py:471
  157.7 4.1 %collective-permute-done.14.refs_6_ = bf16[16,4480]{1,0:T(8,128)(2,1)S(1)} collective-permute-done((bf16[16,4480]{1,0:T(8,128)(2,1)S(1)}, bf16[16,4480]{1,0:T(8,128)(2,1)S(1)}, u32[]{:S(2)}, u32[]{:S(2)}) %collective-permute-start.14) | collective-permute-done | bytes 143392 | tf_op jit(solution)/shard_map/ppermute | solution.py:471
  161.8 3.1 %collective-permute-done.15.refs_7_ = bf16[16,4480]{1,0:T(8,128)(2,1)S(1)} collective-permute-done((bf16[16,4480]{1,0:T(8,128)(2,1)S(1)}, bf16[16,4480]{1,0:T(8,128)(2,1)S(1)}, u32[]{:S(2)}, u32[]{:S(2)}) %collective-permute-start.15) | collective-permute-done | bytes 143392 | tf_op jit(solution)/shard_map/ppermute | solution.py:471
  (75 shorter events, 34.8 us)
Async XLA Ops:
  13.2 20.1 %collective-permute-start.23 = (bf16[16,4480]{1,0:T(8,128)(2,1)S(1)}, bf16[16,4480]{1,0:T(8,128)(2,1)S(1)}, u32[]{:S(2)}, u32[]{:S(2)}) collective-permute-start(bf16[16,4480]{1,0:T(8,128)(2,1)S(1)} %get-tuple-element.65), channel_id=1, source_target_pairs={{0,7},{1,6},{2,5},{3,4},{4,3},{5,2},{6,1},{7,0},{8,15},{9,14},{10,... | collective-permute-start | bytes 430088 | tf_op jit(solution)/shard_map/ppermute | solution.py:457
  14.9 18.4 %collective-permute-start.24 = (bf16[16,4480]{1,0:T(8,128)(2,1)S(1)}, bf16[16,4480]{1,0:T(8,128)(2,1)S(1)}, u32[]{:S(2)}, u32[]{:S(2)}) collective-permute-start(bf16[16,4480]{1,0:T(8,128)(2,1)S(1)} %get-tuple-element.67), channel_id=1, source_target_pairs={{0,1},{1,0},{2,3},{3,2},{4,5},{5,4},{6,7},{7,6},{8,9},{9,8},{10,11... | collective-permute-start | bytes 430088 | tf_op jit(solution)/shard_map/ppermute | solution.py:457
  16.0 18.7 %collective-permute-start.25 = (bf16[16,4480]{1,0:T(8,128)(2,1)S(1)}, bf16[16,4480]{1,0:T(8,128)(2,1)S(1)}, u32[]{:S(2)}, u32[]{:S(2)}) collective-permute-start(bf16[16,4480]{1,0:T(8,128)(2,1)S(1)} %get-tuple-element.68), channel_id=1, source_target_pairs={{0,2},{1,3},{2,0},{3,1},{4,6},{5,7},{6,4},{7,5},{8,10},{9,11},{10,... | collective-permute-start | bytes 430088 | tf_op jit(solution)/shard_map/ppermute | solution.py:457
  29.2 20.5 %collective-permute-start.27 = (bf16[16,4480]{1,0:T(8,128)(2,1)S(1)}, bf16[16,4480]{1,0:T(8,128)(2,1)S(1)}, u32[]{:S(2)}, u32[]{:S(2)}) collective-permute-start(bf16[16,4480]{1,0:T(8,128)(2,1)S(1)} %get-tuple-element.70), channel_id=1, source_target_pairs={{0,4},{1,5},{2,6},{3,7},{4,0},{5,1},{6,2},{7,3},{8,12},{9,13},{10,... | collective-permute-start | bytes 430088 | tf_op jit(solution)/shard_map/ppermute | solution.py:457
  34.7 22.3 %collective-permute-start.30 = (bf16[16,4480]{1,0:T(8,128)(2,1)S(1)}, bf16[16,4480]{1,0:T(8,128)(2,1)S(1)}, u32[]{:S(2)}, u32[]{:S(2)}) collective-permute-start(bf16[16,4480]{1,0:T(8,128)(2,1)S(1)} %get-tuple-element.73), channel_id=1, source_target_pairs={{0,7},{1,6},{2,5},{3,4},{4,3},{5,2},{6,1},{7,0},{8,15},{9,14},{10,... | collective-permute-start | bytes 430088 | tf_op jit(solution)/shard_map/ppermute | solution.py:457
  37.3 43.2 %collective-permute-start.16 = (s32[1,128]{1,0:T(1,128)}, s32[1,128]{1,0:T(1,128)S(1)}, u32[]{:S(2)}, u32[]{:S(2)}) collective-permute-start(s32[1,128]{1,0:T(1,128)} %bitcast.8.ids_ref), channel_id=1, source_target_pairs={{0,24},{8,0},{16,8},{24,16},{1,25},{9,1},{17,9},{25,17},{2,26},{10... | collective-permute-start | bytes 1544 | tf_op jit(solution)/shard_map/ppermute | solution.py:29
  49.6 33.4 %collective-permute-start = (s32[1,128]{1,0:T(1,128)}, s32[1,128]{1,0:T(1,128)S(1)}, u32[]{:S(2)}, u32[]{:S(2)}) collective-permute-start(s32[1,128]{1,0:T(1,128)} %bitcast.ids_ref), channel_id=1, source_target_pairs={{0,8},{8,16},{16,24},{24,0},{1,9},{9,17},{17,25},{25,1},{2,10},{10... | collective-permute-start | bytes 1544 | tf_op jit(solution)/shard_map/ppermute | solution.py:29
  50.8 33.6 %collective-permute-start.1 = (bf16[16,4480]{1,0:T(8,128)(2,1)S(1)}, bf16[16,4480]{1,0:T(8,128)(2,1)S(1)}, u32[]{:S(2)}, u32[]{:S(2)}) collective-permute-start(bf16[16,4480]{1,0:T(8,128)(2,1)S(1)} %get-tuple-element.43), channel_id=1, source_target_pairs={{0,1},{1,0},{2,3},{3,2},{4,5},{5,4},{6,7},{7,6},{8,9},{9,8},{10,11... | collective-permute-start | bytes 430088 | tf_op jit(solution)/shard_map/ppermute | solution.py:457
  51.6 32.9 %collective-permute-start.2 = (bf16[16,4480]{1,0:T(8,128)(2,1)S(1)}, bf16[16,4480]{1,0:T(8,128)(2,1)S(1)}, u32[]{:S(2)}, u32[]{:S(2)}) collective-permute-start(bf16[16,4480]{1,0:T(8,128)(2,1)S(1)} %get-tuple-element.44), channel_id=1, source_target_pairs={{0,2},{1,3},{2,0},{3,1},{4,6},{5,7},{6,4},{7,5},{8,10},{9,11},{10,... | collective-permute-start | bytes 430088 | tf_op jit(solution)/shard_map/ppermute | solution.py:457
  56.9 29.0 %collective-permute-start.3 = (bf16[16,4480]{1,0:T(8,128)(2,1)S(1)}, bf16[16,4480]{1,0:T(8,128)(2,1)S(1)}, u32[]{:S(2)}, u32[]{:S(2)}) collective-permute-start(bf16[16,4480]{1,0:T(8,128)(2,1)S(1)} %get-tuple-element.45), channel_id=1, source_target_pairs={{0,3},{1,2},{2,1},{3,0},{4,7},{5,6},{6,5},{7,4},{8,11},{9,10},{10,... | collective-permute-start | bytes 430088 | tf_op jit(solution)/shard_map/ppermute | solution.py:457
  83.1 18.6 %collective-permute-start.5 = (bf16[16,4480]{1,0:T(8,128)(2,1)S(1)}, bf16[16,4480]{1,0:T(8,128)(2,1)S(1)}, u32[]{:S(2)}, u32[]{:S(2)}) collective-permute-start(bf16[16,4480]{1,0:T(8,128)(2,1)S(1)} %get-tuple-element.47), channel_id=1, source_target_pairs={{0,5},{1,4},{2,7},{3,6},{4,1},{5,0},{6,3},{7,2},{8,13},{9,12},{10,... | collective-permute-start | bytes 430088 | tf_op jit(solution)/shard_map/ppermute | solution.py:457
  84.5 21.5 %collective-permute-start.6 = (bf16[16,4480]{1,0:T(8,128)(2,1)S(1)}, bf16[16,4480]{1,0:T(8,128)(2,1)S(1)}, u32[]{:S(2)}, u32[]{:S(2)}) collective-permute-start(bf16[16,4480]{1,0:T(8,128)(2,1)S(1)} %get-tuple-element.48), channel_id=1, source_target_pairs={{0,6},{1,7},{2,4},{3,5},{4,2},{5,3},{6,0},{7,1},{8,14},{9,15},{10,... | collective-permute-start | bytes 430088 | tf_op jit(solution)/shard_map/ppermute | solution.py:457
  84.5 23.6 %collective-permute-start.7 = (bf16[16,4480]{1,0:T(8,128)(2,1)S(1)}, bf16[16,4480]{1,0:T(8,128)(2,1)S(1)}, u32[]{:S(2)}, u32[]{:S(2)}) collective-permute-start(bf16[16,4480]{1,0:T(8,128)(2,1)S(1)} %get-tuple-element.49), channel_id=1, source_target_pairs={{0,7},{1,6},{2,5},{3,4},{4,3},{5,2},{6,1},{7,0},{8,15},{9,14},{10,... | collective-permute-start | bytes 430088 | tf_op jit(solution)/shard_map/ppermute | solution.py:457
  85.9 23.4 %collective-permute-start.31 = (bf16[16,4480]{1,0:T(8,128)(2,1)S(1)}, bf16[16,4480]{1,0:T(8,128)(2,1)S(1)}, u32[]{:S(2)}, u32[]{:S(2)}) collective-permute-start(bf16[16,4480]{1,0:T(8,128)(2,1)S(1)} %get-tuple-element.74), channel_id=1, source_target_pairs={{0,24},{1,25},{2,26},{3,27},{4,28},{5,29},{6,30},{7,31},{8,0},{9,1... | collective-permute-start | bytes 430088 | tf_op jit(solution)/shard_map/ppermute | solution.py:471
  98.6 23.6 %collective-permute-start.32 = (bf16[16,4480]{1,0:T(8,128)(2,1)S(1)}, bf16[16,4480]{1,0:T(8,128)(2,1)S(1)}, u32[]{:S(2)}, u32[]{:S(2)}) collective-permute-start(bf16[16,4480]{1,0:T(8,128)(2,1)S(1)} %get-tuple-element.75), channel_id=1, source_target_pairs={{0,25},{1,24},{2,27},{3,26},{4,29},{5,28},{6,31},{7,30},{8,1},{9,0... | collective-permute-start | bytes 430088 | tf_op jit(solution)/shard_map/ppermute | solution.py:471
  101.7 24.1 %collective-permute-start.33 = (bf16[16,4480]{1,0:T(8,128)(2,1)S(1)}, bf16[16,4480]{1,0:T(8,128)(2,1)S(1)}, u32[]{:S(2)}, u32[]{:S(2)}) collective-permute-start(bf16[16,4480]{1,0:T(8,128)(2,1)S(1)} %get-tuple-element.76), channel_id=1, source_target_pairs={{0,26},{1,27},{2,24},{3,25},{4,30},{5,31},{6,28},{7,29},{8,2},{9,3... | collective-permute-start | bytes 430088 | tf_op jit(solution)/shard_map/ppermute | solution.py:471
  106.0 19.8 %collective-permute-start.34 = (bf16[16,4480]{1,0:T(8,128)(2,1)S(1)}, bf16[16,4480]{1,0:T(8,128)(2,1)S(1)}, u32[]{:S(2)}, u32[]{:S(2)}) collective-permute-start(bf16[16,4480]{1,0:T(8,128)(2,1)S(1)} %get-tuple-element.77), channel_id=1, source_target_pairs={{0,27},{1,26},{2,25},{3,24},{4,31},{5,30},{6,29},{7,28},{8,3},{9,2... | collective-permute-start | bytes 430088 | tf_op jit(solution)/shard_map/ppermute | solution.py:471
  108.1 20.2 %collective-permute-start.35 = (bf16[16,4480]{1,0:T(8,128)(2,1)S(1)}, bf16[16,4480]{1,0:T(8,128)(2,1)S(1)}, u32[]{:S(2)}, u32[]{:S(2)}) collective-permute-start(bf16[16,4480]{1,0:T(8,128)(2,1)S(1)} %get-tuple-element.78), channel_id=1, source_target_pairs={{0,28},{1,29},{2,30},{3,31},{4,24},{5,25},{6,26},{7,27},{8,4},{9,5... | collective-permute-start | bytes 430088 | tf_op jit(solution)/shard_map/ppermute | solution.py:471
  109.3 19.9 %collective-permute-start.36 = (bf16[16,4480]{1,0:T(8,128)(2,1)S(1)}, bf16[16,4480]{1,0:T(8,128)(2,1)S(1)}, u32[]{:S(2)}, u32[]{:S(2)}) collective-permute-start(bf16[16,4480]{1,0:T(8,128)(2,1)S(1)} %get-tuple-element.79), channel_id=1, source_target_pairs={{0,29},{1,28},{2,31},{3,30},{4,25},{5,24},{6,27},{7,26},{8,5},{9,4... | collective-permute-start | bytes 430088 | tf_op jit(solution)/shard_map/ppermute | solution.py:471
  128.3 27.6 %collective-permute-start.11 = (bf16[16,4480]{1,0:T(8,128)(2,1)S(1)}, bf16[16,4480]{1,0:T(8,128)(2,1)S(1)}, u32[]{:S(2)}, u32[]{:S(2)}) collective-permute-start(bf16[16,4480]{1,0:T(8,128)(2,1)S(1)} %get-tuple-element.53), channel_id=1, source_target_pairs={{0,11},{1,10},{2,9},{3,8},{4,15},{5,14},{6,13},{7,12},{8,19},{9,18... | collective-permute-start | bytes 430088 | tf_op jit(solution)/shard_map/ppermute | solution.py:471
  129.2 26.7 %collective-permute-start.12 = (bf16[16,4480]{1,0:T(8,128)(2,1)S(1)}, bf16[16,4480]{1,0:T(8,128)(2,1)S(1)}, u32[]{:S(2)}, u32[]{:S(2)}) collective-permute-start(bf16[16,4480]{1,0:T(8,128)(2,1)S(1)} %get-tuple-element.54), channel_id=1, source_target_pairs={{0,12},{1,13},{2,14},{3,15},{4,8},{5,9},{6,10},{7,11},{8,20},{9,21... | collective-permute-start | bytes 430088 | tf_op jit(solution)/shard_map/ppermute | solution.py:471
  136.2 21.5 %collective-permute-start.13 = (bf16[16,4480]{1,0:T(8,128)(2,1)S(1)}, bf16[16,4480]{1,0:T(8,128)(2,1)S(1)}, u32[]{:S(2)}, u32[]{:S(2)}) collective-permute-start(bf16[16,4480]{1,0:T(8,128)(2,1)S(1)} %get-tuple-element.55), channel_id=1, source_target_pairs={{0,13},{1,12},{2,15},{3,14},{4,9},{5,8},{6,11},{7,10},{8,21},{9,20... | collective-permute-start | bytes 430088 | tf_op jit(solution)/shard_map/ppermute | solution.py:471
  140.8 21.0 %collective-permute-start.14 = (bf16[16,4480]{1,0:T(8,128)(2,1)S(1)}, bf16[16,4480]{1,0:T(8,128)(2,1)S(1)}, u32[]{:S(2)}, u32[]{:S(2)}) collective-permute-start(bf16[16,4480]{1,0:T(8,128)(2,1)S(1)} %get-tuple-element.56), channel_id=1, source_target_pairs={{0,14},{1,15},{2,12},{3,13},{4,10},{5,11},{6,8},{7,9},{8,22},{9,23... | collective-permute-start | bytes 430088 | tf_op jit(solution)/shard_map/ppermute | solution.py:471
  143.2 21.7 %collective-permute-start.15 = (bf16[16,4480]{1,0:T(8,128)(2,1)S(1)}, bf16[16,4480]{1,0:T(8,128)(2,1)S(1)}, u32[]{:S(2)}, u32[]{:S(2)}) collective-permute-start(bf16[16,4480]{1,0:T(8,128)(2,1)S(1)} %get-tuple-element.57), channel_id=1, source_target_pairs={{0,15},{1,14},{2,13},{3,12},{4,11},{5,10},{6,9},{7,8},{8,23},{9,22... | collective-permute-start | bytes 430088 | tf_op jit(solution)/shard_map/ppermute | solution.py:471
  (22 other events, 310.9 us)

commit v2 on v1

--- a/solution.py
+++ b/solution.py
@@ -197,6 +197,7 @@
 BASE_ROWS = 16
 CUTS = 4
 ROWS_BYTES = 2
+VMEM_BYTES = 44 << 20
 
 
 def transposed_dot(left, right):
@@ -230,27 +231,47 @@
     return base, pieces
 
 
-def pack_kernel(experts, ids_ref, x_ref, *out_refs):
+def pack_kernel(kind, joined, count, experts, ids_ref, *refs):
+    x_refs = refs[:count]
+    held_ref, made_ref, sems, out_sems = refs[-4:]
+    copies = [pltpu.make_async_copy(x_refs[n], held_ref.at[n], sems.at[n]) for n in range(count)]
+    for copy in copies:
+        copy.start()
+    width = held_ref.shape[2]
+    piece = width // CUTS
+    first = 0 if joined else lax.axis_index("ep")
+    base, pieces = slot_masks(ids_ref[kind : kind + 1], first, experts)
+    for n, copy in enumerate(copies):
+        rows = slice(n * BASE_ROWS, (n + 1) * BASE_ROWS)
+        copy.wait()
+        extra = 0.0
+        for q in range(CUTS):
+            columns = slice(q * piece, (q + 1) * piece)
+            part = held_ref[n, :, columns]
+            packed = plain_dot(base, part).astype(jnp.bfloat16)
+            extra = extra + plain_dot(pieces[q], part)
+            for k in range(experts):
+                made_ref[k, rows, columns] = packed[k * BASE_ROWS : (k + 1) * BASE_ROWS]
+        extra = extra.astype(jnp.bfloat16)
+        for k in range(experts):
+            made_ref[k, rows, width:] = extra[k * BASE_ROWS : (k + 1) * BASE_ROWS]
+    if joined:
+        copies = [pltpu.make_async_copy(made_ref, refs[-5], out_sems.at[0])]
+    else:
+        out_refs = refs[-4 - experts : -4]
+        copies = [
+            pltpu.make_async_copy(made_ref.at[k], out_refs[k], out_sems.at[k]) for k in range(experts)
+        ]
+    for copy in copies:
+        copy.start()
+    for copy in copies:
+        copy.wait()
+
+
+def unpack_kernel(order, ids_ref, *refs):
     me = lax.axis_index("ep")
-    width = x_ref.shape[1]
-    piece = width // CUTS
-    base, pieces = slot_masks(ids_ref[...], me, experts)
-    for q in range(CUTS):
-        columns = slice(q * piece, (q + 1) * piece)
-        packed = plain_dot(base, x_ref[:, columns]).astype(jnp.bfloat16)
-        for k in range(experts):
-            out_refs[k][:, columns] = packed[k * BASE_ROWS : (k + 1) * BASE_ROWS]
-    extra = plain_dot(pieces[0], x_ref[:, :piece])
-    for q in range(1, CUTS):
-        extra = extra + plain_dot(pieces[q], x_ref[:, q * piece : (q + 1) * piece])
-    extra = extra.astype(jnp.bfloat16)
-    for k in range(experts):
-        out_refs[k][:, width:] = extra[k * BASE_ROWS : (k + 1) * BASE_ROWS]
-
-
-def unpack_kernel(experts, ids_ref, *refs):
-    me = lax.axis_index("ep")
-    message_refs, out_ref = refs[:experts], refs[experts]
+    experts = len(order)
+    message_refs, out_ref = [refs[order.index(k)] for k in range(experts)], refs[experts]
     width = out_ref.shape[1]
     piece = width // CUTS
     base, pieces = slot_masks(ids_ref[...], me, experts)
@@ -274,20 +295,33 @@
     return jnp.where(same, 1.0, 0.0).astype(jnp.bfloat16)
 
 
-def spread(message_refs, rows_ref):
-    experts = len(message_refs)
+def message_copies(message_refs, place, rows_ref, extra_ref, sems):
+    width = rows_ref.shape[1]
+    taken = slice(place * BASE_ROWS, (place + 1) * BASE_ROWS)
+    copies = []
+    for k, ref in enumerate(message_refs):
+        rows = slice(k * BASE_ROWS, (k + 1) * BASE_ROWS)
+        parts = ((ref.at[taken, :width], rows_ref), (ref.at[taken, width:], extra_ref))
+        for n, (source, target) in enumerate(parts):
+            copies.append(pltpu.make_async_copy(source, target.at[rows, :], sems.at[n, k]))
+    for copy in copies:
+        copy.start()
+    return copies
+
+
+def spread(copies, rows_ref, extra_ref):
     width = rows_ref.shape[1]
     piece = width // CUTS
-    first = experts * BASE_ROWS
-    for k, ref in enumerate(message_refs):
-        rows_ref[k * BASE_ROWS : (k + 1) * BASE_ROWS, :] = ref[:, :width]
-    extra = jnp.concatenate([ref[:, width:] for ref in message_refs], axis=0)
+    experts = extra_ref.shape[0] // BASE_ROWS
+    for copy in copies:
+        copy.wait()
     for q in range(CUTS):
-        picked = plain_dot(piece_places(experts, q), extra)
-        rows_ref[first:, q * piece : (q + 1) * piece] = picked.astype(jnp.bfloat16)
-
-
-def collect(rows_ref, message_refs):
+        picked = plain_dot(piece_places(experts, q), extra_ref[...])
+        columns = slice(q * piece, (q + 1) * piece)
+        rows_ref[experts * BASE_ROWS :, columns] = picked.astype(jnp.bfloat16)
+
+
+def collect(rows_ref, extra_ref, message_refs, sems):
     experts = len(message_refs)
     width = rows_ref.shape[1]
     piece = width // CUTS
@@ -301,10 +335,17 @@
             from_rows,
             preferred_element_type=jnp.float32,
         )
-    extra = extra.astype(jnp.bfloat16)
+    extra_ref[...] = extra.astype(jnp.bfloat16)
+    copies = []
     for k, ref in enumerate(message_refs):
-        ref[:, :width] = rows_ref[k * BASE_ROWS : (k + 1) * BASE_ROWS, :]
-        ref[:, width:] = extra[k * BASE_ROWS : (k + 1) * BASE_ROWS]
+        rows = slice(k * BASE_ROWS, (k + 1) * BASE_ROWS)
+        parts = ((rows_ref, ref.at[:, :width]), (extra_ref, ref.at[:, width:]))
+        for n, (source, target) in enumerate(parts):
+            copies.append(pltpu.make_async_copy(source.at[rows, :], target, sems.at[n, k]))
+    for copy in copies:
+        copy.start()
+    for copy in copies:
+        copy.wait()
 
 
 def row_weight(rows_ref, router_ref):
@@ -314,85 +355,112 @@
     return route_scale * jax.nn.sigmoid(logits)
 
 
-def forward_kernel(experts, router_ref, gate_ref, up_ref, down_ref, *refs):
-    message_refs, out_refs = refs[:experts], refs[experts : 2 * experts]
-    rows_ref, total_ref = refs[2 * experts :]
-    step = pl.program_id(0)
-
-    @pl.when(step == 0)
-    def _():
-        spread(message_refs, rows_ref)
-
-    rows = rows_ref[...]
-    gate_proj = plain_dot(rows, gate_ref[...])
-    up_proj = plain_dot(rows, up_ref[...])
-    hidden = (gate_proj * jax.nn.sigmoid(gate_proj) * up_proj).astype(jnp.bfloat16)
-    part = plain_dot(hidden, down_ref[...])
-
-    @pl.when(step == 0)
-    def _():
-        total_ref[...] = part
-
-    @pl.when(step > 0)
-    def _():
-        total_ref[...] += part
-
-    @pl.when(step == pl.num_programs(0) - 1)
-    def _():
-        weight = row_weight(rows_ref, router_ref)
-        expert = total_ref[...].astype(jnp.bfloat16).astype(jnp.float32)
-        section = rows_ref[...].astype(jnp.float32) + weight * expert
-        rows_ref[...] = section.astype(jnp.bfloat16)
-        collect(rows_ref, out_refs)
-
-
-def backward_kernel(experts, router_ref, gate_ref, up_ref, down_ref, *refs):
-    saved_refs, grad_refs = refs[:experts], refs[experts : 2 * experts]
-    out_refs = refs[2 * experts : 3 * experts]
-    rows_ref, grads_ref, weighted_ref, total_ref = refs[3 * experts :]
-    step = pl.program_id(0)
-
-    @pl.when(step == 0)
-    def _():
-        spread(saved_refs, rows_ref)
-        spread(grad_refs, grads_ref)
-        weight = row_weight(rows_ref, router_ref)
-        weighted = weight * grads_ref[...].astype(jnp.float32)
-        weighted_ref[...] = weighted.astype(jnp.bfloat16)
-
-    rows = rows_ref[...]
-    gate_proj = plain_dot(rows, gate_ref[...])
-    up_proj = plain_dot(rows, up_ref[...])
-    d_hidden = transposed_dot(weighted_ref[...], down_ref[...])
-    sigmoid_gate = jax.nn.sigmoid(gate_proj)
-    d_gate = d_hidden * up_proj * sigmoid_gate * (1.0 + gate_proj * (1.0 - sigmoid_gate))
-    d_up = d_hidden * gate_proj * sigmoid_gate
-    part = transposed_dot(d_gate.astype(jnp.bfloat16), gate_ref[...])
-    part = part + transposed_dot(d_up.astype(jnp.bfloat16), up_ref[...])
-
-    @pl.when(step == 0)
-    def _():
-        total_ref[...] = part
-
-    @pl.when(step > 0)
-    def _():
-        total_ref[...] += part
-
-    @pl.when(step == pl.num_programs(0) - 1)
-    def _():
-        expert = total_ref[...].astype(jnp.bfloat16).astype(jnp.float32)
-        section = grads_ref[...].astype(jnp.float32) + expert
-        rows_ref[...] = section.astype(jnp.bfloat16)
-        collect(rows_ref, out_refs)
-
-
-def pack(ids_row, rows, experts):
-    tokens, width = rows.shape
-    shape = jax.ShapeDtypeStruct((BASE_ROWS, width + width // CUTS), rows.dtype)
-    slots = experts * BASE_ROWS
+def weight_copies(weight_refs, chunk_refs, sems):
+    gate_ref, up_ref, down_ref = weight_refs
+    steps, width, part = chunk_refs[0].shape
+    copies = []
+    for j in range(steps):
+        units = slice(j * part, (j + 1) * part)
+        sources = (gate_ref.at[:, units], up_ref.at[:, units], down_ref.at[units, :])
+        copies.append(
+            [
+                pltpu.make_async_copy(source, chunk.at[j], sems.at[n, j])
+                for n, (source, chunk) in enumerate(zip(sources, chunk_refs))
+            ]
+        )
+    for step in copies:
+        for copy in step:
+            copy.start()
+    return copies
+
+
+def forward_kernel(experts, waited, router_ref, *refs):
+    me = lax.axis_index("ep")
+    weight_refs, message_refs = refs[:3], [refs[3].at[me ^ k] for k in range(experts)]
+    refs = refs[4 + waited :]
+    out_refs = refs[:experts]
+    rows_ref, total_ref, gate_ref, up_ref, down_ref, sems, extra_ref, message_sems = refs[experts:]
+    arriving = message_copies(message_refs, 0, rows_ref, extra_ref, message_sems)
+    copies = weight_copies(weight_refs, (gate_ref, up_ref, down_ref), sems)
+    spread(arriving, rows_ref, extra_ref)
+    weight = row_weight(rows_ref, router_ref)
+    for j, step in enumerate(copies):
+        for copy in step:
+            copy.wait()
+        gate_proj = plain_dot(rows_ref[...], gate_ref[j])
+        up_proj = plain_dot(rows_ref[...], up_ref[j])
+        hidden = (gate_proj * jax.nn.sigmoid(gate_proj) * up_proj).astype(jnp.bfloat16)
+        part = plain_dot(hidden, down_ref[j])
+        total_ref[...] = part if j == 0 else total_ref[...] + part
+    expert = total_ref[...].astype(jnp.bfloat16).astype(jnp.float32)
+    section = rows_ref[...].astype(jnp.float32) + weight * expert
+    rows_ref[...] = section.astype(jnp.bfloat16)
+    collect(rows_ref, extra_ref, out_refs, message_sems)
+
+
+def backward_kernel(experts, waited, router_ref, *refs):
+    weight_refs = refs[:3]
+    message_refs = refs[3 : 3 + experts]
+    refs = refs[3 + experts + waited :]
+    out_refs = refs[:experts]
+    (
+        rows_ref,
+        total_ref,
+        gate_ref,
+        up_ref,
+        down_ref,
+        sems,
+        extra_ref,
+        message_sems,
+        grads_ref,
+        weighted_ref,
+        grads_extra_ref,
+        grad_sems,
+    ) = refs[experts:]
+    arriving = message_copies(message_refs, 0, rows_ref, extra_ref, message_sems)
+    arriving_grads = message_copies(message_refs, 1, grads_ref, grads_extra_ref, grad_sems)
+    copies = weight_copies(weight_refs, (gate_ref, up_ref, down_ref), sems)
+    spread(arriving, rows_ref, extra_ref)
+    spread(arriving_grads, grads_ref, grads_extra_ref)
+    weighted = row_weight(rows_ref, router_ref) * grads_ref[...].astype(jnp.float32)
+    weighted_ref[...] = weighted.astype(jnp.bfloat16)
+    for j, step in enumerate(copies):
+        for copy in step:
+            copy.wait()
+        gate_proj = plain_dot(rows_ref[...], gate_ref[j])
+        up_proj = plain_dot(rows_ref[...], up_ref[j])
+        d_hidden = transposed_dot(weighted_ref[...], down_ref[j])
+        sigmoid_gate = jax.nn.sigmoid(gate_proj)
+        d_gate = d_hidden * up_proj * sigmoid_gate * (1.0 + gate_proj * (1.0 - sigmoid_gate))
+        d_up = d_hidden * gate_proj * sigmoid_gate
+        part = transposed_dot(d_gate.astype(jnp.bfloat16), gate_ref[j])
+        part = part + transposed_dot(d_up.astype(jnp.bfloat16), up_ref[j])
+        total_ref[...] = part if j == 0 else total_ref[...] + part
+    expert = total_ref[...].astype(jnp.bfloat16).astype(jnp.float32)
+    section = grads_ref[...].astype(jnp.float32) + expert
+    rows_ref[...] = section.astype(jnp.bfloat16)
+    collect(rows_ref, extra_ref, out_refs, message_sems)
+
+
+def pack(ids_rows, sources, kind, experts, joined, after=()):
+    tokens, width = sources[0].shape
+    dtype = sources[0].dtype
+    count = len(sources)
+    message = (count * BASE_ROWS, width + width // CUTS)
+    slots = count * experts * BASE_ROWS
+    anywhere = pl.BlockSpec(memory_space=pl.ANY)
+    shapes = [(experts, *message)] if joined else [message] * experts
     return pl.pallas_call(
-        functools.partial(pack_kernel, experts),
-        out_shape=[shape] * experts,
+        functools.partial(pack_kernel, kind, joined, count, experts),
+        in_specs=[pl.BlockSpec(memory_space=pltpu.VMEM)] + [anywhere] * (count + len(after)),
+        out_specs=[anywhere] * len(shapes),
+        out_shape=[jax.ShapeDtypeStruct(shape, dtype) for shape in shapes],
+        scratch_shapes=[
+            pltpu.VMEM((count, tokens, width), dtype),
+            pltpu.VMEM((experts, *message), dtype),
+            pltpu.SemaphoreType.DMA((count,)),
+            pltpu.SemaphoreType.DMA((experts,)),
+        ],
         compiler_params=pltpu.CompilerParams(vmem_limit_bytes=16 << 20),
         cost_estimate=pl.CostEstimate(
             flops=4 * slots * tokens * width,
@@ -400,15 +468,16 @@
             transcendentals=0,
         ),
         name="pack",
-    )(ids_row, rows)
-
-
-def unpack(ids_row, messages, experts):
+    )(ids_rows, *sources, *after)
+
+
+def unpack(ids_row, messages, order):
+    experts = len(order)
     tokens = ids_row.shape[1]
     width = messages[0].shape[1] * CUTS // (CUTS + 1)
     slots = experts * BASE_ROWS
     return pl.pallas_call(
-        functools.partial(unpack_kernel, experts),
+        functools.partial(unpack_kernel, order),
         out_shape=jax.ShapeDtypeStruct((tokens, width), messages[0].dtype),
         compiler_params=pltpu.CompilerParams(vmem_limit_bytes=16 << 20),
         cost_estimate=pl.CostEstimate(
@@ -417,58 +486,67 @@
             transcendentals=0,
         ),
         name="unpack",
-    )(ids_row, *messages)
-
-
-def expert_call(kernel, name, router_rows, gate_cols, up_cols, down_rows, messages, experts, products):
+    )(ids_row, *[messages[k] for k in order])
+
+
+def expert_call(
+    kernel, name, router_rows, gate_cols, up_cols, down_rows, messages, experts, products, after
+):
     width, units = gate_cols.shape
     row_count = experts * (BASE_ROWS + CUTS)
     steps = 4 if units % 512 == 0 else 1
     part = units // steps
-    message_shape = messages[0].shape
-    whole = pl.BlockSpec(message_shape, lambda j: (0, 0))
-    extra_scratch = 2 if len(messages) > experts else 0
+    result_shape = (BASE_ROWS, messages[0].shape[-1])
+    in_vmem = pl.BlockSpec(memory_space=pltpu.VMEM)
+    anywhere = pl.BlockSpec(memory_space=pl.ANY)
+    rows_scratch = pltpu.VMEM((row_count, width), jnp.bfloat16)
+    message_scratch = [
+        pltpu.VMEM((experts * BASE_ROWS, width // CUTS), jnp.bfloat16),
+        pltpu.SemaphoreType.DMA((2, experts)),
+    ]
     return pl.pallas_call(
-        functools.partial(kernel, experts),
-        grid=(steps,),
-        in_specs=[
-            pl.BlockSpec(router_rows.shape, lambda j: (0, 0)),
-            pl.BlockSpec((width, part), lambda j: (0, j)),
-            pl.BlockSpec((width, part), lambda j: (0, j)),
-            pl.BlockSpec((part, width), lambda j: (j, 0)),
+        functools.partial(kernel, experts, len(after)),
+        in_specs=[in_vmem] + [anywhere] * (3 + len(messages) + len(after)),
+        out_specs=[anywhere] * experts,
+        out_shape=[jax.ShapeDtypeStruct(result_shape, messages[0].dtype)] * experts,
+        scratch_shapes=[
+            rows_scratch,
+            pltpu.VMEM((row_count, width), jnp.float32),
+            pltpu.VMEM((steps, width, part), jnp.bfloat16),
+            pltpu.VMEM((steps, width, part), jnp.bfloat16),
+            pltpu.VMEM((steps, part, width), jnp.bfloat16),
+            pltpu.SemaphoreType.DMA((3, steps)),
+            *message_scratch,
         ]
-        + [whole] * len(messages),
-        out_specs=[whole] * experts,
-        out_shape=[jax.ShapeDtypeStruct(message_shape, messages[0].dtype)] * experts,
-        scratch_shapes=[pltpu.VMEM((row_count, width), jnp.bfloat16)] * (1 + extra_scratch)
-        + [pltpu.VMEM((row_count, width), jnp.float32)],
-        compiler_params=pltpu.CompilerParams(vmem_limit_bytes=40 << 20),
+        + ([rows_scratch] * 2 + message_scratch if products > 3 else []),
+        compiler_params=pltpu.CompilerParams(vmem_limit_bytes=VMEM_BYTES),
         cost_estimate=pl.CostEstimate(
             flops=2 * products * row_count * width * units,
             bytes_accessed=3 * ROWS_BYTES * width * units,
             transcendentals=row_count * units,
         ),
         name=name,
-    )(router_rows, gate_cols, up_cols, down_rows, *messages)
-
-
-def exchanged(messages, experts):
-    return [messages[0]] + [
-        lax.ppermute(messages[k], "ep", [(i, i ^ k) for i in range(experts)])
-        for k in range(1, experts)
-    ]
-
-
-def returned(messages, experts, steps):
-    sections = lax.axis_size("pp")
-    back = []
-    for k in range(experts):
+    )(router_rows, gate_cols, up_cols, down_rows, *messages, *after)
+
+
+def exchanged(messages, order):
+    experts = len(messages)
+    arrived = list(messages)
+    for k in order:
+        arrived[k] = lax.ppermute(messages[k], "ep", [(i, i ^ k) for i in range(experts)])
+    return arrived
+
+
+def returned(messages, order, steps):
+    sections, experts = lax.axis_size("pp"), len(messages)
+    back = list(messages)
+    for k in order:
         pairs = [
             (p * experts + e, (p + steps) % sections * experts + (e ^ k))
             for p in range(sections)
             for e in range(experts)
         ]
-        back.append(lax.ppermute(messages[k], ("pp", "ep"), pairs))
+        back[k] = lax.ppermute(messages[k], ("pp", "ep"), pairs)
     return back
 
 
@@ -477,21 +555,29 @@
     token_count = fwd_in.shape[1]
     router_rows = router[0].T
     weights = (w_gate[0], w_up[0], w_down[0])
-    fwd_row = fwd_ids.reshape(1, token_count)
-    bwd_row = bwd_ids.reshape(1, token_count)
-    fwd_rows = exchanged(pack(fwd_row, fwd_in[0], experts), experts)
-    saved_rows = exchanged(pack(bwd_row, saved_in[0], experts), experts)
-    grad_rows = exchanged(pack(bwd_row, grad_in[0], experts), experts)
-    fwd_row_next = from_behind(fwd_row, "pp", 1)
-    bwd_row_next = from_behind(bwd_row, "pp", -1)
-    fwd_out = expert_call(forward_kernel, "forward", router_rows, *weights, fwd_rows, experts, 3)
-    fwd_back = returned(fwd_out, experts, 1)
+    ids = jnp.concatenate([array.reshape(1, token_count) for array in (fwd_ids, bwd_ids)], axis=0)
+    near, far = list(range(1, experts // 2)), list(range(experts // 2, experts))
+    fwd_packed = pack(ids, [fwd_in[0]], 0, experts, True)
+    fwd_rows = lax.all_to_all(fwd_packed[0], "ep", split_axis=0, concat_axis=0, tiled=True)
+    all_ids = lax.all_gather(ids, "pp")
+    section, sections = lax.axis_index("pp"), lax.axis_size("pp")
+    fwd_row_next = lax.dynamic_index_in_dim(all_ids, (section + sections - 1) % sections, 0, False)[:1]
+    bwd_row_next = lax.dynamic_index_in_dim(all_ids, (section + 1) % sections, 0, False)[1:]
+    after = [fwd_packed[0], fwd_row_next, bwd_row_next]
+    bwd_packed = pack(ids, [saved_in[0], grad_in[0]], 1, experts, False, after)
+    bwd_rows = exchanged(bwd_packed, range(1, experts))
+    after = [bwd_rows[k] for k in near]
+    fwd_out = expert_call(
+        forward_kernel, "forward", router_rows, *weights, [fwd_rows], experts, 3, after
+    )
+    fwd_back = returned(fwd_out, range(experts), 1)
+    after = [fwd_back[k] for k in near + [0]]
     bwd_out = expert_call(
-        backward_kernel, "backward", router_rows, *weights, saved_rows + grad_rows, experts, 5
-    )
-    bwd_back = returned(bwd_out, experts, -1)
-    fwd_next = unpack(fwd_row_next, fwd_back, experts)
-    grad_next = unpack(bwd_row_next, bwd_back, experts)
+        backward_kernel, "backward", router_rows, *weights, bwd_rows, experts, 5, after
+    )
+    bwd_back = returned(bwd_out, range(experts), -1)
+    fwd_next = unpack(fwd_row_next, fwd_back, near + [0] + far)
+    grad_next = unpack(bwd_row_next, bwd_back, near[:1] + far + near[1:] + [0])
     return (fwd_next[None], grad_next[None])
 
 

time: 168 us -> 148 us (0.88)
  starting transfers between devices: 75.4 us -> 58.5 us
  waiting for transfers between devices: 46.2 us -> 36.7 us
  blocking collectives: 0 us -> 6.11 us
  local copies, waits for them, and re-layouts: 7.52 us -> 3.56 us
  Pallas kernels: 37.1 us -> 39.9 us
    ppermute x21 -> x7, starting transfers between devices: 24.1 us -> 7.49 us  [exchanged(): lax.ppermute(messages[k], 'ep', [(i, i ^ k) for i in range(experts)])]
    ppermute x21 -> x7, waiting for transfers between devices: 29.2 us -> 23 us  [exchanged(): lax.ppermute(messages[k], 'ep', [(i, i ^ k) for i in range(experts)])]
    all_gather x0 -> x1, blocking collectives: none -> 6.11 us  [per_device_whole(): all_ids = lax.all_gather(ids, 'pp')]
    ppermute x18 -> x16, starting transfers between devices: 51.2 us -> 45.3 us  [returned(): back[k] = lax.ppermute(messages[k], ('pp', 'ep'), pairs)]
    all_to_all x0 -> x1, starting transfers between devices: none -> 5.7 us  [per_device_whole(): lax.all_to_all(fwd_packed[0], 'ep', split_axis=0, concat_axis=0, tiled=True)]
    unnamed x14 -> x16, local copies, waits for them, and re-layouts: 7.52 us -> 3.55 us
    ppermute x18 -> x16, waiting for transfers between devices: 16.9 us -> 13.7 us  [returned(): back[k] = lax.ppermute(messages[k], ('pp', 'ep'), pairs)]
    pallas_call x7 -> x6, Pallas kernels: 37.1 us -> 39.9 us  [the longest x2 31 us: expert_call(): pl.pallas_call(functools.partial(kernel, experts, len(after)), in_specs=[...]
  transfers between devices with their start and end apart: 39 -> 24, of which waited for: 13 -> 9; matrix products, arithmetic and copies ran while one was open for 0% -> 0% of each run, Pallas kernels for 20% -> 25%
where the time goes in v2:
time: 148 us; the launch traced here: 146 us
  starting transfers between devices  58.5 us (40%)
  Pallas kernels  39.9 us (27%)
  waiting for transfers between devices  36.7 us (25%)
  blocking collectives  6.11 us (4%)
  local copies, waits for them, and re-layouts  3.56 us (2%)
    ppermute x16, starting transfers between devices, returned(): back[k] = lax.ppermute(messages[k], ('pp', 'ep'), pairs)  45.3 us
    pallas_call x2, Pallas kernels, expert_call(): pl.pallas_call(functools.partial(kernel, experts, len(after)), in_specs=[...  31 us
    ppermute x7, waiting for transfers between devices, exchanged(): lax.ppermute(messages[k], 'ep', [(i, i ^ k) for i in range(experts)])  23 us
    ppermute x16, waiting for transfers between devices, returned(): back[k] = lax.ppermute(messages[k], ('pp', 'ep'), pairs)  13.7 us
    ppermute x7, starting transfers between devices, exchanged(): lax.ppermute(messages[k], 'ep', [(i, i ^ k) for i in range(experts)])  7.49 us
    all_gather x1, blocking collectives, per_device_whole(): all_ids = lax.all_gather(ids, 'pp')  6.11 us
    all_to_all x1, starting transfers between devices, per_device_whole(): lax.all_to_all(fwd_packed[0], 'ep', split_axis=0, concat_axis=0, tiled=True)  5.7 us
    pallas_call x2, Pallas kernels, pack(): pl.pallas_call(functools.partial(pack_kernel, kind, joined, count, expert...  5.35 us
  transfers between devices with their start and end apart: 24, of which 9 were waited for; matrix products, arithmetic and copies ran while one was open for 0% of the time, Pallas kernels for 25%

profile of v2, /device:TPU:9, one launch (start us, length us, event | category | flops | bytes accessed | tf_op | source)
XLA Modules:
  0.0 146.1 jit_solution(12788535991678471417)
XLA Ops:
  2.5 2.1 %pack.2.refs_2_ = bf16[8,16,4480]{2,1,0:T(8,128)(2,1)} custom-call(s32[2,128]{1,0:T(2,128)S(1)} %get-tuple-element.52.ids_ref, bf16[128,3584]{1,0:T(8,128)(2,1)S(1)} %bitcast.19), custom_call_target="tpu_custom_call" | custom-call | flops 234881024 | bytes 1835008 | tf_op jit(solution)/shard_map/pack/pallas_call | solution.py:453
  4.6 5.7 %all-to-all-start = ((bf16[8,16,4480]{2,1,0:T(8,128)(2,1)}), bf16[8,16,4480]{2,1,0:T(8,128)(2,1)S(1)}, u32[]{:S(2)}, u32[]{:S(2)}) async-start(bf16[8,16,4480]{2,1,0:T(8,128)(2,1)} %pack.2.refs_2_), calls=%async_computation | async-start | bytes 2293760 | tf_op jit(solution)/shard_map/all_to_all | solution.py:561
  10.3 6.1 %all-gather.1 = s32[4,2,128]{2,1,0:T(2,128)S(1)} all-gather(s32[1,2,128]{2,1,0:T(2,128)S(1)} %get-tuple-element.53), channel_id=2, replica_groups=mesh['pp'=4,'ep'=8] {'pp'}, dimensions={0}, use_global_device_ids=true | all-gather | bytes 5120 | tf_op jit(solution)/shard_map/all_gather | solution.py:562
  18.8 3.2 %pack.3 = (bf16[32,4480]{1,0:T(8,128)(2,1)S(1)}, bf16[32,4480]{1,0:T(8,128)(2,1)S(1)}, bf16[32,4480]{1,0:T(8,128)(2,1)S(1)}, bf16[32,4480]{1,0:T(8,128)(2,1)S(1)...) custom-call(s32[2,128]{1,0:T(2,128)S(1)} %get-tuple-element.52.ids_r, ...), custom_call_target="tpu_custom_call" | custom-call | flops 469762048 | bytes 3670016 | tf_op jit(solution)/shard_map/pack/pallas_call | solution.py:453
  24.8 2.1 %collective-permute-start.11 = (bf16[32,4480]{1,0:T(8,128)(2,1)}, bf16[32,4480]{1,0:T(8,128)(2,1)S(1)}, u32[]{:S(2)}, u32[]{:S(2)}) collective-permute-start(bf16[32,4480]{1,0:T(8,128)(2,1)} %get-tuple-element.38), channel_id=1, source_target_pairs={{0,4},{1,5},{2,6},{3,7},{4,0},{5,1},{6,2},{7,3},{8,12},{9,13},{10,... | collective-permute-start | bytes 860168 | tf_op jit(solution)/shard_map/ppermute | solution.py:536
  28.0 8.7 %collective-permute-done.refs_4_ = bf16[32,4480]{1,0:T(8,128)(2,1)S(1)} collective-permute-done((bf16[32,4480]{1,0:T(8,128)(2,1)S(1)}, bf16[32,4480]{1,0:T(8,128)(2,1)S(1)}, u32[]{:S(2)}, u32[]{:S(2)}) %collective-permute-start) | collective-permute-done | bytes 286752 | tf_op jit(solution)/shard_map/ppermute | solution.py:536
  38.2 11.0 %collective-permute-done.2.refs_6_ = bf16[32,4480]{1,0:T(8,128)(2,1)S(1)} collective-permute-done((bf16[32,4480]{1,0:T(8,128)(2,1)S(1)}, bf16[32,4480]{1,0:T(8,128)(2,1)S(1)}, u32[]{:S(2)}, u32[]{:S(2)}) %collective-permute-start.2) | collective-permute-done | bytes 286752 | tf_op jit(solution)/shard_map/ppermute | solution.py:536
  49.3 10.6 %forward.1 = (bf16[16,4480]{1,0:T(8,128)(2,1)S(1)}, bf16[16,4480]{1,0:T(8,128)(2,1)S(1)}, bf16[16,4480]{1,0:T(8,128)(2,1)S(1)}, bf16[16,4480]{1,0:T(8,128)(2,1)S...) custom-call(f32[8,3584]{1,0:T(8,128)S(1)} %bitcast.22, ...), custom_call_target="tpu_custom_call" | custom-call | flops 3523215360 | bytes 22020096 | tf_op jit(solution)/shard_map/forward/pallas_call | solution.py:507
  59.9 2.1 %collective-permute-start.3 = (bf16[16,4480]{1,0:T(8,128)(2,1)S(1)}, bf16[16,4480]{1,0:T(8,128)(2,1)S(1)}, u32[]{:S(2)}, u32[]{:S(2)}) collective-permute-start(bf16[16,4480]{1,0:T(8,128)(2,1)S(1)} %get-tuple-element.29), channel_id=1, source_target_pairs={{0,9},{1,8},{2,11},{3,10},{4,13},{5,12},{6,15},{7,14},{8,17},{9,16... | collective-permute-start | bytes 430088 | tf_op jit(solution)/shard_map/ppermute | solution.py:549
  62.0 10.3 %collective-permute-start.4 = (bf16[16,4480]{1,0:T(8,128)(2,1)S(1)}, bf16[16,4480]{1,0:T(8,128)(2,1)S(1)}, u32[]{:S(2)}, u32[]{:S(2)}) collective-permute-start(bf16[16,4480]{1,0:T(8,128)(2,1)S(1)} %get-tuple-element.30), channel_id=1, source_target_pairs={{0,10},{1,11},{2,8},{3,9},{4,14},{5,15},{6,12},{7,13},{8,18},{9,19... | collective-permute-start | bytes 430088 | tf_op jit(solution)/shard_map/ppermute | solution.py:549
  72.6 6.7 %collective-permute-start.5 = (bf16[16,4480]{1,0:T(8,128)(2,1)S(1)}, bf16[16,4480]{1,0:T(8,128)(2,1)S(1)}, u32[]{:S(2)}, u32[]{:S(2)}) collective-permute-start(bf16[16,4480]{1,0:T(8,128)(2,1)S(1)} %get-tuple-element.31), channel_id=1, source_target_pairs={{0,11},{1,10},{2,9},{3,8},{4,15},{5,14},{6,13},{7,12},{8,19},{9,18... | collective-permute-start | bytes 430088 | tf_op jit(solution)/shard_map/ppermute | solution.py:549
  79.3 4.3 %collective-permute-start.6 = (bf16[16,4480]{1,0:T(8,128)(2,1)S(1)}, bf16[16,4480]{1,0:T(8,128)(2,1)S(1)}, u32[]{:S(2)}, u32[]{:S(2)}) collective-permute-start(bf16[16,4480]{1,0:T(8,128)(2,1)S(1)} %get-tuple-element.32), channel_id=1, source_target_pairs={{0,8},{1,9},{2,10},{3,11},{4,12},{5,13},{6,14},{7,15},{8,16},{9,17... | collective-permute-start | bytes 430088 | tf_op jit(solution)/shard_map/ppermute | solution.py:549
  83.7 3.0 %collective-permute-done.14.refs_10_ = bf16[32,4480]{1,0:T(8,128)(2,1)S(1)} collective-permute-done((bf16[32,4480]{1,0:T(8,128)(2,1)}, bf16[32,4480]{1,0:T(8,128)(2,1)S(1)}, u32[]{:S(2)}, u32[]{:S(2)}) %collective-permute-start.14) | collective-permute-done | bytes 286752 | tf_op jit(solution)/shard_map/ppermute | solution.py:536
  86.7 3.4 %collective-permute-start.8 = (bf16[16,4480]{1,0:T(8,128)(2,1)S(1)}, bf16[16,4480]{1,0:T(8,128)(2,1)S(1)}, u32[]{:S(2)}, u32[]{:S(2)}) collective-permute-start(bf16[16,4480]{1,0:T(8,128)(2,1)S(1)} %get-tuple-element.34), channel_id=1, source_target_pairs={{0,13},{1,12},{2,15},{3,14},{4,9},{5,8},{6,11},{7,10},{8,21},{9,20... | collective-permute-start | bytes 430088 | tf_op jit(solution)/shard_map/ppermute | solution.py:549
  90.1 2.8 %collective-permute-start.9 = (bf16[16,4480]{1,0:T(8,128)(2,1)S(1)}, bf16[16,4480]{1,0:T(8,128)(2,1)S(1)}, u32[]{:S(2)}, u32[]{:S(2)}) collective-permute-start(bf16[16,4480]{1,0:T(8,128)(2,1)S(1)} %get-tuple-element.35), channel_id=1, source_target_pairs={{0,14},{1,15},{2,12},{3,13},{4,10},{5,11},{6,8},{7,9},{8,22},{9,23... | collective-permute-start | bytes 430088 | tf_op jit(solution)/shard_map/ppermute | solution.py:549
  93.1 20.4 %backward.1 = (bf16[16,4480]{1,0:T(8,128)(2,1)S(1)}, bf16[16,4480]{1,0:T(8,128)(2,1)S(1)}, bf16[16,4480]{1,0:T(8,128)(2,1)S(1)}, bf16[16,4480]{1,0:T(8,128)(2,1)...) custom-call(f32[8,3584]{1,0:T(8,128)S(1)} %bitcast.23, ...), custom_call_target="tpu_custom_call" | custom-call | flops 5872025600 | bytes 22020096 | tf_op jit(solution)/shard_map/backward/pallas_call | solution.py:507
  115.2 2.8 %collective-permute-start.16 = (bf16[16,4480]{1,0:T(8,128)(2,1)S(1)}, bf16[16,4480]{1,0:T(8,128)(2,1)S(1)}, u32[]{:S(2)}, u32[]{:S(2)}) collective-permute-start(bf16[16,4480]{1,0:T(8,128)(2,1)S(1)} %get-tuple-element.43), channel_id=1, source_target_pairs={{0,28},{1,29},{2,30},{3,31},{4,24},{5,25},{6,26},{7,27},{8,4},{9,5... | collective-permute-start | bytes 430088 | tf_op jit(solution)/shard_map/ppermute | solution.py:549
  121.4 4.3 %collective-permute-start.20 = (bf16[16,4480]{1,0:T(8,128)(2,1)S(1)}, bf16[16,4480]{1,0:T(8,128)(2,1)S(1)}, u32[]{:S(2)}, u32[]{:S(2)}) collective-permute-start(bf16[16,4480]{1,0:T(8,128)(2,1)S(1)} %get-tuple-element.47), channel_id=1, source_target_pairs={{0,26},{1,27},{2,24},{3,25},{4,30},{5,31},{6,28},{7,29},{8,2},{9,3... | collective-permute-start | bytes 430088 | tf_op jit(solution)/shard_map/ppermute | solution.py:549
  125.7 8.1 %collective-permute-done.16.refs_1_ = bf16[16,4480]{1,0:T(8,128)(2,1)S(1)} collective-permute-done((bf16[16,4480]{1,0:T(8,128)(2,1)S(1)}, bf16[16,4480]{1,0:T(8,128)(2,1)S(1)}, u32[]{:S(2)}, u32[]{:S(2)}) %collective-permute-start.16) | collective-permute-done | bytes 143392 | tf_op jit(solution)/shard_map/ppermute | solution.py:549
  133.9 2.6 %collective-permute-start.21 = (bf16[16,4480]{1,0:T(8,128)(2,1)S(1)}, bf16[16,4480]{1,0:T(8,128)(2,1)S(1)}, u32[]{:S(2)}, u32[]{:S(2)}) collective-permute-start(bf16[16,4480]{1,0:T(8,128)(2,1)S(1)} %get-tuple-element.48), channel_id=1, source_target_pairs={{0,27},{1,26},{2,25},{3,24},{4,31},{5,30},{6,29},{7,28},{8,3},{9,2... | collective-permute-start | bytes 430088 | tf_op jit(solution)/shard_map/ppermute | solution.py:549
  137.5 1.7 %unpack.2 = bf16[128,3584]{1,0:T(8,128)(2,1)} custom-call(s32[1,128]{1,0:T(1,128)S(1)} %copy-done.7, bf16[16,4480]{1,0:T(8,128)(2,1)S(1)} %collective-permute-done.3.refs_0_.refs_11_, bf16[16,4480]{1,0:T(8,128)(2,1)S(1)} %collective-permute-done.4.refs_1_.refs_12_, bf16[16,4480]{1,0:T(8,128)(2,1)S(1)} %collective-permute-done.5.refs_2_.refs_13_, ...), custom_call_target="tpu_custom_call" | custom-call | flops 234881024 | bytes 1835008 | tf_op jit(solution)/shard_map/unpack/pallas_call | solution.py:479
  139.2 1.9 %collective-permute-done.18.refs_3_ = bf16[16,4480]{1,0:T(8,128)(2,1)S(1)} collective-permute-done((bf16[16,4480]{1,0:T(8,128)(2,1)S(1)}, bf16[16,4480]{1,0:T(8,128)(2,1)S(1)}, u32[]{:S(2)}, u32[]{:S(2)}) %collective-permute-start.18) | collective-permute-done | bytes 143392 | tf_op jit(solution)/shard_map/ppermute | solution.py:549
  141.1 3.1 %collective-permute-done.19.refs_4_ = bf16[16,4480]{1,0:T(8,128)(2,1)S(1)} collective-permute-done((bf16[16,4480]{1,0:T(8,128)(2,1)S(1)}, bf16[16,4480]{1,0:T(8,128)(2,1)S(1)}, u32[]{:S(2)}, u32[]{:S(2)}) %collective-permute-start.19) | collective-permute-done | bytes 143392 | tf_op jit(solution)/shard_map/ppermute | solution.py:549
  144.3 1.7 %unpack.3 = bf16[128,3584]{1,0:T(8,128)(2,1)} custom-call(s32[1,128]{1,0:T(1,128)S(1)} %copy-done.5, bf16[16,4480]{1,0:T(8,128)(2,1)S(1)} %collective-permute-done.15.refs_0_, bf16[16,4480]{1,0:T(8,128)(2,1)S(1)} %collective-permute-done.16.refs_1_, bf16[16,4480]{1,0:T(8,128)(2,1)S(1)} %collective-permute-done.17.refs_2_, ...), custom_call_target="tpu_custom_call" | custom-call | flops 234881024 | bytes 1835008 | tf_op jit(solution)/shard_map/unpack/pallas_call | solution.py:479
  (50 shorter events, 16.4 us)
Async XLA Ops:
  4.6 44.6 %all-to-all-start = ((bf16[8,16,4480]{2,1,0:T(8,128)(2,1)}), bf16[8,16,4480]{2,1,0:T(8,128)(2,1)S(1)}, u32[]{:S(2)}, u32[]{:S(2)}) async-start(bf16[8,16,4480]{2,1,0:T(8,128)(2,1)} %pack.2.refs_2_), calls=%async_computation | async-start | bytes 2293760 | tf_op jit(solution)/shard_map/all_to_all | solution.py:561
  22.0 14.7 %collective-permute-start = (bf16[32,4480]{1,0:T(8,128)(2,1)S(1)}, bf16[32,4480]{1,0:T(8,128)(2,1)S(1)}, u32[]{:S(2)}, u32[]{:S(2)}) collective-permute-start(bf16[32,4480]{1,0:T(8,128)(2,1)S(1)} %get-tuple-element.26), channel_id=1, source_target_pairs={{0,1},{1,0},{2,3},{3,2},{4,5},{5,4},{6,7},{7,6},{8,9},{9,8},{10,11... | collective-permute-start | bytes 860168 | tf_op jit(solution)/shard_map/ppermute | solution.py:536
  23.3 13.4 %collective-permute-start.1 = (bf16[32,4480]{1,0:T(8,128)(2,1)S(1)}, bf16[32,4480]{1,0:T(8,128)(2,1)S(1)}, u32[]{:S(2)}, u32[]{:S(2)}) collective-permute-start(bf16[32,4480]{1,0:T(8,128)(2,1)S(1)} %get-tuple-element.27), channel_id=1, source_target_pairs={{0,2},{1,3},{2,0},{3,1},{4,6},{5,7},{6,4},{7,5},{8,10},{9,11},{10,... | collective-permute-start | bytes 860168 | tf_op jit(solution)/shard_map/ppermute | solution.py:536
  23.6 25.7 %collective-permute-start.2 = (bf16[32,4480]{1,0:T(8,128)(2,1)S(1)}, bf16[32,4480]{1,0:T(8,128)(2,1)S(1)}, u32[]{:S(2)}, u32[]{:S(2)}) collective-permute-start(bf16[32,4480]{1,0:T(8,128)(2,1)S(1)} %get-tuple-element.28), channel_id=1, source_target_pairs={{0,3},{1,2},{2,1},{3,0},{4,7},{5,6},{6,5},{7,4},{8,11},{9,10},{10,... | collective-permute-start | bytes 860168 | tf_op jit(solution)/shard_map/ppermute | solution.py:536
  24.8 37.3 %collective-permute-start.11 = (bf16[32,4480]{1,0:T(8,128)(2,1)}, bf16[32,4480]{1,0:T(8,128)(2,1)S(1)}, u32[]{:S(2)}, u32[]{:S(2)}) collective-permute-start(bf16[32,4480]{1,0:T(8,128)(2,1)} %get-tuple-element.38), channel_id=1, source_target_pairs={{0,4},{1,5},{2,6},{3,7},{4,0},{5,1},{6,2},{7,3},{8,12},{9,13},{10,... | collective-permute-start | bytes 860168 | tf_op jit(solution)/shard_map/ppermute | solution.py:536
  26.8 45.7 %collective-permute-start.12 = (bf16[32,4480]{1,0:T(8,128)(2,1)}, bf16[32,4480]{1,0:T(8,128)(2,1)S(1)}, u32[]{:S(2)}, u32[]{:S(2)}) collective-permute-start(bf16[32,4480]{1,0:T(8,128)(2,1)} %get-tuple-element.39), channel_id=1, source_target_pairs={{0,5},{1,4},{2,7},{3,6},{4,1},{5,0},{6,3},{7,2},{8,13},{9,12},{10,... | collective-permute-start | bytes 860168 | tf_op jit(solution)/shard_map/ppermute | solution.py:536
  36.7 42.6 %collective-permute-start.13 = (bf16[32,4480]{1,0:T(8,128)(2,1)}, bf16[32,4480]{1,0:T(8,128)(2,1)S(1)}, u32[]{:S(2)}, u32[]{:S(2)}) collective-permute-start(bf16[32,4480]{1,0:T(8,128)(2,1)} %get-tuple-element.40), channel_id=1, source_target_pairs={{0,6},{1,7},{2,4},{3,5},{4,2},{5,3},{6,0},{7,1},{8,14},{9,15},{10,... | collective-permute-start | bytes 860168 | tf_op jit(solution)/shard_map/ppermute | solution.py:536
  36.7 49.9 %collective-permute-start.14 = (bf16[32,4480]{1,0:T(8,128)(2,1)}, bf16[32,4480]{1,0:T(8,128)(2,1)S(1)}, u32[]{:S(2)}, u32[]{:S(2)}) collective-permute-start(bf16[32,4480]{1,0:T(8,128)(2,1)} %get-tuple-element.41), channel_id=1, source_target_pairs={{0,7},{1,6},{2,5},{3,4},{4,3},{5,2},{6,1},{7,0},{8,15},{9,14},{10,... | collective-permute-start | bytes 860168 | tf_op jit(solution)/shard_map/ppermute | solution.py:536
  59.9 26.8 %collective-permute-start.3 = (bf16[16,4480]{1,0:T(8,128)(2,1)S(1)}, bf16[16,4480]{1,0:T(8,128)(2,1)S(1)}, u32[]{:S(2)}, u32[]{:S(2)}) collective-permute-start(bf16[16,4480]{1,0:T(8,128)(2,1)S(1)} %get-tuple-element.29), channel_id=1, source_target_pairs={{0,9},{1,8},{2,11},{3,10},{4,13},{5,12},{6,15},{7,14},{8,17},{9,16... | collective-permute-start | bytes 430088 | tf_op jit(solution)/shard_map/ppermute | solution.py:549
  62.0 28.1 %collective-permute-start.4 = (bf16[16,4480]{1,0:T(8,128)(2,1)S(1)}, bf16[16,4480]{1,0:T(8,128)(2,1)S(1)}, u32[]{:S(2)}, u32[]{:S(2)}) collective-permute-start(bf16[16,4480]{1,0:T(8,128)(2,1)S(1)} %get-tuple-element.30), channel_id=1, source_target_pairs={{0,10},{1,11},{2,8},{3,9},{4,14},{5,15},{6,12},{7,13},{8,18},{9,19... | collective-permute-start | bytes 430088 | tf_op jit(solution)/shard_map/ppermute | solution.py:549
  72.6 20.3 %collective-permute-start.5 = (bf16[16,4480]{1,0:T(8,128)(2,1)S(1)}, bf16[16,4480]{1,0:T(8,128)(2,1)S(1)}, u32[]{:S(2)}, u32[]{:S(2)}) collective-permute-start(bf16[16,4480]{1,0:T(8,128)(2,1)S(1)} %get-tuple-element.31), channel_id=1, source_target_pairs={{0,11},{1,10},{2,9},{3,8},{4,15},{5,14},{6,13},{7,12},{8,19},{9,18... | collective-permute-start | bytes 430088 | tf_op jit(solution)/shard_map/ppermute | solution.py:549
  79.3 13.8 %collective-permute-start.6 = (bf16[16,4480]{1,0:T(8,128)(2,1)S(1)}, bf16[16,4480]{1,0:T(8,128)(2,1)S(1)}, u32[]{:S(2)}, u32[]{:S(2)}) collective-permute-start(bf16[16,4480]{1,0:T(8,128)(2,1)S(1)} %get-tuple-element.32), channel_id=1, source_target_pairs={{0,8},{1,9},{2,10},{3,11},{4,12},{5,13},{6,14},{7,15},{8,16},{9,17... | collective-permute-start | bytes 430088 | tf_op jit(solution)/shard_map/ppermute | solution.py:549
  86.7 28.5 %collective-permute-start.7 = (bf16[16,4480]{1,0:T(8,128)(2,1)S(1)}, bf16[16,4480]{1,0:T(8,128)(2,1)S(1)}, u32[]{:S(2)}, u32[]{:S(2)}) collective-permute-start(bf16[16,4480]{1,0:T(8,128)(2,1)S(1)} %get-tuple-element.33), channel_id=1, source_target_pairs={{0,12},{1,13},{2,14},{3,15},{4,8},{5,9},{6,10},{7,11},{8,20},{9,21... | collective-permute-start | bytes 430088 | tf_op jit(solution)/shard_map/ppermute | solution.py:549
  86.7 31.3 %collective-permute-start.8 = (bf16[16,4480]{1,0:T(8,128)(2,1)S(1)}, bf16[16,4480]{1,0:T(8,128)(2,1)S(1)}, u32[]{:S(2)}, u32[]{:S(2)}) collective-permute-start(bf16[16,4480]{1,0:T(8,128)(2,1)S(1)} %get-tuple-element.34), channel_id=1, source_target_pairs={{0,13},{1,12},{2,15},{3,14},{4,9},{5,8},{6,11},{7,10},{8,21},{9,20... | collective-permute-start | bytes 430088 | tf_op jit(solution)/shard_map/ppermute | solution.py:549
  90.1 29.3 %collective-permute-start.9 = (bf16[16,4480]{1,0:T(8,128)(2,1)S(1)}, bf16[16,4480]{1,0:T(8,128)(2,1)S(1)}, u32[]{:S(2)}, u32[]{:S(2)}) collective-permute-start(bf16[16,4480]{1,0:T(8,128)(2,1)S(1)} %get-tuple-element.35), channel_id=1, source_target_pairs={{0,14},{1,15},{2,12},{3,13},{4,10},{5,11},{6,8},{7,9},{8,22},{9,23... | collective-permute-start | bytes 430088 | tf_op jit(solution)/shard_map/ppermute | solution.py:549
  92.9 26.8 %collective-permute-start.10 = (bf16[16,4480]{1,0:T(8,128)(2,1)S(1)}, bf16[16,4480]{1,0:T(8,128)(2,1)S(1)}, u32[]{:S(2)}, u32[]{:S(2)}) collective-permute-start(bf16[16,4480]{1,0:T(8,128)(2,1)S(1)} %get-tuple-element.36), channel_id=1, source_target_pairs={{0,15},{1,14},{2,13},{3,12},{4,11},{5,10},{6,9},{7,8},{8,23},{9,22... | collective-permute-start | bytes 430088 | tf_op jit(solution)/shard_map/ppermute | solution.py:549
  113.5 7.9 %collective-permute-start.15 = (bf16[16,4480]{1,0:T(8,128)(2,1)S(1)}, bf16[16,4480]{1,0:T(8,128)(2,1)S(1)}, u32[]{:S(2)}, u32[]{:S(2)}) collective-permute-start(bf16[16,4480]{1,0:T(8,128)(2,1)S(1)} %get-tuple-element.42), channel_id=1, source_target_pairs={{0,25},{1,24},{2,27},{3,26},{4,29},{5,28},{6,31},{7,30},{8,1},{9,0... | collective-permute-start | bytes 430088 | tf_op jit(solution)/shard_map/ppermute | solution.py:549
  115.2 18.6 %collective-permute-start.16 = (bf16[16,4480]{1,0:T(8,128)(2,1)S(1)}, bf16[16,4480]{1,0:T(8,128)(2,1)S(1)}, u32[]{:S(2)}, u32[]{:S(2)}) collective-permute-start(bf16[16,4480]{1,0:T(8,128)(2,1)S(1)} %get-tuple-element.43), channel_id=1, source_target_pairs={{0,28},{1,29},{2,30},{3,31},{4,24},{5,25},{6,26},{7,27},{8,4},{9,5... | collective-permute-start | bytes 430088 | tf_op jit(solution)/shard_map/ppermute | solution.py:549
  118.0 19.0 %collective-permute-start.17 = (bf16[16,4480]{1,0:T(8,128)(2,1)S(1)}, bf16[16,4480]{1,0:T(8,128)(2,1)S(1)}, u32[]{:S(2)}, u32[]{:S(2)}) collective-permute-start(bf16[16,4480]{1,0:T(8,128)(2,1)S(1)} %get-tuple-element.44), channel_id=1, source_target_pairs={{0,29},{1,28},{2,31},{3,30},{4,25},{5,24},{6,27},{7,26},{8,5},{9,4... | collective-permute-start | bytes 430088 | tf_op jit(solution)/shard_map/ppermute | solution.py:549
  119.4 21.6 %collective-permute-start.18 = (bf16[16,4480]{1,0:T(8,128)(2,1)S(1)}, bf16[16,4480]{1,0:T(8,128)(2,1)S(1)}, u32[]{:S(2)}, u32[]{:S(2)}) collective-permute-start(bf16[16,4480]{1,0:T(8,128)(2,1)S(1)} %get-tuple-element.45), channel_id=1, source_target_pairs={{0,30},{1,31},{2,28},{3,29},{4,26},{5,27},{6,24},{7,25},{8,6},{9,7... | collective-permute-start | bytes 430088 | tf_op jit(solution)/shard_map/ppermute | solution.py:549
  119.7 24.5 %collective-permute-start.19 = (bf16[16,4480]{1,0:T(8,128)(2,1)S(1)}, bf16[16,4480]{1,0:T(8,128)(2,1)S(1)}, u32[]{:S(2)}, u32[]{:S(2)}) collective-permute-start(bf16[16,4480]{1,0:T(8,128)(2,1)S(1)} %get-tuple-element.46), channel_id=1, source_target_pairs={{0,31},{1,30},{2,29},{3,28},{4,27},{5,26},{6,25},{7,24},{8,7},{9,6... | collective-permute-start | bytes 430088 | tf_op jit(solution)/shard_map/ppermute | solution.py:549
  121.4 22.7 %collective-permute-start.20 = (bf16[16,4480]{1,0:T(8,128)(2,1)S(1)}, bf16[16,4480]{1,0:T(8,128)(2,1)S(1)}, u32[]{:S(2)}, u32[]{:S(2)}) collective-permute-start(bf16[16,4480]{1,0:T(8,128)(2,1)S(1)} %get-tuple-element.47), channel_id=1, source_target_pairs={{0,26},{1,27},{2,24},{3,25},{4,30},{5,31},{6,28},{7,29},{8,2},{9,3... | collective-permute-start | bytes 430088 | tf_op jit(solution)/shard_map/ppermute | solution.py:549
  133.9 10.3 %collective-permute-start.21 = (bf16[16,4480]{1,0:T(8,128)(2,1)S(1)}, bf16[16,4480]{1,0:T(8,128)(2,1)S(1)}, u32[]{:S(2)}, u32[]{:S(2)}) collective-permute-start(bf16[16,4480]{1,0:T(8,128)(2,1)S(1)} %get-tuple-element.48), channel_id=1, source_target_pairs={{0,27},{1,26},{2,25},{3,24},{4,31},{5,30},{6,29},{7,28},{8,3},{9,2... | collective-permute-start | bytes 430088 | tf_op jit(solution)/shard_map/ppermute | solution.py:549
  136.9 7.4 %collective-permute-start.22 = (bf16[16,4480]{1,0:T(8,128)(2,1)S(1)}, bf16[16,4480]{1,0:T(8,128)(2,1)S(1)}, u32[]{:S(2)}, u32[]{:S(2)}) collective-permute-start(bf16[16,4480]{1,0:T(8,128)(2,1)S(1)} %get-tuple-element.49), channel_id=1, source_target_pairs={{0,24},{1,25},{2,26},{3,27},{4,28},{5,29},{6,30},{7,31},{8,0},{9,1... | collective-permute-start | bytes 430088 | tf_op jit(solution)/shard_map/ppermute | solution.py:549
  (8 other events, 189.5 us)

commit v3 on v2

--- a/solution.py
+++ b/solution.py
@@ -196,8 +196,10 @@
 
 BASE_ROWS = 16
 CUTS = 4
+COLUMNS = 512
 ROWS_BYTES = 2
 VMEM_BYTES = 44 << 20
+PACK_BYTES = 60 << 20
 
 
 def transposed_dot(left, right):
@@ -231,16 +233,20 @@
     return base, pieces
 
 
-def pack_kernel(kind, joined, count, experts, ids_ref, *refs):
+def pack_kernel(joined, count, experts, own_ids_ref, *refs):
     x_refs = refs[:count]
-    held_ref, made_ref, sems, out_sems = refs[-4:]
+    held_ref, made_ref, sems, out_sems, ids_ref, ids_sem = refs[-6:]
+    refs = refs[:-2]
+    ids_copy = pltpu.make_async_copy(own_ids_ref, ids_ref, ids_sem)
+    ids_copy.start()
     copies = [pltpu.make_async_copy(x_refs[n], held_ref.at[n], sems.at[n]) for n in range(count)]
     for copy in copies:
         copy.start()
     width = held_ref.shape[2]
     piece = width // CUTS
     first = 0 if joined else lax.axis_index("ep")
-    base, pieces = slot_masks(ids_ref[kind : kind + 1], first, experts)
+    ids_copy.wait()
+    base, pieces = slot_masks(ids_ref[...], first, experts)
     for n, copy in enumerate(copies):
         rows = slice(n * BASE_ROWS, (n + 1) * BASE_ROWS)
         copy.wait()
@@ -348,30 +354,55 @@
         copy.wait()
 
 
+def column_loop(width, step, body):
+    for n in range(width // step):
+        body(pl.ds(n * step, step))
+
+
 def row_weight(rows_ref, router_ref):
-    me = lax.axis_index("ep")
-    centroid = router_ref[pl.ds(me, 1), :]
-    logits = jnp.sum(rows_ref[...].astype(jnp.float32) * centroid, axis=1, keepdims=True)
-    return route_scale * jax.nn.sigmoid(logits)
-
-
-def weight_copies(weight_refs, chunk_refs, sems):
+    row_count, width = rows_ref.shape
+    experts = router_ref.shape[0]
+    own = lax.broadcasted_iota(jnp.int32, (experts, 128), 0) == lax.axis_index("ep")
+
+    def add(n, total):
+        lanes = pl.ds(pl.multiple_of(n * 128, 128), 128)
+        centroid = jnp.sum(jnp.where(own, router_ref[:, lanes], 0.0), axis=0, keepdims=True)
+        return total + rows_ref[:, lanes].astype(jnp.float32) * centroid
+
+    total = lax.fori_loop(0, width // 128, add, jnp.zeros((row_count, 128), jnp.float32), unroll=4)
+    return route_scale * jax.nn.sigmoid(jnp.sum(total, axis=1, keepdims=True))
+
+
+def weight_copies(weight_refs, held_refs, sems):
     gate_ref, up_ref, down_ref = weight_refs
-    steps, width, part = chunk_refs[0].shape
-    copies = []
+    steps = sems.shape[1]
+    part = gate_ref.shape[1] // steps
+
+    def copies(j):
+        units = pl.ds(pl.multiple_of(j * part, part), part)
+        places = ((slice(None), units), (slice(None), units), (units, slice(None)))
+        return [
+            pltpu.make_async_copy(source.at[place], held.at[place], sems.at[n, j])
+            for n, (source, held, place) in enumerate(zip(weight_refs, held_refs, places))
+        ]
+
     for j in range(steps):
-        units = slice(j * part, (j + 1) * part)
-        sources = (gate_ref.at[:, units], up_ref.at[:, units], down_ref.at[units, :])
-        copies.append(
-            [
-                pltpu.make_async_copy(source, chunk.at[j], sems.at[n, j])
-                for n, (source, chunk) in enumerate(zip(sources, chunk_refs))
-            ]
-        )
-    for step in copies:
-        for copy in step:
+        for copy in copies(j):
             copy.start()
-    return copies
+
+    def wait(j):
+        for copy in copies(j):
+            copy.wait()
+
+    return wait
+
+
+def unit_loop(sems, units, body):
+    steps = sems.shape[1]
+    part = units // steps
+
+    for j in range(steps):
+        body(j, pl.ds(j * part, part))
 
 
 def forward_kernel(experts, waited, router_ref, *refs):
@@ -379,19 +410,21 @@
     weight_refs, message_refs = refs[:3], [refs[3].at[me ^ k] for k in range(experts)]
     refs = refs[4 + waited :]
     out_refs = refs[:experts]
-    rows_ref, total_ref, gate_ref, up_ref, down_ref, sems, extra_ref, message_sems = refs[experts:]
+    rows_ref, gate_ref, up_ref, down_ref, sems, extra_ref, message_sems, total_ref = refs[experts:]
     arriving = message_copies(message_refs, 0, rows_ref, extra_ref, message_sems)
-    copies = weight_copies(weight_refs, (gate_ref, up_ref, down_ref), sems)
+    wait = weight_copies(weight_refs, (gate_ref, up_ref, down_ref), sems)
     spread(arriving, rows_ref, extra_ref)
     weight = row_weight(rows_ref, router_ref)
-    for j, step in enumerate(copies):
-        for copy in step:
-            copy.wait()
-        gate_proj = plain_dot(rows_ref[...], gate_ref[j])
-        up_proj = plain_dot(rows_ref[...], up_ref[j])
+
+    def project(j, units):
+        wait(j)
+        gate_proj = plain_dot(rows_ref[...], gate_ref[:, units])
+        up_proj = plain_dot(rows_ref[...], up_ref[:, units])
         hidden = (gate_proj * jax.nn.sigmoid(gate_proj) * up_proj).astype(jnp.bfloat16)
-        part = plain_dot(hidden, down_ref[j])
+        part = plain_dot(hidden, down_ref[units, :])
         total_ref[...] = part if j == 0 else total_ref[...] + part
+
+    unit_loop(sems, gate_ref.shape[1], project)
     expert = total_ref[...].astype(jnp.bfloat16).astype(jnp.float32)
     section = rows_ref[...].astype(jnp.float32) + weight * expert
     rows_ref[...] = section.astype(jnp.bfloat16)
@@ -405,13 +438,14 @@
     out_refs = refs[:experts]
     (
         rows_ref,
-        total_ref,
         gate_ref,
         up_ref,
         down_ref,
         sems,
         extra_ref,
         message_sems,
+        d_gate_ref,
+        d_up_ref,
         grads_ref,
         weighted_ref,
         grads_extra_ref,
@@ -419,30 +453,40 @@
     ) = refs[experts:]
     arriving = message_copies(message_refs, 0, rows_ref, extra_ref, message_sems)
     arriving_grads = message_copies(message_refs, 1, grads_ref, grads_extra_ref, grad_sems)
-    copies = weight_copies(weight_refs, (gate_ref, up_ref, down_ref), sems)
+    wait = weight_copies(weight_refs, (gate_ref, up_ref, down_ref), sems)
     spread(arriving, rows_ref, extra_ref)
     spread(arriving_grads, grads_ref, grads_extra_ref)
-    weighted = row_weight(rows_ref, router_ref) * grads_ref[...].astype(jnp.float32)
-    weighted_ref[...] = weighted.astype(jnp.bfloat16)
-    for j, step in enumerate(copies):
-        for copy in step:
-            copy.wait()
-        gate_proj = plain_dot(rows_ref[...], gate_ref[j])
-        up_proj = plain_dot(rows_ref[...], up_ref[j])
-        d_hidden = transposed_dot(weighted_ref[...], down_ref[j])
+    weight = row_weight(rows_ref, router_ref)
+
+    def weigh(columns):
+        weighted = weight * grads_ref[:, columns].astype(jnp.float32)
+        weighted_ref[:, columns] = weighted.astype(jnp.bfloat16)
+
+    def project(j, units):
+        wait(j)
+        gate_proj = plain_dot(rows_ref[...], gate_ref[:, units])
+        up_proj = plain_dot(rows_ref[...], up_ref[:, units])
+        d_hidden = transposed_dot(weighted_ref[...], down_ref[units, :])
         sigmoid_gate = jax.nn.sigmoid(gate_proj)
         d_gate = d_hidden * up_proj * sigmoid_gate * (1.0 + gate_proj * (1.0 - sigmoid_gate))
         d_up = d_hidden * gate_proj * sigmoid_gate
-        part = transposed_dot(d_gate.astype(jnp.bfloat16), gate_ref[j])
-        part = part + transposed_dot(d_up.astype(jnp.bfloat16), up_ref[j])
-        total_ref[...] = part if j == 0 else total_ref[...] + part
-    expert = total_ref[...].astype(jnp.bfloat16).astype(jnp.float32)
-    section = grads_ref[...].astype(jnp.float32) + expert
-    rows_ref[...] = section.astype(jnp.bfloat16)
+        d_gate_ref[:, units] = d_gate.astype(jnp.bfloat16)
+        d_up_ref[:, units] = d_up.astype(jnp.bfloat16)
+
+    def finish(columns):
+        total = transposed_dot(d_gate_ref[...], gate_ref[columns, :])
+        total = total + transposed_dot(d_up_ref[...], up_ref[columns, :])
+        expert = total.astype(jnp.bfloat16).astype(jnp.float32)
+        section = grads_ref[:, columns].astype(jnp.float32) + expert
+        rows_ref[:, columns] = section.astype(jnp.bfloat16)
+
+    column_loop(rows_ref.shape[1], COLUMNS, weigh)
+    unit_loop(sems, d_gate_ref.shape[1], project)
+    column_loop(rows_ref.shape[1], COLUMNS, finish)
     collect(rows_ref, extra_ref, out_refs, message_sems)
 
 
-def pack(ids_rows, sources, kind, experts, joined, after=()):
+def pack(ids_row, sources, experts, joined, after=()):
     tokens, width = sources[0].shape
     dtype = sources[0].dtype
     count = len(sources)
@@ -451,8 +495,8 @@
     anywhere = pl.BlockSpec(memory_space=pl.ANY)
     shapes = [(experts, *message)] if joined else [message] * experts
     return pl.pallas_call(
-        functools.partial(pack_kernel, kind, joined, count, experts),
-        in_specs=[pl.BlockSpec(memory_space=pltpu.VMEM)] + [anywhere] * (count + len(after)),
+        functools.partial(pack_kernel, joined, count, experts),
+        in_specs=[anywhere] * (1 + count + len(after)),
         out_specs=[anywhere] * len(shapes),
         out_shape=[jax.ShapeDtypeStruct(shape, dtype) for shape in shapes],
         scratch_shapes=[
@@ -460,15 +504,17 @@
             pltpu.VMEM((experts, *message), dtype),
             pltpu.SemaphoreType.DMA((count,)),
             pltpu.SemaphoreType.DMA((experts,)),
+            pltpu.VMEM(ids_row.shape, ids_row.dtype),
+            pltpu.SemaphoreType.DMA(()),
         ],
-        compiler_params=pltpu.CompilerParams(vmem_limit_bytes=16 << 20),
+        compiler_params=pltpu.CompilerParams(vmem_limit_bytes=PACK_BYTES),
         cost_estimate=pl.CostEstimate(
             flops=4 * slots * tokens * width,
             bytes_accessed=2 * ROWS_BYTES * slots * width,
             transcendentals=0,
         ),
         name="pack",
-    )(ids_rows, *sources, *after)
+    )(ids_row, *sources, *after)
 
 
 def unpack(ids_row, messages, order):
@@ -495,7 +541,6 @@
     width, units = gate_cols.shape
     row_count = experts * (BASE_ROWS + CUTS)
     steps = 4 if units % 512 == 0 else 1
-    part = units // steps
     result_shape = (BASE_ROWS, messages[0].shape[-1])
     in_vmem = pl.BlockSpec(memory_space=pltpu.VMEM)
     anywhere = pl.BlockSpec(memory_space=pl.ANY)
@@ -504,6 +549,11 @@
         pltpu.VMEM((experts * BASE_ROWS, width // CUTS), jnp.bfloat16),
         pltpu.SemaphoreType.DMA((2, experts)),
     ]
+    if products > 3:
+        own_scratch = [pltpu.VMEM((row_count, units), jnp.bfloat16)] * 2
+        own_scratch += [rows_scratch] * 2 + message_scratch
+    else:
+        own_scratch = [pltpu.VMEM((row_count, width), jnp.float32)]
     return pl.pallas_call(
         functools.partial(kernel, experts, len(after)),
         in_specs=[in_vmem] + [anywhere] * (3 + len(messages) + len(after)),
@@ -511,14 +561,13 @@
         out_shape=[jax.ShapeDtypeStruct(result_shape, messages[0].dtype)] * experts,
         scratch_shapes=[
             rows_scratch,
-            pltpu.VMEM((row_count, width), jnp.float32),
-            pltpu.VMEM((steps, width, part), jnp.bfloat16),
-            pltpu.VMEM((steps, width, part), jnp.bfloat16),
-            pltpu.VMEM((steps, part, width), jnp.bfloat16),
+            pltpu.VMEM((width, units), jnp.bfloat16),
+            pltpu.VMEM((width, units), jnp.bfloat16),
+            pltpu.VMEM((units, width), jnp.bfloat16),
             pltpu.SemaphoreType.DMA((3, steps)),
             *message_scratch,
-        ]
-        + ([rows_scratch] * 2 + message_scratch if products > 3 else []),
+            *own_scratch,
+        ],
         compiler_params=pltpu.CompilerParams(vmem_limit_bytes=VMEM_BYTES),
         cost_estimate=pl.CostEstimate(
             flops=2 * products * row_count * width * units,
@@ -555,16 +604,16 @@
     token_count = fwd_in.shape[1]
     router_rows = router[0].T
     weights = (w_gate[0], w_up[0], w_down[0])
-    ids = jnp.concatenate([array.reshape(1, token_count) for array in (fwd_ids, bwd_ids)], axis=0)
+    fwd_row, bwd_row = fwd_ids.reshape(1, token_count), bwd_ids.reshape(1, token_count)
     near, far = list(range(1, experts // 2)), list(range(experts // 2, experts))
-    fwd_packed = pack(ids, [fwd_in[0]], 0, experts, True)
+    fwd_packed = pack(fwd_row, [fwd_in[0]], experts, True)
     fwd_rows = lax.all_to_all(fwd_packed[0], "ep", split_axis=0, concat_axis=0, tiled=True)
-    all_ids = lax.all_gather(ids, "pp")
+    all_ids = lax.all_gather(jnp.concatenate([fwd_row, bwd_row], axis=0), "pp")
     section, sections = lax.axis_index("pp"), lax.axis_size("pp")
     fwd_row_next = lax.dynamic_index_in_dim(all_ids, (section + sections - 1) % sections, 0, False)[:1]
     bwd_row_next = lax.dynamic_index_in_dim(all_ids, (section + 1) % sections, 0, False)[1:]
     after = [fwd_packed[0], fwd_row_next, bwd_row_next]
-    bwd_packed = pack(ids, [saved_in[0], grad_in[0]], 1, experts, False, after)
+    bwd_packed = pack(bwd_row, [saved_in[0], grad_in[0]], experts, False, after)
     bwd_rows = exchanged(bwd_packed, range(1, experts))
     after = [bwd_rows[k] for k in near]
     fwd_out = expert_call(
@@ -577,7 +626,7 @@
     )
     bwd_back = returned(bwd_out, range(experts), -1)
     fwd_next = unpack(fwd_row_next, fwd_back, near + [0] + far)
-    grad_next = unpack(bwd_row_next, bwd_back, near[:1] + far + near[1:] + [0])
+    grad_next = unpack(bwd_row_next, bwd_back, far[:1] + near[:1] + far[1:] + near[1:] + [0])
     return (fwd_next[None], grad_next[None])
 
 

time: 148 us -> 143 us (0.966); the launches traced: 146 us -> 143 us
  local copies, waits for them, and re-layouts: 3.56 us -> 0.61 us
  Pallas kernels: 39.9 us -> 37.7 us
  waiting for transfers between devices: 36.7 us -> 38.9 us
    pallas_call x2, Pallas kernels: 31 us -> 27.3 us  [expert_call(): pl.pallas_call(functools.partial(kernel, experts, len(after)), in_specs=[...]
    unnamed x16 -> x8, local copies, waits for them, and re-layouts: 3.55 us -> 0.02 us
    ppermute x16, waiting for transfers between devices: 13.7 us -> 16.1 us  [returned(): back[k] = lax.ppermute(messages[k], ('pp', 'ep'), pairs)]
    pallas_call x2, Pallas kernels: 5.35 us -> 6.89 us  [pack(): pl.pallas_call(functools.partial(pack_kernel, joined, count, experts), in...]
  transfers between devices with their start and end apart: 24 -> 24, of which waited for: 9 -> 7; matrix products, arithmetic and copies ran while one was open for 0% -> 1% of each run, Pallas kernels for 25% -> 23%
where the time goes in v3:
time: 143 us
  starting transfers between devices  58.1 us (41%)
  waiting for transfers between devices  38.9 us (27%)
  Pallas kernels  37.7 us (26%)
  blocking collectives  6.1 us (4%)
    ppermute x16, starting transfers between devices, returned(): back[k] = lax.ppermute(messages[k], ('pp', 'ep'), pairs)  44.3 us
    pallas_call x2, Pallas kernels, expert_call(): pl.pallas_call(functools.partial(kernel, experts, len(after)), in_specs=[...  27.3 us
    ppermute x7, waiting for transfers between devices, exchanged(): lax.ppermute(messages[k], 'ep', [(i, i ^ k) for i in range(experts)])  22.8 us
    ppermute x16, waiting for transfers between devices, returned(): back[k] = lax.ppermute(messages[k], ('pp', 'ep'), pairs)  16.1 us
    ppermute x7, starting transfers between devices, exchanged(): lax.ppermute(messages[k], 'ep', [(i, i ^ k) for i in range(experts)])  8.06 us
    pallas_call x2, Pallas kernels, pack(): pl.pallas_call(functools.partial(pack_kernel, joined, count, experts), in...  6.89 us
    all_gather x1, blocking collectives, per_device_whole(): all_ids = lax.all_gather(jnp.concatenate([fwd_row, bwd_row], axis=0), 'pp')  6.1 us
    all_to_all x1, starting transfers between devices, per_device_whole(): lax.all_to_all(fwd_packed[0], 'ep', split_axis=0, concat_axis=0, tiled=True)  5.7 us
  transfers between devices with their start and end apart: 24, of which 7 were waited for; matrix products, arithmetic and copies ran while one was open for 1% of the time, Pallas kernels for 23%

profile of v3, /device:TPU:9, one launch (start us, length us, event | category | flops | bytes accessed | tf_op | source)
XLA Modules:
  0.0 142.8 jit_solution(11908301518471887952)
XLA Ops:
  0.6 3.0 %pack.2.refs_2_ = bf16[8,16,4480]{2,1,0:T(8,128)(2,1)} custom-call(s32[1,128]{1,0:T(1,128)} %bitcast.32, bf16[128,3584]{1,0:T(8,128)(2,1)} %bitcast.27), custom_call_target="tpu_custom_call" | custom-call | flops 234881024 | bytes 1835008 | tf_op jit(solution)/shard_map/pack/pallas_call | solution.py:497
  3.6 5.7 %all-to-all-start = ((bf16[8,16,4480]{2,1,0:T(8,128)(2,1)}), bf16[8,16,4480]{2,1,0:T(8,128)(2,1)S(1)}, u32[]{:S(2)}, u32[]{:S(2)}) async-start(bf16[8,16,4480]{2,1,0:T(8,128)(2,1)} %pack.2.refs_2_), calls=%async_computation | async-start | bytes 2293760 | tf_op jit(solution)/shard_map/all_to_all | solution.py:610
  10.0 6.1 %all-gather.1 = s32[4,2,128]{2,1,0:T(2,128)S(1)} all-gather(s32[1,2,128]{2,1,0:T(2,128)S(1)} %add_bitcast_fusion), channel_id=2, replica_groups=mesh['pp'=4,'ep'=8] {'pp'}, dimensions={0}, use_global_device_ids=true | all-gather | bytes 5120 | tf_op jit(solution)/shard_map/all_gather | solution.py:611
  16.7 3.9 %pack.3 = (bf16[32,4480]{1,0:T(8,128)(2,1)}, bf16[32,4480]{1,0:T(8,128)(2,1)}, bf16[32,4480]{1,0:T(8,128)(2,1)}, bf16[32,4480]{1,0:T(8,128)(2,1)}, bf16[32,4480]...) custom-call(s32[1,128]{1,0:T(1,128)} %bitcast.35, ...), custom_call_target="tpu_custom_call" | custom-call | flops 469762048 | bytes 3670016 | tf_op jit(solution)/shard_map/pack/pallas_call | solution.py:497
  23.3 2.1 %collective-permute-start.11 = (bf16[32,4480]{1,0:T(8,128)(2,1)}, bf16[32,4480]{1,0:T(8,128)(2,1)S(1)}, u32[]{:S(2)}, u32[]{:S(2)}) collective-permute-start(bf16[32,4480]{1,0:T(8,128)(2,1)} %get-tuple-element.38), channel_id=1, source_target_pairs={{0,4},{1,5},{2,6},{3,7},{4,0},{5,1},{6,2},{7,3},{8,12},{9,13},{10,... | collective-permute-start | bytes 860168 | tf_op jit(solution)/shard_map/ppermute | solution.py:585
  26.6 8.5 %collective-permute-done.refs_4_ = bf16[32,4480]{1,0:T(8,128)(2,1)S(1)} collective-permute-done((bf16[32,4480]{1,0:T(8,128)(2,1)}, bf16[32,4480]{1,0:T(8,128)(2,1)S(1)}, u32[]{:S(2)}, u32[]{:S(2)}) %collective-permute-start) | collective-permute-done | bytes 286752 | tf_op jit(solution)/shard_map/ppermute | solution.py:585
  35.4 1.9 %collective-permute-start.14 = (bf16[32,4480]{1,0:T(8,128)(2,1)}, bf16[32,4480]{1,0:T(8,128)(2,1)S(1)}, u32[]{:S(2)}, u32[]{:S(2)}) collective-permute-start(bf16[32,4480]{1,0:T(8,128)(2,1)} %get-tuple-element.41), channel_id=1, source_target_pairs={{0,7},{1,6},{2,5},{3,4},{4,3},{5,2},{6,1},{7,0},{8,15},{9,14},{10,... | collective-permute-start | bytes 860168 | tf_op jit(solution)/shard_map/ppermute | solution.py:585
  37.2 11.0 %collective-permute-done.2.refs_6_ = bf16[32,4480]{1,0:T(8,128)(2,1)S(1)} collective-permute-done((bf16[32,4480]{1,0:T(8,128)(2,1)}, bf16[32,4480]{1,0:T(8,128)(2,1)S(1)}, u32[]{:S(2)}, u32[]{:S(2)}) %collective-permute-start.2) | collective-permute-done | bytes 286752 | tf_op jit(solution)/shard_map/ppermute | solution.py:585
  48.3 10.7 %forward.1 = (bf16[16,4480]{1,0:T(8,128)(2,1)S(1)}, bf16[16,4480]{1,0:T(8,128)(2,1)S(1)}, bf16[16,4480]{1,0:T(8,128)(2,1)S(1)}, bf16[16,4480]{1,0:T(8,128)(2,1)S...) custom-call(f32[8,3584]{1,0:T(8,128)S(1)} %bitcast.19, ...), custom_call_target="tpu_custom_call" | custom-call | flops 3523215360 | bytes 22020096 | tf_op jit(solution)/shard_map/forward/pallas_call | solution.py:557
  59.0 2.2 %collective-permute-start.3 = (bf16[16,4480]{1,0:T(8,128)(2,1)S(1)}, bf16[16,4480]{1,0:T(8,128)(2,1)S(1)}, u32[]{:S(2)}, u32[]{:S(2)}) collective-permute-start(bf16[16,4480]{1,0:T(8,128)(2,1)S(1)} %get-tuple-element.29), channel_id=1, source_target_pairs={{0,9},{1,8},{2,11},{3,10},{4,13},{5,12},{6,15},{7,14},{8,17},{9,16... | collective-permute-start | bytes 430088 | tf_op jit(solution)/shard_map/ppermute | solution.py:598
  61.2 10.2 %collective-permute-start.4 = (bf16[16,4480]{1,0:T(8,128)(2,1)S(1)}, bf16[16,4480]{1,0:T(8,128)(2,1)S(1)}, u32[]{:S(2)}, u32[]{:S(2)}) collective-permute-start(bf16[16,4480]{1,0:T(8,128)(2,1)S(1)} %get-tuple-element.30), channel_id=1, source_target_pairs={{0,10},{1,11},{2,8},{3,9},{4,14},{5,15},{6,12},{7,13},{8,18},{9,19... | collective-permute-start | bytes 430088 | tf_op jit(solution)/shard_map/ppermute | solution.py:598
  71.6 6.7 %collective-permute-start.5 = (bf16[16,4480]{1,0:T(8,128)(2,1)S(1)}, bf16[16,4480]{1,0:T(8,128)(2,1)S(1)}, u32[]{:S(2)}, u32[]{:S(2)}) collective-permute-start(bf16[16,4480]{1,0:T(8,128)(2,1)S(1)} %get-tuple-element.31), channel_id=1, source_target_pairs={{0,11},{1,10},{2,9},{3,8},{4,15},{5,14},{6,13},{7,12},{8,19},{9,18... | collective-permute-start | bytes 430088 | tf_op jit(solution)/shard_map/ppermute | solution.py:598
  78.3 4.3 %collective-permute-start.6 = (bf16[16,4480]{1,0:T(8,128)(2,1)S(1)}, bf16[16,4480]{1,0:T(8,128)(2,1)S(1)}, u32[]{:S(2)}, u32[]{:S(2)}) collective-permute-start(bf16[16,4480]{1,0:T(8,128)(2,1)S(1)} %get-tuple-element.32), channel_id=1, source_target_pairs={{0,8},{1,9},{2,10},{3,11},{4,12},{5,13},{6,14},{7,15},{8,16},{9,17... | collective-permute-start | bytes 430088 | tf_op jit(solution)/shard_map/ppermute | solution.py:598
  82.7 3.0 %collective-permute-done.14.refs_10_ = bf16[32,4480]{1,0:T(8,128)(2,1)S(1)} collective-permute-done((bf16[32,4480]{1,0:T(8,128)(2,1)}, bf16[32,4480]{1,0:T(8,128)(2,1)S(1)}, u32[]{:S(2)}, u32[]{:S(2)}) %collective-permute-start.14) | collective-permute-done | bytes 286752 | tf_op jit(solution)/shard_map/ppermute | solution.py:585
  85.7 3.4 %collective-permute-start.8 = (bf16[16,4480]{1,0:T(8,128)(2,1)S(1)}, bf16[16,4480]{1,0:T(8,128)(2,1)S(1)}, u32[]{:S(2)}, u32[]{:S(2)}) collective-permute-start(bf16[16,4480]{1,0:T(8,128)(2,1)S(1)} %get-tuple-element.34), channel_id=1, source_target_pairs={{0,13},{1,12},{2,15},{3,14},{4,9},{5,8},{6,11},{7,10},{8,21},{9,20... | collective-permute-start | bytes 430088 | tf_op jit(solution)/shard_map/ppermute | solution.py:598
  89.1 2.8 %collective-permute-start.9 = (bf16[16,4480]{1,0:T(8,128)(2,1)S(1)}, bf16[16,4480]{1,0:T(8,128)(2,1)S(1)}, u32[]{:S(2)}, u32[]{:S(2)}) collective-permute-start(bf16[16,4480]{1,0:T(8,128)(2,1)S(1)} %get-tuple-element.35), channel_id=1, source_target_pairs={{0,14},{1,15},{2,12},{3,13},{4,10},{5,11},{6,8},{7,9},{8,22},{9,23... | collective-permute-start | bytes 430088 | tf_op jit(solution)/shard_map/ppermute | solution.py:598
  92.1 16.6 %backward.1 = (bf16[16,4480]{1,0:T(8,128)(2,1)S(1)}, bf16[16,4480]{1,0:T(8,128)(2,1)S(1)}, bf16[16,4480]{1,0:T(8,128)(2,1)S(1)}, bf16[16,4480]{1,0:T(8,128)(2,1)...) custom-call(f32[8,3584]{1,0:T(8,128)S(1)} %bitcast.20, ...), custom_call_target="tpu_custom_call" | custom-call | flops 5872025600 | bytes 22020096 | tf_op jit(solution)/shard_map/backward/pallas_call | solution.py:557
  110.4 2.8 %collective-permute-start.16 = (bf16[16,4480]{1,0:T(8,128)(2,1)S(1)}, bf16[16,4480]{1,0:T(8,128)(2,1)S(1)}, u32[]{:S(2)}, u32[]{:S(2)}) collective-permute-start(bf16[16,4480]{1,0:T(8,128)(2,1)S(1)} %get-tuple-element.43), channel_id=1, source_target_pairs={{0,25},{1,24},{2,27},{3,26},{4,29},{5,28},{6,31},{7,30},{8,1},{9,0... | collective-permute-start | bytes 430088 | tf_op jit(solution)/shard_map/ppermute | solution.py:598
  116.7 8.5 %collective-permute-done.15.refs_0_ = bf16[16,4480]{1,0:T(8,128)(2,1)S(1)} collective-permute-done((bf16[16,4480]{1,0:T(8,128)(2,1)S(1)}, bf16[16,4480]{1,0:T(8,128)(2,1)S(1)}, u32[]{:S(2)}, u32[]{:S(2)}) %collective-permute-start.15) | collective-permute-done | bytes 143392 | tf_op jit(solution)/shard_map/ppermute | solution.py:598
  125.2 4.0 %collective-permute-start.20 = (bf16[16,4480]{1,0:T(8,128)(2,1)S(1)}, bf16[16,4480]{1,0:T(8,128)(2,1)S(1)}, u32[]{:S(2)}, u32[]{:S(2)}) collective-permute-start(bf16[16,4480]{1,0:T(8,128)(2,1)S(1)} %get-tuple-element.47), channel_id=1, source_target_pairs={{0,26},{1,27},{2,24},{3,25},{4,30},{5,31},{6,28},{7,29},{8,2},{9,3... | collective-permute-start | bytes 430088 | tf_op jit(solution)/shard_map/ppermute | solution.py:598
  131.7 1.7 %unpack.2 = bf16[128,3584]{1,0:T(8,128)(2,1)} custom-call(s32[1,128]{1,0:T(1,128)S(1)} %copy-done.3, bf16[16,4480]{1,0:T(8,128)(2,1)S(1)} %collective-permute-done.3.refs_0_.refs_11_, bf16[16,4480]{1,0:T(8,128)(2,1)S(1)} %collective-permute-done.4.refs_1_.refs_12_, bf16[16,4480]{1,0:T(8,128)(2,1)S(1)} %collective-permute-done.5.refs_2_.refs_13_, ...), custom_call_target="tpu_custom_call" | custom-call | flops 234881024 | bytes 1835008 | tf_op jit(solution)/shard_map/unpack/pallas_call | solution.py:525
  133.5 2.5 %collective-permute-done.18.refs_3_ = bf16[16,4480]{1,0:T(8,128)(2,1)S(1)} collective-permute-done((bf16[16,4480]{1,0:T(8,128)(2,1)S(1)}, bf16[16,4480]{1,0:T(8,128)(2,1)S(1)}, u32[]{:S(2)}, u32[]{:S(2)}) %collective-permute-start.18) | collective-permute-done | bytes 143392 | tf_op jit(solution)/shard_map/ppermute | solution.py:598
  135.9 5.1 %collective-permute-done.19.refs_4_ = bf16[16,4480]{1,0:T(8,128)(2,1)S(1)} collective-permute-done((bf16[16,4480]{1,0:T(8,128)(2,1)S(1)}, bf16[16,4480]{1,0:T(8,128)(2,1)S(1)}, u32[]{:S(2)}, u32[]{:S(2)}) %collective-permute-start.19) | collective-permute-done | bytes 143392 | tf_op jit(solution)/shard_map/ppermute | solution.py:598
  141.1 1.7 %unpack.3 = bf16[128,3584]{1,0:T(8,128)(2,1)} custom-call(s32[1,128]{1,0:T(1,128)S(1)} %copy-done.2, bf16[16,4480]{1,0:T(8,128)(2,1)S(1)} %collective-permute-done.15.refs_0_, bf16[16,4480]{1,0:T(8,128)(2,1)S(1)} %collective-permute-done.16.refs_1_, bf16[16,4480]{1,0:T(8,128)(2,1)S(1)} %collective-permute-done.17.refs_2_, ...), custom_call_target="tpu_custom_call" | custom-call | flops 234881024 | bytes 1835008 | tf_op jit(solution)/shard_map/unpack/pallas_call | solution.py:525
  (42 shorter events, 13.5 us)
Async XLA Ops:
  3.6 44.7 %all-to-all-start = ((bf16[8,16,4480]{2,1,0:T(8,128)(2,1)}), bf16[8,16,4480]{2,1,0:T(8,128)(2,1)S(1)}, u32[]{:S(2)}, u32[]{:S(2)}) async-start(bf16[8,16,4480]{2,1,0:T(8,128)(2,1)} %pack.2.refs_2_), calls=%async_computation | async-start | bytes 2293760 | tf_op jit(solution)/shard_map/all_to_all | solution.py:610
  20.6 14.5 %collective-permute-start = (bf16[32,4480]{1,0:T(8,128)(2,1)}, bf16[32,4480]{1,0:T(8,128)(2,1)S(1)}, u32[]{:S(2)}, u32[]{:S(2)}) collective-permute-start(bf16[32,4480]{1,0:T(8,128)(2,1)} %get-tuple-element.26), channel_id=1, source_target_pairs={{0,1},{1,0},{2,3},{3,2},{4,5},{5,4},{6,7},{7,6},{8,9},{9,8},{10,11... | collective-permute-start | bytes 860168 | tf_op jit(solution)/shard_map/ppermute | solution.py:585
  21.9 13.5 %collective-permute-start.1 = (bf16[32,4480]{1,0:T(8,128)(2,1)}, bf16[32,4480]{1,0:T(8,128)(2,1)S(1)}, u32[]{:S(2)}, u32[]{:S(2)}) collective-permute-start(bf16[32,4480]{1,0:T(8,128)(2,1)} %get-tuple-element.27), channel_id=1, source_target_pairs={{0,2},{1,3},{2,0},{3,1},{4,6},{5,7},{6,4},{7,5},{8,10},{9,11},{10,... | collective-permute-start | bytes 860168 | tf_op jit(solution)/shard_map/ppermute | solution.py:585
  22.2 26.1 %collective-permute-start.2 = (bf16[32,4480]{1,0:T(8,128)(2,1)}, bf16[32,4480]{1,0:T(8,128)(2,1)S(1)}, u32[]{:S(2)}, u32[]{:S(2)}) collective-permute-start(bf16[32,4480]{1,0:T(8,128)(2,1)} %get-tuple-element.28), channel_id=1, source_target_pairs={{0,3},{1,2},{2,1},{3,0},{4,7},{5,6},{6,5},{7,4},{8,11},{9,10},{10,... | collective-permute-start | bytes 860168 | tf_op jit(solution)/shard_map/ppermute | solution.py:585
  23.3 37.8 %collective-permute-start.11 = (bf16[32,4480]{1,0:T(8,128)(2,1)}, bf16[32,4480]{1,0:T(8,128)(2,1)S(1)}, u32[]{:S(2)}, u32[]{:S(2)}) collective-permute-start(bf16[32,4480]{1,0:T(8,128)(2,1)} %get-tuple-element.38), channel_id=1, source_target_pairs={{0,4},{1,5},{2,6},{3,7},{4,0},{5,1},{6,2},{7,3},{8,12},{9,13},{10,... | collective-permute-start | bytes 860168 | tf_op jit(solution)/shard_map/ppermute | solution.py:585
  25.4 46.1 %collective-permute-start.12 = (bf16[32,4480]{1,0:T(8,128)(2,1)}, bf16[32,4480]{1,0:T(8,128)(2,1)S(1)}, u32[]{:S(2)}, u32[]{:S(2)}) collective-permute-start(bf16[32,4480]{1,0:T(8,128)(2,1)} %get-tuple-element.39), channel_id=1, source_target_pairs={{0,5},{1,4},{2,7},{3,6},{4,1},{5,0},{6,3},{7,2},{8,13},{9,12},{10,... | collective-permute-start | bytes 860168 | tf_op jit(solution)/shard_map/ppermute | solution.py:585
  35.2 43.2 %collective-permute-start.13 = (bf16[32,4480]{1,0:T(8,128)(2,1)}, bf16[32,4480]{1,0:T(8,128)(2,1)S(1)}, u32[]{:S(2)}, u32[]{:S(2)}) collective-permute-start(bf16[32,4480]{1,0:T(8,128)(2,1)} %get-tuple-element.40), channel_id=1, source_target_pairs={{0,6},{1,7},{2,4},{3,5},{4,2},{5,3},{6,0},{7,1},{8,14},{9,15},{10,... | collective-permute-start | bytes 860168 | tf_op jit(solution)/shard_map/ppermute | solution.py:585
  35.4 50.3 %collective-permute-start.14 = (bf16[32,4480]{1,0:T(8,128)(2,1)}, bf16[32,4480]{1,0:T(8,128)(2,1)S(1)}, u32[]{:S(2)}, u32[]{:S(2)}) collective-permute-start(bf16[32,4480]{1,0:T(8,128)(2,1)} %get-tuple-element.41), channel_id=1, source_target_pairs={{0,7},{1,6},{2,5},{3,4},{4,3},{5,2},{6,1},{7,0},{8,15},{9,14},{10,... | collective-permute-start | bytes 860168 | tf_op jit(solution)/shard_map/ppermute | solution.py:585
  59.0 26.7 %collective-permute-start.3 = (bf16[16,4480]{1,0:T(8,128)(2,1)S(1)}, bf16[16,4480]{1,0:T(8,128)(2,1)S(1)}, u32[]{:S(2)}, u32[]{:S(2)}) collective-permute-start(bf16[16,4480]{1,0:T(8,128)(2,1)S(1)} %get-tuple-element.29), channel_id=1, source_target_pairs={{0,9},{1,8},{2,11},{3,10},{4,13},{5,12},{6,15},{7,14},{8,17},{9,16... | collective-permute-start | bytes 430088 | tf_op jit(solution)/shard_map/ppermute | solution.py:598
  61.2 27.9 %collective-permute-start.4 = (bf16[16,4480]{1,0:T(8,128)(2,1)S(1)}, bf16[16,4480]{1,0:T(8,128)(2,1)S(1)}, u32[]{:S(2)}, u32[]{:S(2)}) collective-permute-start(bf16[16,4480]{1,0:T(8,128)(2,1)S(1)} %get-tuple-element.30), channel_id=1, source_target_pairs={{0,10},{1,11},{2,8},{3,9},{4,14},{5,15},{6,12},{7,13},{8,18},{9,19... | collective-permute-start | bytes 430088 | tf_op jit(solution)/shard_map/ppermute | solution.py:598
  71.6 20.3 %collective-permute-start.5 = (bf16[16,4480]{1,0:T(8,128)(2,1)S(1)}, bf16[16,4480]{1,0:T(8,128)(2,1)S(1)}, u32[]{:S(2)}, u32[]{:S(2)}) collective-permute-start(bf16[16,4480]{1,0:T(8,128)(2,1)S(1)} %get-tuple-element.31), channel_id=1, source_target_pairs={{0,11},{1,10},{2,9},{3,8},{4,15},{5,14},{6,13},{7,12},{8,19},{9,18... | collective-permute-start | bytes 430088 | tf_op jit(solution)/shard_map/ppermute | solution.py:598
  78.3 13.8 %collective-permute-start.6 = (bf16[16,4480]{1,0:T(8,128)(2,1)S(1)}, bf16[16,4480]{1,0:T(8,128)(2,1)S(1)}, u32[]{:S(2)}, u32[]{:S(2)}) collective-permute-start(bf16[16,4480]{1,0:T(8,128)(2,1)S(1)} %get-tuple-element.32), channel_id=1, source_target_pairs={{0,8},{1,9},{2,10},{3,11},{4,12},{5,13},{6,14},{7,15},{8,16},{9,17... | collective-permute-start | bytes 430088 | tf_op jit(solution)/shard_map/ppermute | solution.py:598
  85.7 24.7 %collective-permute-start.7 = (bf16[16,4480]{1,0:T(8,128)(2,1)S(1)}, bf16[16,4480]{1,0:T(8,128)(2,1)S(1)}, u32[]{:S(2)}, u32[]{:S(2)}) collective-permute-start(bf16[16,4480]{1,0:T(8,128)(2,1)S(1)} %get-tuple-element.33), channel_id=1, source_target_pairs={{0,12},{1,13},{2,14},{3,15},{4,8},{5,9},{6,10},{7,11},{8,20},{9,21... | collective-permute-start | bytes 430088 | tf_op jit(solution)/shard_map/ppermute | solution.py:598
  85.7 27.5 %collective-permute-start.8 = (bf16[16,4480]{1,0:T(8,128)(2,1)S(1)}, bf16[16,4480]{1,0:T(8,128)(2,1)S(1)}, u32[]{:S(2)}, u32[]{:S(2)}) collective-permute-start(bf16[16,4480]{1,0:T(8,128)(2,1)S(1)} %get-tuple-element.34), channel_id=1, source_target_pairs={{0,13},{1,12},{2,15},{3,14},{4,9},{5,8},{6,11},{7,10},{8,21},{9,20... | collective-permute-start | bytes 430088 | tf_op jit(solution)/shard_map/ppermute | solution.py:598
  89.1 25.6 %collective-permute-start.9 = (bf16[16,4480]{1,0:T(8,128)(2,1)S(1)}, bf16[16,4480]{1,0:T(8,128)(2,1)S(1)}, u32[]{:S(2)}, u32[]{:S(2)}) collective-permute-start(bf16[16,4480]{1,0:T(8,128)(2,1)S(1)} %get-tuple-element.35), channel_id=1, source_target_pairs={{0,14},{1,15},{2,12},{3,13},{4,10},{5,11},{6,8},{7,9},{8,22},{9,23... | collective-permute-start | bytes 430088 | tf_op jit(solution)/shard_map/ppermute | solution.py:598
  91.9 23.1 %collective-permute-start.10 = (bf16[16,4480]{1,0:T(8,128)(2,1)S(1)}, bf16[16,4480]{1,0:T(8,128)(2,1)S(1)}, u32[]{:S(2)}, u32[]{:S(2)}) collective-permute-start(bf16[16,4480]{1,0:T(8,128)(2,1)S(1)} %get-tuple-element.36), channel_id=1, source_target_pairs={{0,15},{1,14},{2,13},{3,12},{4,11},{5,10},{6,9},{7,8},{8,23},{9,22... | collective-permute-start | bytes 430088 | tf_op jit(solution)/shard_map/ppermute | solution.py:598
  108.7 16.4 %collective-permute-start.15 = (bf16[16,4480]{1,0:T(8,128)(2,1)S(1)}, bf16[16,4480]{1,0:T(8,128)(2,1)S(1)}, u32[]{:S(2)}, u32[]{:S(2)}) collective-permute-start(bf16[16,4480]{1,0:T(8,128)(2,1)S(1)} %get-tuple-element.42), channel_id=1, source_target_pairs={{0,28},{1,29},{2,30},{3,31},{4,24},{5,25},{6,26},{7,27},{8,4},{9,5... | collective-permute-start | bytes 430088 | tf_op jit(solution)/shard_map/ppermute | solution.py:598
  110.4 18.8 %collective-permute-start.16 = (bf16[16,4480]{1,0:T(8,128)(2,1)S(1)}, bf16[16,4480]{1,0:T(8,128)(2,1)S(1)}, u32[]{:S(2)}, u32[]{:S(2)}) collective-permute-start(bf16[16,4480]{1,0:T(8,128)(2,1)S(1)} %get-tuple-element.43), channel_id=1, source_target_pairs={{0,25},{1,24},{2,27},{3,26},{4,29},{5,28},{6,31},{7,30},{8,1},{9,0... | collective-permute-start | bytes 430088 | tf_op jit(solution)/shard_map/ppermute | solution.py:598
  113.2 17.3 %collective-permute-start.17 = (bf16[16,4480]{1,0:T(8,128)(2,1)S(1)}, bf16[16,4480]{1,0:T(8,128)(2,1)S(1)}, u32[]{:S(2)}, u32[]{:S(2)}) collective-permute-start(bf16[16,4480]{1,0:T(8,128)(2,1)S(1)} %get-tuple-element.44), channel_id=1, source_target_pairs={{0,29},{1,28},{2,31},{3,30},{4,25},{5,24},{6,27},{7,26},{8,5},{9,4... | collective-permute-start | bytes 430088 | tf_op jit(solution)/shard_map/ppermute | solution.py:598
  114.7 21.3 %collective-permute-start.18 = (bf16[16,4480]{1,0:T(8,128)(2,1)S(1)}, bf16[16,4480]{1,0:T(8,128)(2,1)S(1)}, u32[]{:S(2)}, u32[]{:S(2)}) collective-permute-start(bf16[16,4480]{1,0:T(8,128)(2,1)S(1)} %get-tuple-element.45), channel_id=1, source_target_pairs={{0,30},{1,31},{2,28},{3,29},{4,26},{5,27},{6,24},{7,25},{8,6},{9,7... | collective-permute-start | bytes 430088 | tf_op jit(solution)/shard_map/ppermute | solution.py:598
  114.9 26.1 %collective-permute-start.19 = (bf16[16,4480]{1,0:T(8,128)(2,1)S(1)}, bf16[16,4480]{1,0:T(8,128)(2,1)S(1)}, u32[]{:S(2)}, u32[]{:S(2)}) collective-permute-start(bf16[16,4480]{1,0:T(8,128)(2,1)S(1)} %get-tuple-element.46), channel_id=1, source_target_pairs={{0,31},{1,30},{2,29},{3,28},{4,27},{5,26},{6,25},{7,24},{8,7},{9,6... | collective-permute-start | bytes 430088 | tf_op jit(solution)/shard_map/ppermute | solution.py:598
  125.2 15.9 %collective-permute-start.20 = (bf16[16,4480]{1,0:T(8,128)(2,1)S(1)}, bf16[16,4480]{1,0:T(8,128)(2,1)S(1)}, u32[]{:S(2)}, u32[]{:S(2)}) collective-permute-start(bf16[16,4480]{1,0:T(8,128)(2,1)S(1)} %get-tuple-element.47), channel_id=1, source_target_pairs={{0,26},{1,27},{2,24},{3,25},{4,30},{5,31},{6,28},{7,29},{8,2},{9,3... | collective-permute-start | bytes 430088 | tf_op jit(solution)/shard_map/ppermute | solution.py:598
  129.2 11.9 %collective-permute-start.21 = (bf16[16,4480]{1,0:T(8,128)(2,1)S(1)}, bf16[16,4480]{1,0:T(8,128)(2,1)S(1)}, u32[]{:S(2)}, u32[]{:S(2)}) collective-permute-start(bf16[16,4480]{1,0:T(8,128)(2,1)S(1)} %get-tuple-element.48), channel_id=1, source_target_pairs={{0,27},{1,26},{2,25},{3,24},{4,31},{5,30},{6,29},{7,28},{8,3},{9,2... | collective-permute-start | bytes 430088 | tf_op jit(solution)/shard_map/ppermute | solution.py:598
  130.5 10.5 %collective-permute-start.22 = (bf16[16,4480]{1,0:T(8,128)(2,1)S(1)}, bf16[16,4480]{1,0:T(8,128)(2,1)S(1)}, u32[]{:S(2)}, u32[]{:S(2)}) collective-permute-start(bf16[16,4480]{1,0:T(8,128)(2,1)S(1)} %get-tuple-element.49), channel_id=1, source_target_pairs={{0,24},{1,25},{2,26},{3,27},{4,28},{5,29},{6,30},{7,31},{8,0},{9,1... | collective-permute-start | bytes 430088 | tf_op jit(solution)/shard_map/ppermute | solution.py:598
  (4 other events, 180.1 us)

commit v4 on v3

--- a/solution.py
+++ b/solution.py
@@ -277,8 +277,10 @@
 def unpack_kernel(order, ids_ref, *refs):
     me = lax.axis_index("ep")
     experts = len(order)
-    message_refs, out_ref = [refs[order.index(k)] for k in range(experts)], refs[experts]
+    message_refs = [refs[order.index(k)] for k in range(experts)]
+    out_ref, made_ref, sems = refs[experts:]
     width = out_ref.shape[1]
+    sent = []
     piece = width // CUTS
     base, pieces = slot_masks(ids_ref[...], me, experts)
     from_rows = (((0,), (0,)), ((), ()))
@@ -290,7 +292,13 @@
         total = total + lax.dot_general(
             pieces[q], extra, from_rows, preferred_element_type=jnp.float32
         )
-        out_ref[:, columns] = total.astype(jnp.bfloat16)
+        made_ref[:, columns] = total.astype(jnp.bfloat16)
+        sent.append(
+            pltpu.make_async_copy(made_ref.at[:, columns], out_ref.at[:, columns], sems.at[q])
+        )
+        sent[q].start()
+    for copy in sent:
+        copy.wait()
 
 
 def piece_places(experts, q):
@@ -431,9 +439,9 @@
     collect(rows_ref, extra_ref, out_refs, message_sems)
 
 
-def backward_kernel(experts, waited, router_ref, *refs):
+def backward_kernel(order, experts, waited, router_ref, *refs):
     weight_refs = refs[:3]
-    message_refs = refs[3 : 3 + experts]
+    message_refs = [refs[3 + order.index(k)] for k in range(experts)]
     refs = refs[3 + experts + waited :]
     out_refs = refs[:experts]
     (
@@ -524,7 +532,12 @@
     slots = experts * BASE_ROWS
     return pl.pallas_call(
         functools.partial(unpack_kernel, order),
+        out_specs=pl.BlockSpec(memory_space=pl.ANY),
         out_shape=jax.ShapeDtypeStruct((tokens, width), messages[0].dtype),
+        scratch_shapes=[
+            pltpu.VMEM((tokens, width), messages[0].dtype),
+            pltpu.SemaphoreType.DMA((CUTS,)),
+        ],
         compiler_params=pltpu.CompilerParams(vmem_limit_bytes=16 << 20),
         cost_estimate=pl.CostEstimate(
             flops=4 * slots * tokens * width,
@@ -612,21 +625,22 @@
     section, sections = lax.axis_index("pp"), lax.axis_size("pp")
     fwd_row_next = lax.dynamic_index_in_dim(all_ids, (section + sections - 1) % sections, 0, False)[:1]
     bwd_row_next = lax.dynamic_index_in_dim(all_ids, (section + 1) % sections, 0, False)[1:]
-    after = [fwd_packed[0], fwd_row_next, bwd_row_next]
+    after = [fwd_packed[0]]
     bwd_packed = pack(bwd_row, [saved_in[0], grad_in[0]], experts, False, after)
-    bwd_rows = exchanged(bwd_packed, range(1, experts))
-    after = [bwd_rows[k] for k in near]
+    order = [0, *near, *far]
+    bwd_rows = exchanged(bwd_packed, order[1:])
+    after = [bwd_rows[k] for k in near] + [fwd_row_next, bwd_row_next]
     fwd_out = expert_call(
         forward_kernel, "forward", router_rows, *weights, [fwd_rows], experts, 3, after
     )
     fwd_back = returned(fwd_out, range(experts), 1)
     after = [fwd_back[k] for k in near + [0]]
     bwd_out = expert_call(
-        backward_kernel, "backward", router_rows, *weights, bwd_rows, experts, 5, after
+        functools.partial(backward_kernel, order), "backward", router_rows, *weights, [bwd_rows[k] for k in order], experts, 5, after
     )
     bwd_back = returned(bwd_out, range(experts), -1)
     fwd_next = unpack(fwd_row_next, fwd_back, near + [0] + far)
-    grad_next = unpack(bwd_row_next, bwd_back, far[:1] + near[:1] + far[1:] + near[1:] + [0])
+    grad_next = unpack(bwd_row_next, bwd_back, far[:1] + near + far[1:] + [0])
     return (fwd_next[None], grad_next[None])
 
 

time: 143 us -> 141 us (0.986)
  waiting for transfers between devices: 38.9 us -> 34.8 us
  starting transfers between devices: 58.1 us -> 60.1 us
    ppermute x7, waiting for transfers between devices: 22.8 us -> 18.4 us  [exchanged(): lax.ppermute(messages[k], 'ep', [(i, i ^ k) for i in range(experts)])]
    ppermute x7, starting transfers between devices: 8.06 us -> 10.7 us  [exchanged(): lax.ppermute(messages[k], 'ep', [(i, i ^ k) for i in range(experts)])]
  transfers between devices with their start and end apart: 24 -> 24, of which waited for: 7 -> 8; matrix products, arithmetic and copies ran while one was open for 1% -> 0% of each run, Pallas kernels for 23% -> 23%
where the time goes in v4:
time: 141 us
  starting transfers between devices  60.1 us (43%)
  Pallas kernels  37.3 us (26%)
  waiting for transfers between devices  34.8 us (25%)
  blocking collectives  7.51 us (5%)
    ppermute x16, starting transfers between devices, returned(): back[k] = lax.ppermute(messages[k], ('pp', 'ep'), pairs)  43.7 us
    pallas_call x2, Pallas kernels, expert_call(): pl.pallas_call(functools.partial(kernel, experts, len(after)), in_specs=[...  27.3 us
    ppermute x7, waiting for transfers between devices, exchanged(): lax.ppermute(messages[k], 'ep', [(i, i ^ k) for i in range(experts)])  18.4 us
    ppermute x16, waiting for transfers between devices, returned(): back[k] = lax.ppermute(messages[k], ('pp', 'ep'), pairs)  16.4 us
    ppermute x7, starting transfers between devices, exchanged(): lax.ppermute(messages[k], 'ep', [(i, i ^ k) for i in range(experts)])  10.7 us
    all_gather x1, blocking collectives, per_device_whole(): all_ids = lax.all_gather(jnp.concatenate([fwd_row, bwd_row], axis=0), 'pp')  7.51 us
    pallas_call x2, Pallas kernels, pack(): pl.pallas_call(functools.partial(pack_kernel, joined, count, experts), in...  6.91 us
    all_to_all x1, starting transfers between devices, per_device_whole(): lax.all_to_all(fwd_packed[0], 'ep', split_axis=0, concat_axis=0, tiled=True)  5.7 us
  transfers between devices with their start and end apart: 24, of which 8 were waited for; matrix products, arithmetic and copies ran while one was open for 0% of the time, Pallas kernels for 23%

profile of v4, /device:TPU:9, one launch (start us, length us, event | category | flops | bytes accessed | tf_op | source)
XLA Modules:
  0.0 140.6 jit_solution(3419359997513895168)
XLA Ops:
  0.7 3.0 %pack.2.refs_2_ = bf16[8,16,4480]{2,1,0:T(8,128)(2,1)} custom-call(s32[1,128]{1,0:T(1,128)} %bitcast.34, bf16[128,3584]{1,0:T(8,128)(2,1)} %bitcast.27), custom_call_target="tpu_custom_call" | custom-call | flops 234881024 | bytes 1835008 | tf_op jit(solution)/shard_map/pack/pallas_call | solution.py:505
  3.6 5.7 %all-to-all-start = ((bf16[8,16,4480]{2,1,0:T(8,128)(2,1)}), bf16[8,16,4480]{2,1,0:T(8,128)(2,1)S(1)}, u32[]{:S(2)}, u32[]{:S(2)}) async-start(bf16[8,16,4480]{2,1,0:T(8,128)(2,1)} %pack.2.refs_2_), calls=%async_computation | async-start | bytes 2293760 | tf_op jit(solution)/shard_map/all_to_all | solution.py:623
  9.4 3.9 %pack.3 = (bf16[32,4480]{1,0:T(8,128)(2,1)}, bf16[32,4480]{1,0:T(8,128)(2,1)}, bf16[32,4480]{1,0:T(8,128)(2,1)}, bf16[32,4480]{1,0:T(8,128)(2,1)}, bf16[32,4480]...) custom-call(s32[1,128]{1,0:T(1,128)} %bitcast.32, ...), custom_call_target="tpu_custom_call" | custom-call | flops 469762048 | bytes 3670016 | tf_op jit(solution)/shard_map/pack/pallas_call | solution.py:505
  16.0 2.1 %collective-permute-start.11 = (bf16[32,4480]{1,0:T(8,128)(2,1)}, bf16[32,4480]{1,0:T(8,128)(2,1)S(1)}, u32[]{:S(2)}, u32[]{:S(2)}) collective-permute-start(bf16[32,4480]{1,0:T(8,128)(2,1)} %get-tuple-element.38), channel_id=1, source_target_pairs={{0,4},{1,5},{2,6},{3,7},{4,0},{5,1},{6,2},{7,3},{8,12},{9,13},{10,... | collective-permute-start | bytes 860168 | tf_op jit(solution)/shard_map/ppermute | solution.py:598
  19.3 7.5 %all-gather.1 = s32[4,2,128]{2,1,0:T(2,128)S(1)} all-gather(s32[1,2,128]{2,1,0:T(2,128)S(1)} %add_bitcast_fusion), channel_id=2, replica_groups=mesh['pp'=4,'ep'=8] {'pp'}, dimensions={0}, use_global_device_ids=true | all-gather | bytes 5120 | tf_op jit(solution)/shard_map/all_gather | solution.py:624
  26.8 2.0 %collective-permute-start.13 = (bf16[32,4480]{1,0:T(8,128)(2,1)}, bf16[32,4480]{1,0:T(8,128)(2,1)S(1)}, u32[]{:S(2)}, u32[]{:S(2)}) collective-permute-start(bf16[32,4480]{1,0:T(8,128)(2,1)} %get-tuple-element.40), channel_id=1, source_target_pairs={{0,6},{1,7},{2,4},{3,5},{4,2},{5,3},{6,0},{7,1},{8,14},{9,15},{10,... | collective-permute-start | bytes 860168 | tf_op jit(solution)/shard_map/ppermute | solution.py:598
  28.8 5.7 %collective-permute-done.1.refs_5_ = bf16[32,4480]{1,0:T(8,128)(2,1)S(1)} collective-permute-done((bf16[32,4480]{1,0:T(8,128)(2,1)}, bf16[32,4480]{1,0:T(8,128)(2,1)S(1)}, u32[]{:S(2)}, u32[]{:S(2)}) %collective-permute-start.1) | collective-permute-done | bytes 286752 | tf_op jit(solution)/shard_map/ppermute | solution.py:598
  34.5 2.7 %collective-permute-start.14 = (bf16[32,4480]{1,0:T(8,128)(2,1)}, bf16[32,4480]{1,0:T(8,128)(2,1)S(1)}, u32[]{:S(2)}, u32[]{:S(2)}) collective-permute-start(bf16[32,4480]{1,0:T(8,128)(2,1)} %get-tuple-element.41), channel_id=1, source_target_pairs={{0,7},{1,6},{2,5},{3,4},{4,3},{5,2},{6,1},{7,0},{8,15},{9,14},{10,... | collective-permute-start | bytes 860168 | tf_op jit(solution)/shard_map/ppermute | solution.py:598
  37.3 9.4 %collective-permute-done.2.refs_6_ = bf16[32,4480]{1,0:T(8,128)(2,1)S(1)} collective-permute-done((bf16[32,4480]{1,0:T(8,128)(2,1)}, bf16[32,4480]{1,0:T(8,128)(2,1)S(1)}, u32[]{:S(2)}, u32[]{:S(2)}) %collective-permute-start.2) | collective-permute-done | bytes 286752 | tf_op jit(solution)/shard_map/ppermute | solution.py:598
  46.6 10.7 %forward.1 = (bf16[16,4480]{1,0:T(8,128)(2,1)S(1)}, bf16[16,4480]{1,0:T(8,128)(2,1)S(1)}, bf16[16,4480]{1,0:T(8,128)(2,1)S(1)}, bf16[16,4480]{1,0:T(8,128)(2,1)S...) custom-call(f32[8,3584]{1,0:T(8,128)S(1)} %bitcast.19, ...), custom_call_target="tpu_custom_call" | custom-call | flops 3523215360 | bytes 22020096 | tf_op jit(solution)/shard_map/forward/pallas_call | solution.py:570
  57.3 3.9 %collective-permute-start.3 = (bf16[16,4480]{1,0:T(8,128)(2,1)S(1)}, bf16[16,4480]{1,0:T(8,128)(2,1)S(1)}, u32[]{:S(2)}, u32[]{:S(2)}) collective-permute-start(bf16[16,4480]{1,0:T(8,128)(2,1)S(1)} %get-tuple-element.29), channel_id=1, source_target_pairs={{0,9},{1,8},{2,11},{3,10},{4,13},{5,12},{6,15},{7,14},{8,17},{9,16... | collective-permute-start | bytes 430088 | tf_op jit(solution)/shard_map/ppermute | solution.py:611
  61.2 10.1 %collective-permute-start.4 = (bf16[16,4480]{1,0:T(8,128)(2,1)S(1)}, bf16[16,4480]{1,0:T(8,128)(2,1)S(1)}, u32[]{:S(2)}, u32[]{:S(2)}) collective-permute-start(bf16[16,4480]{1,0:T(8,128)(2,1)S(1)} %get-tuple-element.30), channel_id=1, source_target_pairs={{0,10},{1,11},{2,8},{3,9},{4,14},{5,15},{6,12},{7,13},{8,18},{9,19... | collective-permute-start | bytes 430088 | tf_op jit(solution)/shard_map/ppermute | solution.py:611
  71.6 6.7 %collective-permute-start.5 = (bf16[16,4480]{1,0:T(8,128)(2,1)S(1)}, bf16[16,4480]{1,0:T(8,128)(2,1)S(1)}, u32[]{:S(2)}, u32[]{:S(2)}) collective-permute-start(bf16[16,4480]{1,0:T(8,128)(2,1)S(1)} %get-tuple-element.31), channel_id=1, source_target_pairs={{0,11},{1,10},{2,9},{3,8},{4,15},{5,14},{6,13},{7,12},{8,19},{9,18... | collective-permute-start | bytes 430088 | tf_op jit(solution)/shard_map/ppermute | solution.py:611
  78.3 4.3 %collective-permute-start.6 = (bf16[16,4480]{1,0:T(8,128)(2,1)S(1)}, bf16[16,4480]{1,0:T(8,128)(2,1)S(1)}, u32[]{:S(2)}, u32[]{:S(2)}) collective-permute-start(bf16[16,4480]{1,0:T(8,128)(2,1)S(1)} %get-tuple-element.32), channel_id=1, source_target_pairs={{0,8},{1,9},{2,10},{3,11},{4,12},{5,13},{6,14},{7,15},{8,16},{9,17... | collective-permute-start | bytes 430088 | tf_op jit(solution)/shard_map/ppermute | solution.py:611
  82.6 3.0 %collective-permute-done.14.refs_10_ = bf16[32,4480]{1,0:T(8,128)(2,1)S(1)} collective-permute-done((bf16[32,4480]{1,0:T(8,128)(2,1)}, bf16[32,4480]{1,0:T(8,128)(2,1)S(1)}, u32[]{:S(2)}, u32[]{:S(2)}) %collective-permute-start.14) | collective-permute-done | bytes 286752 | tf_op jit(solution)/shard_map/ppermute | solution.py:598
  85.7 3.4 %collective-permute-start.8 = (bf16[16,4480]{1,0:T(8,128)(2,1)S(1)}, bf16[16,4480]{1,0:T(8,128)(2,1)S(1)}, u32[]{:S(2)}, u32[]{:S(2)}) collective-permute-start(bf16[16,4480]{1,0:T(8,128)(2,1)S(1)} %get-tuple-element.34), channel_id=1, source_target_pairs={{0,13},{1,12},{2,15},{3,14},{4,9},{5,8},{6,11},{7,10},{8,21},{9,20... | collective-permute-start | bytes 430088 | tf_op jit(solution)/shard_map/ppermute | solution.py:611
  89.1 2.8 %collective-permute-start.9 = (bf16[16,4480]{1,0:T(8,128)(2,1)S(1)}, bf16[16,4480]{1,0:T(8,128)(2,1)S(1)}, u32[]{:S(2)}, u32[]{:S(2)}) collective-permute-start(bf16[16,4480]{1,0:T(8,128)(2,1)S(1)} %get-tuple-element.35), channel_id=1, source_target_pairs={{0,14},{1,15},{2,12},{3,13},{4,10},{5,11},{6,8},{7,9},{8,22},{9,23... | collective-permute-start | bytes 430088 | tf_op jit(solution)/shard_map/ppermute | solution.py:611
  92.1 16.6 %backward.1 = (bf16[16,4480]{1,0:T(8,128)(2,1)S(1)}, bf16[16,4480]{1,0:T(8,128)(2,1)S(1)}, bf16[16,4480]{1,0:T(8,128)(2,1)S(1)}, bf16[16,4480]{1,0:T(8,128)(2,1)...) custom-call(f32[8,3584]{1,0:T(8,128)S(1)} %bitcast.20, ...), custom_call_target="tpu_custom_call" | custom-call | flops 5872025600 | bytes 22020096 | tf_op jit(solution)/shard_map/backward/pallas_call | solution.py:570
  110.4 2.8 %collective-permute-start.16 = (bf16[16,4480]{1,0:T(8,128)(2,1)S(1)}, bf16[16,4480]{1,0:T(8,128)(2,1)S(1)}, u32[]{:S(2)}, u32[]{:S(2)}) collective-permute-start(bf16[16,4480]{1,0:T(8,128)(2,1)S(1)} %get-tuple-element.43), channel_id=1, source_target_pairs={{0,25},{1,24},{2,27},{3,26},{4,29},{5,28},{6,31},{7,30},{8,1},{9,0... | collective-permute-start | bytes 430088 | tf_op jit(solution)/shard_map/ppermute | solution.py:611
  116.7 2.3 %collective-permute-start.20 = (bf16[16,4480]{1,0:T(8,128)(2,1)S(1)}, bf16[16,4480]{1,0:T(8,128)(2,1)S(1)}, u32[]{:S(2)}, u32[]{:S(2)}) collective-permute-start(bf16[16,4480]{1,0:T(8,128)(2,1)S(1)} %get-tuple-element.47), channel_id=1, source_target_pairs={{0,30},{1,31},{2,28},{3,29},{4,26},{5,27},{6,24},{7,25},{8,6},{9,7... | collective-permute-start | bytes 430088 | tf_op jit(solution)/shard_map/ppermute | solution.py:611
  120.1 2.3 %collective-permute-done.17.refs_2_ = bf16[16,4480]{1,0:T(8,128)(2,1)S(1)} collective-permute-done((bf16[16,4480]{1,0:T(8,128)(2,1)S(1)}, bf16[16,4480]{1,0:T(8,128)(2,1)S(1)}, u32[]{:S(2)}, u32[]{:S(2)}) %collective-permute-start.17) | collective-permute-done | bytes 143392 | tf_op jit(solution)/shard_map/ppermute | solution.py:611
  124.9 6.9 %collective-permute-done.18.refs_3_ = bf16[16,4480]{1,0:T(8,128)(2,1)S(1)} collective-permute-done((bf16[16,4480]{1,0:T(8,128)(2,1)S(1)}, bf16[16,4480]{1,0:T(8,128)(2,1)S(1)}, u32[]{:S(2)}, u32[]{:S(2)}) %collective-permute-start.18) | collective-permute-done | bytes 143392 | tf_op jit(solution)/shard_map/ppermute | solution.py:611
  131.8 3.7 %collective-permute-done.20.refs_5_ = bf16[16,4480]{1,0:T(8,128)(2,1)S(1)} collective-permute-done((bf16[16,4480]{1,0:T(8,128)(2,1)S(1)}, bf16[16,4480]{1,0:T(8,128)(2,1)S(1)}, u32[]{:S(2)}, u32[]{:S(2)}) %collective-permute-start.20) | collective-permute-done | bytes 143392 | tf_op jit(solution)/shard_map/ppermute | solution.py:611
  135.5 3.4 %collective-permute-done.21.refs_6_ = bf16[16,4480]{1,0:T(8,128)(2,1)S(1)} collective-permute-done((bf16[16,4480]{1,0:T(8,128)(2,1)S(1)}, bf16[16,4480]{1,0:T(8,128)(2,1)S(1)}, u32[]{:S(2)}, u32[]{:S(2)}) %collective-permute-start.21) | collective-permute-done | bytes 143392 | tf_op jit(solution)/shard_map/ppermute | solution.py:611
  (42 shorter events, 14.8 us)
Async XLA Ops:
  3.6 43.0 %all-to-all-start = ((bf16[8,16,4480]{2,1,0:T(8,128)(2,1)}), bf16[8,16,4480]{2,1,0:T(8,128)(2,1)S(1)}, u32[]{:S(2)}, u32[]{:S(2)}) async-start(bf16[8,16,4480]{2,1,0:T(8,128)(2,1)} %pack.2.refs_2_), calls=%async_computation | async-start | bytes 2293760 | tf_op jit(solution)/shard_map/all_to_all | solution.py:623
  13.3 13.5 %collective-permute-start = (bf16[32,4480]{1,0:T(8,128)(2,1)}, bf16[32,4480]{1,0:T(8,128)(2,1)S(1)}, u32[]{:S(2)}, u32[]{:S(2)}) collective-permute-start(bf16[32,4480]{1,0:T(8,128)(2,1)} %get-tuple-element.26), channel_id=1, source_target_pairs={{0,1},{1,0},{2,3},{3,2},{4,5},{5,4},{6,7},{7,6},{8,9},{9,8},{10,11... | collective-permute-start | bytes 860168 | tf_op jit(solution)/shard_map/ppermute | solution.py:598
  14.5 20.0 %collective-permute-start.1 = (bf16[32,4480]{1,0:T(8,128)(2,1)}, bf16[32,4480]{1,0:T(8,128)(2,1)S(1)}, u32[]{:S(2)}, u32[]{:S(2)}) collective-permute-start(bf16[32,4480]{1,0:T(8,128)(2,1)} %get-tuple-element.27), channel_id=1, source_target_pairs={{0,2},{1,3},{2,0},{3,1},{4,6},{5,7},{6,4},{7,5},{8,10},{9,11},{10,... | collective-permute-start | bytes 860168 | tf_op jit(solution)/shard_map/ppermute | solution.py:598
  14.8 31.8 %collective-permute-start.2 = (bf16[32,4480]{1,0:T(8,128)(2,1)}, bf16[32,4480]{1,0:T(8,128)(2,1)S(1)}, u32[]{:S(2)}, u32[]{:S(2)}) collective-permute-start(bf16[32,4480]{1,0:T(8,128)(2,1)} %get-tuple-element.28), channel_id=1, source_target_pairs={{0,3},{1,2},{2,1},{3,0},{4,7},{5,6},{6,5},{7,4},{8,11},{9,10},{10,... | collective-permute-start | bytes 860168 | tf_op jit(solution)/shard_map/ppermute | solution.py:598
  16.0 45.2 %collective-permute-start.11 = (bf16[32,4480]{1,0:T(8,128)(2,1)}, bf16[32,4480]{1,0:T(8,128)(2,1)S(1)}, u32[]{:S(2)}, u32[]{:S(2)}) collective-permute-start(bf16[32,4480]{1,0:T(8,128)(2,1)} %get-tuple-element.38), channel_id=1, source_target_pairs={{0,4},{1,5},{2,6},{3,7},{4,0},{5,1},{6,2},{7,3},{8,12},{9,13},{10,... | collective-permute-start | bytes 860168 | tf_op jit(solution)/shard_map/ppermute | solution.py:598
  18.1 53.5 %collective-permute-start.12 = (bf16[32,4480]{1,0:T(8,128)(2,1)}, bf16[32,4480]{1,0:T(8,128)(2,1)S(1)}, u32[]{:S(2)}, u32[]{:S(2)}) collective-permute-start(bf16[32,4480]{1,0:T(8,128)(2,1)} %get-tuple-element.39), channel_id=1, source_target_pairs={{0,5},{1,4},{2,7},{3,6},{4,1},{5,0},{6,3},{7,2},{8,13},{9,12},{10,... | collective-permute-start | bytes 860168 | tf_op jit(solution)/shard_map/ppermute | solution.py:598
  26.8 51.5 %collective-permute-start.13 = (bf16[32,4480]{1,0:T(8,128)(2,1)}, bf16[32,4480]{1,0:T(8,128)(2,1)S(1)}, u32[]{:S(2)}, u32[]{:S(2)}) collective-permute-start(bf16[32,4480]{1,0:T(8,128)(2,1)} %get-tuple-element.40), channel_id=1, source_target_pairs={{0,6},{1,7},{2,4},{3,5},{4,2},{5,3},{6,0},{7,1},{8,14},{9,15},{10,... | collective-permute-start | bytes 860168 | tf_op jit(solution)/shard_map/ppermute | solution.py:598
  34.5 51.1 %collective-permute-start.14 = (bf16[32,4480]{1,0:T(8,128)(2,1)}, bf16[32,4480]{1,0:T(8,128)(2,1)S(1)}, u32[]{:S(2)}, u32[]{:S(2)}) collective-permute-start(bf16[32,4480]{1,0:T(8,128)(2,1)} %get-tuple-element.41), channel_id=1, source_target_pairs={{0,7},{1,6},{2,5},{3,4},{4,3},{5,2},{6,1},{7,0},{8,15},{9,14},{10,... | collective-permute-start | bytes 860168 | tf_op jit(solution)/shard_map/ppermute | solution.py:598
  57.3 28.4 %collective-permute-start.3 = (bf16[16,4480]{1,0:T(8,128)(2,1)S(1)}, bf16[16,4480]{1,0:T(8,128)(2,1)S(1)}, u32[]{:S(2)}, u32[]{:S(2)}) collective-permute-start(bf16[16,4480]{1,0:T(8,128)(2,1)S(1)} %get-tuple-element.29), channel_id=1, source_target_pairs={{0,9},{1,8},{2,11},{3,10},{4,13},{5,12},{6,15},{7,14},{8,17},{9,16... | collective-permute-start | bytes 430088 | tf_op jit(solution)/shard_map/ppermute | solution.py:611
  61.2 27.9 %collective-permute-start.4 = (bf16[16,4480]{1,0:T(8,128)(2,1)S(1)}, bf16[16,4480]{1,0:T(8,128)(2,1)S(1)}, u32[]{:S(2)}, u32[]{:S(2)}) collective-permute-start(bf16[16,4480]{1,0:T(8,128)(2,1)S(1)} %get-tuple-element.30), channel_id=1, source_target_pairs={{0,10},{1,11},{2,8},{3,9},{4,14},{5,15},{6,12},{7,13},{8,18},{9,19... | collective-permute-start | bytes 430088 | tf_op jit(solution)/shard_map/ppermute | solution.py:611
  71.6 20.3 %collective-permute-start.5 = (bf16[16,4480]{1,0:T(8,128)(2,1)S(1)}, bf16[16,4480]{1,0:T(8,128)(2,1)S(1)}, u32[]{:S(2)}, u32[]{:S(2)}) collective-permute-start(bf16[16,4480]{1,0:T(8,128)(2,1)S(1)} %get-tuple-element.31), channel_id=1, source_target_pairs={{0,11},{1,10},{2,9},{3,8},{4,15},{5,14},{6,13},{7,12},{8,19},{9,18... | collective-permute-start | bytes 430088 | tf_op jit(solution)/shard_map/ppermute | solution.py:611
  78.3 13.8 %collective-permute-start.6 = (bf16[16,4480]{1,0:T(8,128)(2,1)S(1)}, bf16[16,4480]{1,0:T(8,128)(2,1)S(1)}, u32[]{:S(2)}, u32[]{:S(2)}) collective-permute-start(bf16[16,4480]{1,0:T(8,128)(2,1)S(1)} %get-tuple-element.32), channel_id=1, source_target_pairs={{0,8},{1,9},{2,10},{3,11},{4,12},{5,13},{6,14},{7,15},{8,16},{9,17... | collective-permute-start | bytes 430088 | tf_op jit(solution)/shard_map/ppermute | solution.py:611
  85.7 24.7 %collective-permute-start.7 = (bf16[16,4480]{1,0:T(8,128)(2,1)S(1)}, bf16[16,4480]{1,0:T(8,128)(2,1)S(1)}, u32[]{:S(2)}, u32[]{:S(2)}) collective-permute-start(bf16[16,4480]{1,0:T(8,128)(2,1)S(1)} %get-tuple-element.33), channel_id=1, source_target_pairs={{0,12},{1,13},{2,14},{3,15},{4,8},{5,9},{6,10},{7,11},{8,20},{9,21... | collective-permute-start | bytes 430088 | tf_op jit(solution)/shard_map/ppermute | solution.py:611
  85.7 27.5 %collective-permute-start.8 = (bf16[16,4480]{1,0:T(8,128)(2,1)S(1)}, bf16[16,4480]{1,0:T(8,128)(2,1)S(1)}, u32[]{:S(2)}, u32[]{:S(2)}) collective-permute-start(bf16[16,4480]{1,0:T(8,128)(2,1)S(1)} %get-tuple-element.34), channel_id=1, source_target_pairs={{0,13},{1,12},{2,15},{3,14},{4,9},{5,8},{6,11},{7,10},{8,21},{9,20... | collective-permute-start | bytes 430088 | tf_op jit(solution)/shard_map/ppermute | solution.py:611
  89.1 24.7 %collective-permute-start.9 = (bf16[16,4480]{1,0:T(8,128)(2,1)S(1)}, bf16[16,4480]{1,0:T(8,128)(2,1)S(1)}, u32[]{:S(2)}, u32[]{:S(2)}) collective-permute-start(bf16[16,4480]{1,0:T(8,128)(2,1)S(1)} %get-tuple-element.35), channel_id=1, source_target_pairs={{0,14},{1,15},{2,12},{3,13},{4,10},{5,11},{6,8},{7,9},{8,22},{9,23... | collective-permute-start | bytes 430088 | tf_op jit(solution)/shard_map/ppermute | solution.py:611
  91.9 23.7 %collective-permute-start.10 = (bf16[16,4480]{1,0:T(8,128)(2,1)S(1)}, bf16[16,4480]{1,0:T(8,128)(2,1)S(1)}, u32[]{:S(2)}, u32[]{:S(2)}) collective-permute-start(bf16[16,4480]{1,0:T(8,128)(2,1)S(1)} %get-tuple-element.36), channel_id=1, source_target_pairs={{0,15},{1,14},{2,13},{3,12},{4,11},{5,10},{6,9},{7,8},{8,23},{9,22... | collective-permute-start | bytes 430088 | tf_op jit(solution)/shard_map/ppermute | solution.py:611
  108.7 7.9 %collective-permute-start.15 = (bf16[16,4480]{1,0:T(8,128)(2,1)S(1)}, bf16[16,4480]{1,0:T(8,128)(2,1)S(1)}, u32[]{:S(2)}, u32[]{:S(2)}) collective-permute-start(bf16[16,4480]{1,0:T(8,128)(2,1)S(1)} %get-tuple-element.42), channel_id=1, source_target_pairs={{0,28},{1,29},{2,30},{3,31},{4,24},{5,25},{6,26},{7,27},{8,4},{9,5... | collective-permute-start | bytes 430088 | tf_op jit(solution)/shard_map/ppermute | solution.py:611
  110.4 8.5 %collective-permute-start.16 = (bf16[16,4480]{1,0:T(8,128)(2,1)S(1)}, bf16[16,4480]{1,0:T(8,128)(2,1)S(1)}, u32[]{:S(2)}, u32[]{:S(2)}) collective-permute-start(bf16[16,4480]{1,0:T(8,128)(2,1)S(1)} %get-tuple-element.43), channel_id=1, source_target_pairs={{0,25},{1,24},{2,27},{3,26},{4,29},{5,28},{6,31},{7,30},{8,1},{9,0... | collective-permute-start | bytes 430088 | tf_op jit(solution)/shard_map/ppermute | solution.py:611
  113.2 9.3 %collective-permute-start.17 = (bf16[16,4480]{1,0:T(8,128)(2,1)S(1)}, bf16[16,4480]{1,0:T(8,128)(2,1)S(1)}, u32[]{:S(2)}, u32[]{:S(2)}) collective-permute-start(bf16[16,4480]{1,0:T(8,128)(2,1)S(1)} %get-tuple-element.44), channel_id=1, source_target_pairs={{0,26},{1,27},{2,24},{3,25},{4,30},{5,31},{6,28},{7,29},{8,2},{9,3... | collective-permute-start | bytes 430088 | tf_op jit(solution)/shard_map/ppermute | solution.py:611
  113.8 18.0 %collective-permute-start.18 = (bf16[16,4480]{1,0:T(8,128)(2,1)S(1)}, bf16[16,4480]{1,0:T(8,128)(2,1)S(1)}, u32[]{:S(2)}, u32[]{:S(2)}) collective-permute-start(bf16[16,4480]{1,0:T(8,128)(2,1)S(1)} %get-tuple-element.45), channel_id=1, source_target_pairs={{0,27},{1,26},{2,25},{3,24},{4,31},{5,30},{6,29},{7,28},{8,3},{9,2... | collective-permute-start | bytes 430088 | tf_op jit(solution)/shard_map/ppermute | solution.py:611
  115.6 16.2 %collective-permute-start.19 = (bf16[16,4480]{1,0:T(8,128)(2,1)S(1)}, bf16[16,4480]{1,0:T(8,128)(2,1)S(1)}, u32[]{:S(2)}, u32[]{:S(2)}) collective-permute-start(bf16[16,4480]{1,0:T(8,128)(2,1)S(1)} %get-tuple-element.46), channel_id=1, source_target_pairs={{0,29},{1,28},{2,31},{3,30},{4,25},{5,24},{6,27},{7,26},{8,5},{9,4... | collective-permute-start | bytes 430088 | tf_op jit(solution)/shard_map/ppermute | solution.py:611
  116.7 18.8 %collective-permute-start.20 = (bf16[16,4480]{1,0:T(8,128)(2,1)S(1)}, bf16[16,4480]{1,0:T(8,128)(2,1)S(1)}, u32[]{:S(2)}, u32[]{:S(2)}) collective-permute-start(bf16[16,4480]{1,0:T(8,128)(2,1)S(1)} %get-tuple-element.47), channel_id=1, source_target_pairs={{0,30},{1,31},{2,28},{3,29},{4,26},{5,27},{6,24},{7,25},{8,6},{9,7... | collective-permute-start | bytes 430088 | tf_op jit(solution)/shard_map/ppermute | solution.py:611
  119.0 19.9 %collective-permute-start.21 = (bf16[16,4480]{1,0:T(8,128)(2,1)S(1)}, bf16[16,4480]{1,0:T(8,128)(2,1)S(1)}, u32[]{:S(2)}, u32[]{:S(2)}) collective-permute-start(bf16[16,4480]{1,0:T(8,128)(2,1)S(1)} %get-tuple-element.48), channel_id=1, source_target_pairs={{0,31},{1,30},{2,29},{3,28},{4,27},{5,26},{6,25},{7,24},{8,7},{9,6... | collective-permute-start | bytes 430088 | tf_op jit(solution)/shard_map/ppermute | solution.py:611
  122.4 16.4 %collective-permute-start.22 = (bf16[16,4480]{1,0:T(8,128)(2,1)S(1)}, bf16[16,4480]{1,0:T(8,128)(2,1)S(1)}, u32[]{:S(2)}, u32[]{:S(2)}) collective-permute-start(bf16[16,4480]{1,0:T(8,128)(2,1)S(1)} %get-tuple-element.49), channel_id=1, source_target_pairs={{0,24},{1,25},{2,26},{3,27},{4,28},{5,29},{6,30},{7,31},{8,0},{9,1... | collective-permute-start | bytes 430088 | tf_op jit(solution)/shard_map/ppermute | solution.py:611
  (4 other events, 128.7 us)

commit v5 on v4

--- a/solution.py
+++ b/solution.py
@@ -629,7 +629,7 @@
     bwd_packed = pack(bwd_row, [saved_in[0], grad_in[0]], experts, False, after)
     order = [0, *near, *far]
     bwd_rows = exchanged(bwd_packed, order[1:])
-    after = [bwd_rows[k] for k in near] + [fwd_row_next, bwd_row_next]
+    after = [bwd_rows[k] for k in near[:1]] + [fwd_row_next, bwd_row_next]
     fwd_out = expert_call(
         forward_kernel, "forward", router_rows, *weights, [fwd_rows], experts, 3, after
     )
@@ -640,7 +640,7 @@
     )
     bwd_back = returned(bwd_out, range(experts), -1)
     fwd_next = unpack(fwd_row_next, fwd_back, near + [0] + far)
-    grad_next = unpack(bwd_row_next, bwd_back, far[:1] + near + far[1:] + [0])
+    grad_next = unpack(bwd_row_next, bwd_back, far[:1] + near + far[1:2] + [0] + far[2:])
     return (fwd_next[None], grad_next[None])
 
 

time: 141 us -> 141 us (level)
  waiting for transfers between devices: 34.8 us -> 26.8 us
  starting transfers between devices: 60.1 us -> 66.6 us
  local copies, waits for them, and re-layouts: 0.03 us -> 3.11 us
  Pallas kernels: 37.3 us -> 35.6 us
    ppermute x7, waiting for transfers between devices: 18.4 us -> 8.99 us  [exchanged(): lax.ppermute(messages[k], 'ep', [(i, i ^ k) for i in range(experts)])]
    ppermute x16, starting transfers between devices: 43.7 us -> 50.2 us  [returned(): back[k] = lax.ppermute(messages[k], ('pp', 'ep'), pairs)]
    unnamed x8 -> x10, local copies, waits for them, and re-layouts: 0.02 us -> 3.1 us
    pallas_call x2, Pallas kernels: 27.3 us -> 25.6 us  [expert_call(): pl.pallas_call(functools.partial(kernel, experts, len(after)), in_specs=[...]
    ppermute x16, waiting for transfers between devices: 16.4 us -> 17.8 us  [returned(): back[k] = lax.ppermute(messages[k], ('pp', 'ep'), pairs)]
  transfers between devices with their start and end apart: 24 -> 24, of which waited for: 8 -> 7; matrix products, arithmetic and copies ran while one was open for 0% -> 0% of each run, Pallas kernels for 23% -> 22%
where the time goes in v5:
time: 141 us
  starting transfers between devices  66.6 us (47%)
  Pallas kernels  35.6 us (25%)
  waiting for transfers between devices  26.8 us (19%)
  blocking collectives  7.52 us (5%)
  local copies, waits for them, and re-layouts  3.11 us (2%)
    ppermute x16, starting transfers between devices, returned(): back[k] = lax.ppermute(messages[k], ('pp', 'ep'), pairs)  50.2 us
    pallas_call x2, Pallas kernels, expert_call(): pl.pallas_call(functools.partial(kernel, experts, len(after)), in_specs=[...  25.6 us
    ppermute x16, waiting for transfers between devices, returned(): back[k] = lax.ppermute(messages[k], ('pp', 'ep'), pairs)  17.8 us
    ppermute x7, starting transfers between devices, exchanged(): lax.ppermute(messages[k], 'ep', [(i, i ^ k) for i in range(experts)])  10.7 us
    ppermute x7, waiting for transfers between devices, exchanged(): lax.ppermute(messages[k], 'ep', [(i, i ^ k) for i in range(experts)])  8.99 us
    all_gather x1, blocking collectives, per_device_whole(): all_ids = lax.all_gather(jnp.concatenate([fwd_row, bwd_row], axis=0), 'pp')  7.52 us
    pallas_call x2, Pallas kernels, pack(): pl.pallas_call(functools.partial(pack_kernel, joined, count, experts), in...  6.93 us
    all_to_all x1, starting transfers between devices, per_device_whole(): lax.all_to_all(fwd_packed[0], 'ep', split_axis=0, concat_axis=0, tiled=True)  5.7 us
  transfers between devices with their start and end apart: 24, of which 7 were waited for; matrix products, arithmetic and copies ran while one was open for 0% of the time, Pallas kernels for 22%

profile of v5, /device:TPU:9, one launch (start us, length us, event | category | flops | bytes accessed | tf_op | source)
XLA Modules:
  0.0 140.5 jit_solution(1825664210622671851)
XLA Ops:
  0.7 3.0 %pack.2.refs_2_ = bf16[8,16,4480]{2,1,0:T(8,128)(2,1)} custom-call(s32[1,128]{1,0:T(1,128)} %bitcast.34, bf16[128,3584]{1,0:T(8,128)(2,1)} %bitcast.27), custom_call_target="tpu_custom_call" | custom-call | flops 234881024 | bytes 1835008 | tf_op jit(solution)/shard_map/pack/pallas_call | solution.py:505
  3.6 5.7 %all-to-all-start = ((bf16[8,16,4480]{2,1,0:T(8,128)(2,1)}), bf16[8,16,4480]{2,1,0:T(8,128)(2,1)S(1)}, u32[]{:S(2)}, u32[]{:S(2)}) async-start(bf16[8,16,4480]{2,1,0:T(8,128)(2,1)} %pack.2.refs_2_), calls=%async_computation | async-start | bytes 2293760 | tf_op jit(solution)/shard_map/all_to_all | solution.py:623
  9.3 4.0 %pack.3 = (bf16[32,4480]{1,0:T(8,128)(2,1)}, bf16[32,4480]{1,0:T(8,128)(2,1)}, bf16[32,4480]{1,0:T(8,128)(2,1)}, bf16[32,4480]{1,0:T(8,128)(2,1)}, bf16[32,4480]...) custom-call(s32[1,128]{1,0:T(1,128)} %bitcast.32, ...), custom_call_target="tpu_custom_call" | custom-call | flops 469762048 | bytes 3670016 | tf_op jit(solution)/shard_map/pack/pallas_call | solution.py:505
  16.0 2.1 %collective-permute-start.11 = (bf16[32,4480]{1,0:T(8,128)(2,1)}, bf16[32,4480]{1,0:T(8,128)(2,1)S(1)}, u32[]{:S(2)}, u32[]{:S(2)}) collective-permute-start(bf16[32,4480]{1,0:T(8,128)(2,1)} %get-tuple-element.38), channel_id=1, source_target_pairs={{0,4},{1,5},{2,6},{3,7},{4,0},{5,1},{6,2},{7,3},{8,12},{9,13},{10,... | collective-permute-start | bytes 860168 | tf_op jit(solution)/shard_map/ppermute | solution.py:598
  19.3 7.5 %all-gather.1 = s32[4,2,128]{2,1,0:T(2,128)S(1)} all-gather(s32[1,2,128]{2,1,0:T(2,128)S(1)} %add_bitcast_fusion), channel_id=2, replica_groups=mesh['pp'=4,'ep'=8] {'pp'}, dimensions={0}, use_global_device_ids=true | all-gather | bytes 5120 | tf_op jit(solution)/shard_map/all_gather | solution.py:624
  26.8 2.0 %collective-permute-start.13 = (bf16[32,4480]{1,0:T(8,128)(2,1)}, bf16[32,4480]{1,0:T(8,128)(2,1)S(1)}, u32[]{:S(2)}, u32[]{:S(2)}) collective-permute-start(bf16[32,4480]{1,0:T(8,128)(2,1)} %get-tuple-element.40), channel_id=1, source_target_pairs={{0,6},{1,7},{2,4},{3,5},{4,2},{5,3},{6,0},{7,1},{8,14},{9,15},{10,... | collective-permute-start | bytes 860168 | tf_op jit(solution)/shard_map/ppermute | solution.py:598
  28.8 5.7 %collective-permute-done.9.refs_5_ = bf16[32,4480]{1,0:T(8,128)(2,1)S(1)} collective-permute-done((bf16[32,4480]{1,0:T(8,128)(2,1)}, bf16[32,4480]{1,0:T(8,128)(2,1)S(1)}, u32[]{:S(2)}, u32[]{:S(2)}) %collective-permute-start.9) | collective-permute-done | bytes 286752 | tf_op jit(solution)/shard_map/ppermute | solution.py:598
  34.5 2.7 %collective-permute-start.14 = (bf16[32,4480]{1,0:T(8,128)(2,1)}, bf16[32,4480]{1,0:T(8,128)(2,1)S(1)}, u32[]{:S(2)}, u32[]{:S(2)}) collective-permute-start(bf16[32,4480]{1,0:T(8,128)(2,1)} %get-tuple-element.41), channel_id=1, source_target_pairs={{0,7},{1,6},{2,5},{3,4},{4,3},{5,2},{6,1},{7,0},{8,15},{9,14},{10,... | collective-permute-start | bytes 860168 | tf_op jit(solution)/shard_map/ppermute | solution.py:598
  37.3 3.1 %copy-done = bf16[1,3584,1024]{2,1,0:T(8,128)(2,1)S(1)} copy-done((bf16[1,3584,1024]{2,1,0:T(8,128)(2,1)S(1)}, bf16[1,3584,1024]{2,1,0:T(8,128)(2,1)}, u32[]{:S(2)}) %copy-start) | copy-done | bytes 7340056
  40.4 9.0 %forward.1 = (bf16[16,4480]{1,0:T(8,128)(2,1)S(1)}, bf16[16,4480]{1,0:T(8,128)(2,1)S(1)}, bf16[16,4480]{1,0:T(8,128)(2,1)S(1)}, bf16[16,4480]{1,0:T(8,128)(2,1)S...) custom-call(f32[8,3584]{1,0:T(8,128)S(1)} %bitcast.21, ...), custom_call_target="tpu_custom_call" | custom-call | flops 3523215360 | bytes 22020096 | tf_op jit(solution)/shard_map/forward/pallas_call | solution.py:570
  49.4 4.7 %collective-permute-start.1 = (bf16[16,4480]{1,0:T(8,128)(2,1)S(1)}, bf16[16,4480]{1,0:T(8,128)(2,1)S(1)}, u32[]{:S(2)}, u32[]{:S(2)}) collective-permute-start(bf16[16,4480]{1,0:T(8,128)(2,1)S(1)} %get-tuple-element.27), channel_id=1, source_target_pairs={{0,9},{1,8},{2,11},{3,10},{4,13},{5,12},{6,15},{7,14},{8,17},{9,16... | collective-permute-start | bytes 430088 | tf_op jit(solution)/shard_map/ppermute | solution.py:611
  54.1 17.2 %collective-permute-start.2 = (bf16[16,4480]{1,0:T(8,128)(2,1)S(1)}, bf16[16,4480]{1,0:T(8,128)(2,1)S(1)}, u32[]{:S(2)}, u32[]{:S(2)}) collective-permute-start(bf16[16,4480]{1,0:T(8,128)(2,1)S(1)} %get-tuple-element.28), channel_id=1, source_target_pairs={{0,10},{1,11},{2,8},{3,9},{4,14},{5,15},{6,12},{7,13},{8,18},{9,19... | collective-permute-start | bytes 430088 | tf_op jit(solution)/shard_map/ppermute | solution.py:611
  71.6 6.7 %collective-permute-start.3 = (bf16[16,4480]{1,0:T(8,128)(2,1)S(1)}, bf16[16,4480]{1,0:T(8,128)(2,1)S(1)}, u32[]{:S(2)}, u32[]{:S(2)}) collective-permute-start(bf16[16,4480]{1,0:T(8,128)(2,1)S(1)} %get-tuple-element.29), channel_id=1, source_target_pairs={{0,11},{1,10},{2,9},{3,8},{4,15},{5,14},{6,13},{7,12},{8,19},{9,18... | collective-permute-start | bytes 430088 | tf_op jit(solution)/shard_map/ppermute | solution.py:611
  78.3 4.3 %collective-permute-start.4 = (bf16[16,4480]{1,0:T(8,128)(2,1)S(1)}, bf16[16,4480]{1,0:T(8,128)(2,1)S(1)}, u32[]{:S(2)}, u32[]{:S(2)}) collective-permute-start(bf16[16,4480]{1,0:T(8,128)(2,1)S(1)} %get-tuple-element.30), channel_id=1, source_target_pairs={{0,8},{1,9},{2,10},{3,11},{4,12},{5,13},{6,14},{7,15},{8,16},{9,17... | collective-permute-start | bytes 430088 | tf_op jit(solution)/shard_map/ppermute | solution.py:611
  82.6 3.0 %collective-permute-done.14.refs_10_ = bf16[32,4480]{1,0:T(8,128)(2,1)S(1)} collective-permute-done((bf16[32,4480]{1,0:T(8,128)(2,1)}, bf16[32,4480]{1,0:T(8,128)(2,1)S(1)}, u32[]{:S(2)}, u32[]{:S(2)}) %collective-permute-start.14) | collective-permute-done | bytes 286752 | tf_op jit(solution)/shard_map/ppermute | solution.py:598
  85.6 3.5 %collective-permute-start.6 = (bf16[16,4480]{1,0:T(8,128)(2,1)S(1)}, bf16[16,4480]{1,0:T(8,128)(2,1)S(1)}, u32[]{:S(2)}, u32[]{:S(2)}) collective-permute-start(bf16[16,4480]{1,0:T(8,128)(2,1)S(1)} %get-tuple-element.32), channel_id=1, source_target_pairs={{0,13},{1,12},{2,15},{3,14},{4,9},{5,8},{6,11},{7,10},{8,21},{9,20... | collective-permute-start | bytes 430088 | tf_op jit(solution)/shard_map/ppermute | solution.py:611
  89.1 2.7 %collective-permute-start.7 = (bf16[16,4480]{1,0:T(8,128)(2,1)S(1)}, bf16[16,4480]{1,0:T(8,128)(2,1)S(1)}, u32[]{:S(2)}, u32[]{:S(2)}) collective-permute-start(bf16[16,4480]{1,0:T(8,128)(2,1)S(1)} %get-tuple-element.33), channel_id=1, source_target_pairs={{0,14},{1,15},{2,12},{3,13},{4,10},{5,11},{6,8},{7,9},{8,22},{9,23... | collective-permute-start | bytes 430088 | tf_op jit(solution)/shard_map/ppermute | solution.py:611
  92.0 16.6 %backward.1 = (bf16[16,4480]{1,0:T(8,128)(2,1)S(1)}, bf16[16,4480]{1,0:T(8,128)(2,1)S(1)}, bf16[16,4480]{1,0:T(8,128)(2,1)S(1)}, bf16[16,4480]{1,0:T(8,128)(2,1)...) custom-call(f32[8,3584]{1,0:T(8,128)S(1)} %bitcast.22, ...), custom_call_target="tpu_custom_call" | custom-call | flops 5872025600 | bytes 22020096 | tf_op jit(solution)/shard_map/backward/pallas_call | solution.py:570
  110.4 2.8 %collective-permute-start.16 = (bf16[16,4480]{1,0:T(8,128)(2,1)S(1)}, bf16[16,4480]{1,0:T(8,128)(2,1)S(1)}, u32[]{:S(2)}, u32[]{:S(2)}) collective-permute-start(bf16[16,4480]{1,0:T(8,128)(2,1)S(1)} %get-tuple-element.43), channel_id=1, source_target_pairs={{0,25},{1,24},{2,27},{3,26},{4,29},{5,28},{6,31},{7,30},{8,1},{9,0... | collective-permute-start | bytes 430088 | tf_op jit(solution)/shard_map/ppermute | solution.py:611
  113.8 1.7 %collective-permute-start.18 = (bf16[16,4480]{1,0:T(8,128)(2,1)S(1)}, bf16[16,4480]{1,0:T(8,128)(2,1)S(1)}, u32[]{:S(2)}, u32[]{:S(2)}) collective-permute-start(bf16[16,4480]{1,0:T(8,128)(2,1)S(1)} %get-tuple-element.45), channel_id=1, source_target_pairs={{0,27},{1,26},{2,25},{3,24},{4,31},{5,30},{6,29},{7,28},{8,3},{9,2... | collective-permute-start | bytes 430088 | tf_op jit(solution)/shard_map/ppermute | solution.py:611
  119.2 3.3 %collective-permute-done.17.refs_2_ = bf16[16,4480]{1,0:T(8,128)(2,1)S(1)} collective-permute-done((bf16[16,4480]{1,0:T(8,128)(2,1)S(1)}, bf16[16,4480]{1,0:T(8,128)(2,1)S(1)}, u32[]{:S(2)}, u32[]{:S(2)}) %collective-permute-start.17) | collective-permute-done | bytes 143392 | tf_op jit(solution)/shard_map/ppermute | solution.py:611
  124.3 7.5 %collective-permute-done.18.refs_3_ = bf16[16,4480]{1,0:T(8,128)(2,1)S(1)} collective-permute-done((bf16[16,4480]{1,0:T(8,128)(2,1)S(1)}, bf16[16,4480]{1,0:T(8,128)(2,1)S(1)}, u32[]{:S(2)}, u32[]{:S(2)}) %collective-permute-start.18) | collective-permute-done | bytes 143392 | tf_op jit(solution)/shard_map/ppermute | solution.py:611
  131.8 3.8 %collective-permute-done.21.refs_6_ = bf16[16,4480]{1,0:T(8,128)(2,1)S(1)} collective-permute-done((bf16[16,4480]{1,0:T(8,128)(2,1)S(1)}, bf16[16,4480]{1,0:T(8,128)(2,1)S(1)}, u32[]{:S(2)}, u32[]{:S(2)}) %collective-permute-start.21) | collective-permute-done | bytes 143392 | tf_op jit(solution)/shard_map/ppermute | solution.py:611
  135.6 3.3 %collective-permute-done.22.refs_7_ = bf16[16,4480]{1,0:T(8,128)(2,1)S(1)} collective-permute-done((bf16[16,4480]{1,0:T(8,128)(2,1)S(1)}, bf16[16,4480]{1,0:T(8,128)(2,1)S(1)}, u32[]{:S(2)}, u32[]{:S(2)}) %collective-permute-start.22) | collective-permute-done | bytes 143392 | tf_op jit(solution)/shard_map/ppermute | solution.py:611
  (44 shorter events, 13.8 us)
Async XLA Ops:
  3.6 33.6 %all-to-all-start = ((bf16[8,16,4480]{2,1,0:T(8,128)(2,1)}), bf16[8,16,4480]{2,1,0:T(8,128)(2,1)S(1)}, u32[]{:S(2)}, u32[]{:S(2)}) async-start(bf16[8,16,4480]{2,1,0:T(8,128)(2,1)} %pack.2.refs_2_), calls=%async_computation | async-start | bytes 2293760 | tf_op jit(solution)/shard_map/all_to_all | solution.py:623
  13.3 13.5 %collective-permute-start = (bf16[32,4480]{1,0:T(8,128)(2,1)}, bf16[32,4480]{1,0:T(8,128)(2,1)S(1)}, u32[]{:S(2)}, u32[]{:S(2)}) collective-permute-start(bf16[32,4480]{1,0:T(8,128)(2,1)} %get-tuple-element.26), channel_id=1, source_target_pairs={{0,1},{1,0},{2,3},{3,2},{4,5},{5,4},{6,7},{7,6},{8,9},{9,8},{10,11... | collective-permute-start | bytes 860168 | tf_op jit(solution)/shard_map/ppermute | solution.py:598
  14.5 20.0 %collective-permute-start.9 = (bf16[32,4480]{1,0:T(8,128)(2,1)}, bf16[32,4480]{1,0:T(8,128)(2,1)S(1)}, u32[]{:S(2)}, u32[]{:S(2)}) collective-permute-start(bf16[32,4480]{1,0:T(8,128)(2,1)} %get-tuple-element.36), channel_id=1, source_target_pairs={{0,2},{1,3},{2,0},{3,1},{4,6},{5,7},{6,4},{7,5},{8,10},{9,11},{10,... | collective-permute-start | bytes 860168 | tf_op jit(solution)/shard_map/ppermute | solution.py:598
  14.8 34.5 %collective-permute-start.10 = (bf16[32,4480]{1,0:T(8,128)(2,1)}, bf16[32,4480]{1,0:T(8,128)(2,1)S(1)}, u32[]{:S(2)}, u32[]{:S(2)}) collective-permute-start(bf16[32,4480]{1,0:T(8,128)(2,1)} %get-tuple-element.37), channel_id=1, source_target_pairs={{0,3},{1,2},{2,1},{3,0},{4,7},{5,6},{6,5},{7,4},{8,11},{9,10},{10,... | collective-permute-start | bytes 860168 | tf_op jit(solution)/shard_map/ppermute | solution.py:598
  16.0 38.0 %collective-permute-start.11 = (bf16[32,4480]{1,0:T(8,128)(2,1)}, bf16[32,4480]{1,0:T(8,128)(2,1)S(1)}, u32[]{:S(2)}, u32[]{:S(2)}) collective-permute-start(bf16[32,4480]{1,0:T(8,128)(2,1)} %get-tuple-element.38), channel_id=1, source_target_pairs={{0,4},{1,5},{2,6},{3,7},{4,0},{5,1},{6,2},{7,3},{8,12},{9,13},{10,... | collective-permute-start | bytes 860168 | tf_op jit(solution)/shard_map/ppermute | solution.py:598
  18.1 53.5 %collective-permute-start.12 = (bf16[32,4480]{1,0:T(8,128)(2,1)}, bf16[32,4480]{1,0:T(8,128)(2,1)S(1)}, u32[]{:S(2)}, u32[]{:S(2)}) collective-permute-start(bf16[32,4480]{1,0:T(8,128)(2,1)} %get-tuple-element.39), channel_id=1, source_target_pairs={{0,5},{1,4},{2,7},{3,6},{4,1},{5,0},{6,3},{7,2},{8,13},{9,12},{10,... | collective-permute-start | bytes 860168 | tf_op jit(solution)/shard_map/ppermute | solution.py:598
  26.8 51.5 %collective-permute-start.13 = (bf16[32,4480]{1,0:T(8,128)(2,1)}, bf16[32,4480]{1,0:T(8,128)(2,1)S(1)}, u32[]{:S(2)}, u32[]{:S(2)}) collective-permute-start(bf16[32,4480]{1,0:T(8,128)(2,1)} %get-tuple-element.40), channel_id=1, source_target_pairs={{0,6},{1,7},{2,4},{3,5},{4,2},{5,3},{6,0},{7,1},{8,14},{9,15},{10,... | collective-permute-start | bytes 860168 | tf_op jit(solution)/shard_map/ppermute | solution.py:598
  34.5 51.1 %collective-permute-start.14 = (bf16[32,4480]{1,0:T(8,128)(2,1)}, bf16[32,4480]{1,0:T(8,128)(2,1)S(1)}, u32[]{:S(2)}, u32[]{:S(2)}) collective-permute-start(bf16[32,4480]{1,0:T(8,128)(2,1)} %get-tuple-element.41), channel_id=1, source_target_pairs={{0,7},{1,6},{2,5},{3,4},{4,3},{5,2},{6,1},{7,0},{8,15},{9,14},{10,... | collective-permute-start | bytes 860168 | tf_op jit(solution)/shard_map/ppermute | solution.py:598
  49.4 36.3 %collective-permute-start.1 = (bf16[16,4480]{1,0:T(8,128)(2,1)S(1)}, bf16[16,4480]{1,0:T(8,128)(2,1)S(1)}, u32[]{:S(2)}, u32[]{:S(2)}) collective-permute-start(bf16[16,4480]{1,0:T(8,128)(2,1)S(1)} %get-tuple-element.27), channel_id=1, source_target_pairs={{0,9},{1,8},{2,11},{3,10},{4,13},{5,12},{6,15},{7,14},{8,17},{9,16... | collective-permute-start | bytes 430088 | tf_op jit(solution)/shard_map/ppermute | solution.py:611
  54.1 35.0 %collective-permute-start.2 = (bf16[16,4480]{1,0:T(8,128)(2,1)S(1)}, bf16[16,4480]{1,0:T(8,128)(2,1)S(1)}, u32[]{:S(2)}, u32[]{:S(2)}) collective-permute-start(bf16[16,4480]{1,0:T(8,128)(2,1)S(1)} %get-tuple-element.28), channel_id=1, source_target_pairs={{0,10},{1,11},{2,8},{3,9},{4,14},{5,15},{6,12},{7,13},{8,18},{9,19... | collective-permute-start | bytes 430088 | tf_op jit(solution)/shard_map/ppermute | solution.py:611
  71.6 20.3 %collective-permute-start.3 = (bf16[16,4480]{1,0:T(8,128)(2,1)S(1)}, bf16[16,4480]{1,0:T(8,128)(2,1)S(1)}, u32[]{:S(2)}, u32[]{:S(2)}) collective-permute-start(bf16[16,4480]{1,0:T(8,128)(2,1)S(1)} %get-tuple-element.29), channel_id=1, source_target_pairs={{0,11},{1,10},{2,9},{3,8},{4,15},{5,14},{6,13},{7,12},{8,19},{9,18... | collective-permute-start | bytes 430088 | tf_op jit(solution)/shard_map/ppermute | solution.py:611
  78.3 13.8 %collective-permute-start.4 = (bf16[16,4480]{1,0:T(8,128)(2,1)S(1)}, bf16[16,4480]{1,0:T(8,128)(2,1)S(1)}, u32[]{:S(2)}, u32[]{:S(2)}) collective-permute-start(bf16[16,4480]{1,0:T(8,128)(2,1)S(1)} %get-tuple-element.30), channel_id=1, source_target_pairs={{0,8},{1,9},{2,10},{3,11},{4,12},{5,13},{6,14},{7,15},{8,16},{9,17... | collective-permute-start | bytes 430088 | tf_op jit(solution)/shard_map/ppermute | solution.py:611
  85.6 24.8 %collective-permute-start.5 = (bf16[16,4480]{1,0:T(8,128)(2,1)S(1)}, bf16[16,4480]{1,0:T(8,128)(2,1)S(1)}, u32[]{:S(2)}, u32[]{:S(2)}) collective-permute-start(bf16[16,4480]{1,0:T(8,128)(2,1)S(1)} %get-tuple-element.31), channel_id=1, source_target_pairs={{0,12},{1,13},{2,14},{3,15},{4,8},{5,9},{6,10},{7,11},{8,20},{9,21... | collective-permute-start | bytes 430088 | tf_op jit(solution)/shard_map/ppermute | solution.py:611
  85.6 27.5 %collective-permute-start.6 = (bf16[16,4480]{1,0:T(8,128)(2,1)S(1)}, bf16[16,4480]{1,0:T(8,128)(2,1)S(1)}, u32[]{:S(2)}, u32[]{:S(2)}) collective-permute-start(bf16[16,4480]{1,0:T(8,128)(2,1)S(1)} %get-tuple-element.32), channel_id=1, source_target_pairs={{0,13},{1,12},{2,15},{3,14},{4,9},{5,8},{6,11},{7,10},{8,21},{9,20... | collective-permute-start | bytes 430088 | tf_op jit(solution)/shard_map/ppermute | solution.py:611
  89.1 24.7 %collective-permute-start.7 = (bf16[16,4480]{1,0:T(8,128)(2,1)S(1)}, bf16[16,4480]{1,0:T(8,128)(2,1)S(1)}, u32[]{:S(2)}, u32[]{:S(2)}) collective-permute-start(bf16[16,4480]{1,0:T(8,128)(2,1)S(1)} %get-tuple-element.33), channel_id=1, source_target_pairs={{0,14},{1,15},{2,12},{3,13},{4,10},{5,11},{6,8},{7,9},{8,22},{9,23... | collective-permute-start | bytes 430088 | tf_op jit(solution)/shard_map/ppermute | solution.py:611
  91.8 23.7 %collective-permute-start.8 = (bf16[16,4480]{1,0:T(8,128)(2,1)S(1)}, bf16[16,4480]{1,0:T(8,128)(2,1)S(1)}, u32[]{:S(2)}, u32[]{:S(2)}) collective-permute-start(bf16[16,4480]{1,0:T(8,128)(2,1)S(1)} %get-tuple-element.34), channel_id=1, source_target_pairs={{0,15},{1,14},{2,13},{3,12},{4,11},{5,10},{6,9},{7,8},{8,23},{9,22... | collective-permute-start | bytes 430088 | tf_op jit(solution)/shard_map/ppermute | solution.py:611
  108.7 7.9 %collective-permute-start.15 = (bf16[16,4480]{1,0:T(8,128)(2,1)S(1)}, bf16[16,4480]{1,0:T(8,128)(2,1)S(1)}, u32[]{:S(2)}, u32[]{:S(2)}) collective-permute-start(bf16[16,4480]{1,0:T(8,128)(2,1)S(1)} %get-tuple-element.42), channel_id=1, source_target_pairs={{0,28},{1,29},{2,30},{3,31},{4,24},{5,25},{6,26},{7,27},{8,4},{9,5... | collective-permute-start | bytes 430088 | tf_op jit(solution)/shard_map/ppermute | solution.py:611
  110.4 7.1 %collective-permute-start.16 = (bf16[16,4480]{1,0:T(8,128)(2,1)S(1)}, bf16[16,4480]{1,0:T(8,128)(2,1)S(1)}, u32[]{:S(2)}, u32[]{:S(2)}) collective-permute-start(bf16[16,4480]{1,0:T(8,128)(2,1)S(1)} %get-tuple-element.43), channel_id=1, source_target_pairs={{0,25},{1,24},{2,27},{3,26},{4,29},{5,28},{6,31},{7,30},{8,1},{9,0... | collective-permute-start | bytes 430088 | tf_op jit(solution)/shard_map/ppermute | solution.py:611
  113.2 9.3 %collective-permute-start.17 = (bf16[16,4480]{1,0:T(8,128)(2,1)S(1)}, bf16[16,4480]{1,0:T(8,128)(2,1)S(1)}, u32[]{:S(2)}, u32[]{:S(2)}) collective-permute-start(bf16[16,4480]{1,0:T(8,128)(2,1)S(1)} %get-tuple-element.44), channel_id=1, source_target_pairs={{0,26},{1,27},{2,24},{3,25},{4,30},{5,31},{6,28},{7,29},{8,2},{9,3... | collective-permute-start | bytes 430088 | tf_op jit(solution)/shard_map/ppermute | solution.py:611
  113.8 18.0 %collective-permute-start.18 = (bf16[16,4480]{1,0:T(8,128)(2,1)S(1)}, bf16[16,4480]{1,0:T(8,128)(2,1)S(1)}, u32[]{:S(2)}, u32[]{:S(2)}) collective-permute-start(bf16[16,4480]{1,0:T(8,128)(2,1)S(1)} %get-tuple-element.45), channel_id=1, source_target_pairs={{0,27},{1,26},{2,25},{3,24},{4,31},{5,30},{6,29},{7,28},{8,3},{9,2... | collective-permute-start | bytes 430088 | tf_op jit(solution)/shard_map/ppermute | solution.py:611
  115.5 16.3 %collective-permute-start.19 = (bf16[16,4480]{1,0:T(8,128)(2,1)S(1)}, bf16[16,4480]{1,0:T(8,128)(2,1)S(1)}, u32[]{:S(2)}, u32[]{:S(2)}) collective-permute-start(bf16[16,4480]{1,0:T(8,128)(2,1)S(1)} %get-tuple-element.46), channel_id=1, source_target_pairs={{0,29},{1,28},{2,31},{3,30},{4,25},{5,24},{6,27},{7,26},{8,5},{9,4... | collective-permute-start | bytes 430088 | tf_op jit(solution)/shard_map/ppermute | solution.py:611
  116.6 15.2 %collective-permute-start.20 = (bf16[16,4480]{1,0:T(8,128)(2,1)S(1)}, bf16[16,4480]{1,0:T(8,128)(2,1)S(1)}, u32[]{:S(2)}, u32[]{:S(2)}) collective-permute-start(bf16[16,4480]{1,0:T(8,128)(2,1)S(1)} %get-tuple-element.47), channel_id=1, source_target_pairs={{0,24},{1,25},{2,26},{3,27},{4,28},{5,29},{6,30},{7,31},{8,0},{9,1... | collective-permute-start | bytes 430088 | tf_op jit(solution)/shard_map/ppermute | solution.py:611
  117.5 18.1 %collective-permute-start.21 = (bf16[16,4480]{1,0:T(8,128)(2,1)S(1)}, bf16[16,4480]{1,0:T(8,128)(2,1)S(1)}, u32[]{:S(2)}, u32[]{:S(2)}) collective-permute-start(bf16[16,4480]{1,0:T(8,128)(2,1)S(1)} %get-tuple-element.48), channel_id=1, source_target_pairs={{0,30},{1,31},{2,28},{3,29},{4,26},{5,27},{6,24},{7,25},{8,6},{9,7... | collective-permute-start | bytes 430088 | tf_op jit(solution)/shard_map/ppermute | solution.py:611
  122.5 16.4 %collective-permute-start.22 = (bf16[16,4480]{1,0:T(8,128)(2,1)S(1)}, bf16[16,4480]{1,0:T(8,128)(2,1)S(1)}, u32[]{:S(2)}, u32[]{:S(2)}) collective-permute-start(bf16[16,4480]{1,0:T(8,128)(2,1)S(1)} %get-tuple-element.49), channel_id=1, source_target_pairs={{0,31},{1,30},{2,29},{3,28},{4,27},{5,26},{6,25},{7,24},{8,7},{9,6... | collective-permute-start | bytes 430088 | tf_op jit(solution)/shard_map/ppermute | solution.py:611
  (5 other events, 128.7 us)
